TPU v7x, 128 devices: a whole 4x4x4 slice. The times are simulated.
128 devices in a mesh: ctx: 8 (over x, core), fsdp: 16 (over z, y).
Axes of the slice: x: 4, y: 4, z: 4, core: 2. Of those that a mesh axis runs over, the one named last changes fastest.
Arguments:
- tokens: bfloat16 [16, 16, 128, 768], P('fsdp', 'ctx'), may hold values from -6 to 6
- dealing: int32 [16, 16], P('fsdp'), may hold values from 0 to 15, each once within a row
- qkv_weight: bfloat16 [768, 2304], P('fsdp'), may hold values from -0.21875 to 0.21875
- ln1_gain: bfloat16 [768], P('fsdp'), may hold values from 0.5 to 1.5
- ln1_bias: bfloat16 [768], P('fsdp'), may hold values from -1 to 1
- q_bias: bfloat16 [768], P('fsdp'), may hold values from -0.5 to 0.5
- v_bias: bfloat16 [768], P('fsdp'), may hold values from -0.14941406 to 0.14941406
- out_weight: bfloat16 [768, 768], P('fsdp'), may hold values from -9.75 to 9.75
- out_bias: bfloat16 [768], P('fsdp'), may hold values from -1 to 1
- ln2_gain: bfloat16 [768], P('fsdp'), may hold values from 0.5 to 1.5
- ln2_bias: bfloat16 [768], P('fsdp'), may hold values from -1 to 1
- fc_weight: bfloat16 [3072, 768], P('fsdp'), may hold values from -0.21875 to 0.21875
- fc_bias: bfloat16 [3072], P('fsdp'), may hold values from -1 to 1
- proj_weight: bfloat16 [3072, 768], P('fsdp'), may hold values from -0.109375 to 0.109375
- proj_bias: bfloat16 [768], P('fsdp'), may hold values from -1 to 1
- cotangent: bfloat16 [16, 16, 128, 768], P('fsdp', 'ctx'), may hold values from -6 to 6
Outputs:
- output: bfloat16 [16, 16, 128, 768], P('fsdp', 'ctx')
- token_grad: float32 [16, 16, 128, 768], P('fsdp', 'ctx')
- qkv_weight_grad: float32 [768, 2304], P('fsdp')
- ln1_gain_grad: float32 [768], P('fsdp')
- ln1_bias_grad: float32 [768], P('fsdp')
- q_bias_grad: float32 [768], P('fsdp')
- v_bias_grad: float32 [768], P('fsdp')
- out_weight_grad: float32 [768, 768], P('fsdp')
- out_bias_grad: float32 [768], P('fsdp')
- ln2_gain_grad: float32 [768], P('fsdp')
- ln2_bias_grad: float32 [768], P('fsdp')
- fc_weight_grad: float32 [3072, 768], P('fsdp')
- hidden_bias_gradient: float32 [3072], P('fsdp')
- proj_weight_grad: float32 [3072, 768], P('fsdp')
- proj_bias_grad: float32 [768], P('fsdp')
Inputs may be any that keep to these rules, and one draw needn't show every extreme that they name: Each row of dealing names every causal block of its sequence once.
All inputs are finite; a program needn't handle non-finite values.
Results may differ from a plain program's by a relative error of at most 0.022.
Values may be sent and summed in bfloat16 or wider, within the bound.
No kernel may reach another device: no remote copies, remote signals or barrier semaphores. Data moves between devices by JAX's collectives and lax.ppermute only.
A program may use at most 192 MiB of HBM per device.

v0:
```python
import jax
import jax.numpy as jnp
from jax import lax
from jax.sharding import PartitionSpec as P

HEADS = 12


NORM_EPSILON = 1e-05


def layer_norm(values, gain_vector, bias_vector):
    centre = values - jnp.mean(values, axis=-1, keepdims=True)
    spread = jnp.mean(centre * centre, axis=-1, keepdims=True)
    return centre * lax.rsqrt(spread + NORM_EPSILON) * gain_vector + bias_vector


def gelu_tanh(values):
    return jax.nn.gelu(values, approximate=True)


def contract_rows(left_side, right_side):
    return lax.dot_general(
        left_side, right_side, (((0,), (0,)), ((), ())), preferred_element_type=jnp.float32
    )


def contract_cols(left_side, right_side):
    return lax.dot_general(
        left_side, right_side, (((1,), (1,)), ((), ())), preferred_element_type=jnp.float32
    )


def body(
    tokens,
    dealing,
    qkv_weight,
    ln1_gain,
    ln1_bias,
    q_bias,
    v_bias,
    out_weight,
    out_bias,
    ln2_gain,
    ln2_bias,
    fc_weight,
    fc_bias,
    proj_weight,
    proj_bias,
    cotangent,
):
    slot_count = tokens.shape[1]
    block_rows = tokens.shape[2]
    model_width = tokens.shape[3]
    local_rows = slot_count * block_rows
    head_count = HEADS
    head_size = model_width // head_count
    score_scale = head_size ** (-0.5)
    ctx_index = lax.axis_index("ctx")
    gathered = (
        lax.all_gather(qkv_weight, "fsdp", axis=0, tiled=True),
        lax.all_gather(out_weight, "fsdp", axis=0, tiled=True),
        lax.all_gather(ln1_gain, "fsdp", axis=0, tiled=True),
        lax.all_gather(ln1_bias, "fsdp", axis=0, tiled=True),
        lax.all_gather(q_bias, "fsdp", axis=0, tiled=True),
        lax.all_gather(v_bias, "fsdp", axis=0, tiled=True),
        lax.all_gather(out_bias, "fsdp", axis=0, tiled=True),
        lax.all_gather(ln2_gain, "fsdp", axis=0, tiled=True),
        lax.all_gather(ln2_bias, "fsdp", axis=0, tiled=True),
        lax.all_gather(proj_bias, "fsdp", axis=0, tiled=True),
    )
    w_qkv, w_out = (gathered[0], gathered[1])
    gain_one = gathered[2].astype(jnp.float32)
    bias_one = gathered[3].astype(jnp.float32)
    bias_query = gathered[4].astype(jnp.float32)
    bias_value = gathered[5].astype(jnp.float32)
    bias_out = gathered[6].astype(jnp.float32)
    gain_two = gathered[7].astype(jnp.float32)
    bias_two = gathered[8].astype(jnp.float32)
    bias_proj = gathered[9].astype(jnp.float32)
    w_fc, w_proj, bias_fc = (
        lax.all_gather(fc_weight, "fsdp", axis=0, tiled=True),
        lax.all_gather(proj_weight, "fsdp", axis=0, tiled=True),
        lax.all_gather(fc_bias, "fsdp", axis=0, tiled=True),
    )
    deal_row = dealing[0]
    own_blocks = lax.dynamic_slice_in_dim(deal_row, ctx_index * slot_count, slot_count)
    offsets = jnp.arange(block_rows, dtype=jnp.int32)
    query_places = (own_blocks[:, None] * block_rows + offsets[None, :]).reshape(local_rows)
    inputs = tokens.reshape(local_rows, model_width).astype(jnp.float32)
    normed = layer_norm(inputs, gain_one, bias_one)
    normed_low = normed.astype(jnp.bfloat16)
    projected = jnp.dot(normed_low, w_qkv, preferred_element_type=jnp.float32)
    queries = (
        (projected[:, :model_width] + bias_query)
        .astype(jnp.bfloat16)
        .reshape(local_rows, head_count, head_size)
    )
    keys_values = jnp.concatenate(
        [projected[:, model_width : 2 * model_width], projected[:, 2 * model_width :] + bias_value],
        axis=1,
    ).astype(jnp.bfloat16)
    own_kv = keys_values.reshape(slot_count, block_rows, 2 * model_width)

    def key_scores(portion):
        visits = portion.shape[0]
        flattened = portion.reshape(visits * block_rows, 2 * model_width)
        key_part = flattened[:, :model_width].reshape(visits * block_rows, head_count, head_size)
        value_part = flattened[:, model_width:].reshape(visits * block_rows, head_count, head_size)
        key_places = (deal_row[:, None] * block_rows + offsets[None, :]).reshape(
            visits * block_rows
        )
        scores = (
            jnp.einsum("qhd,khd->qhk", queries, key_part, preferred_element_type=jnp.float32)
            * score_scale
        )
        allowed = (key_places[None, :] <= query_places[:, None])[:, None, :]
        return (scores, allowed, key_part, value_part)

    row_max = jnp.full((local_rows, head_count), -1e30, jnp.float32)
    scores, allowed, key_part, value_part = key_scores(
        lax.all_gather(own_kv, "ctx", axis=0, tiled=True)
    )
    masked = jnp.where(allowed, scores, -1e30)
    new_max = jnp.maximum(row_max, jnp.max(masked, axis=-1))
    weights = jnp.where(allowed, jnp.exp(masked - new_max[..., None]), 0.0)
    row_sum = jnp.sum(weights, axis=-1)
    weighted = jnp.einsum(
        "qhk,khd->qhd", weights.astype(jnp.bfloat16), value_part, preferred_element_type=jnp.float32
    )
    row_max, row_sum, weighted = (new_max, row_sum, weighted)
    attended = weighted / row_sum[..., None]
    log_total = row_max + jnp.log(row_sum)
    attended_low = attended.reshape(local_rows, model_width).astype(jnp.bfloat16)
    branch = jnp.dot(attended_low, w_out, preferred_element_type=jnp.float32) + bias_out
    middle = inputs + branch
    normed_two = layer_norm(middle, gain_two, bias_two)
    low_two = normed_two.astype(jnp.bfloat16)
    hidden = contract_cols(low_two, w_fc) + bias_fc.astype(jnp.float32)
    active_low = gelu_tanh(hidden).astype(jnp.bfloat16)
    ffn_out = jnp.dot(active_low, w_proj, preferred_element_type=jnp.float32)
    outcome = (middle + ffn_out + bias_proj).astype(jnp.bfloat16).reshape(tokens.shape)
    upstream = cotangent.reshape(local_rows, model_width)
    grad_proj_b = jnp.sum(upstream.astype(jnp.float32), axis=0)
    grad_proj_w = contract_rows(active_low, upstream)
    grad_active = contract_cols(upstream, w_proj)
    _, gelu_back = jax.vjp(gelu_tanh, hidden)
    grad_hidden = gelu_back(grad_active)[0].astype(jnp.bfloat16)
    grad_fc_b = jnp.sum(grad_hidden.astype(jnp.float32), axis=0)
    grad_fc_w = contract_rows(grad_hidden, low_two)
    grad_normed_two = jnp.dot(grad_hidden, w_fc, preferred_element_type=jnp.float32)
    _, norm_two_back = jax.vjp(layer_norm, middle, gain_two, bias_two)
    grad_middle_part, grad_gain_two, grad_bias_two = norm_two_back(grad_normed_two)
    grad_middle = upstream.astype(jnp.float32) + grad_middle_part
    grad_branch = grad_middle.astype(jnp.bfloat16)
    grad_out_w = contract_rows(attended_low, grad_branch)
    grad_out_b = jnp.sum(grad_branch.astype(jnp.float32), axis=0)
    grad_attended = (
        contract_cols(grad_branch, w_out)
        .astype(jnp.bfloat16)
        .reshape(local_rows, head_count, head_size)
    )
    correction = jnp.sum(grad_attended.astype(jnp.float32) * attended, axis=-1)
    every_kv = lax.all_gather(own_kv, "ctx", axis=0, tiled=True)
    scores, allowed, key_part, value_part = key_scores(every_kv)
    probabilities = jnp.where(allowed, jnp.exp(scores - log_total[..., None]), 0.0)
    grad_values = jnp.einsum(
        "qhk,qhd->khd",
        probabilities.astype(jnp.bfloat16),
        grad_attended,
        preferred_element_type=jnp.float32,
    )
    grad_probs = jnp.einsum(
        "qhd,khd->qhk", grad_attended, value_part, preferred_element_type=jnp.float32
    )
    grad_scores = (probabilities * (grad_probs - correction[..., None])).astype(jnp.bfloat16)
    grad_queries = (
        jnp.einsum("qhk,khd->qhd", grad_scores, key_part, preferred_element_type=jnp.float32)
        * score_scale
    )
    grad_keys = (
        jnp.einsum("qhk,qhd->khd", grad_scores, queries, preferred_element_type=jnp.float32)
        * score_scale
    )
    key_total = grad_keys.shape[0]
    kv_terms = jnp.concatenate(
        [grad_keys.reshape(key_total, model_width), grad_values.reshape(key_total, model_width)],
        axis=1,
    )
    kv_terms = kv_terms.reshape(every_kv.shape[0], block_rows, 2 * model_width)
    own_grad = (
        lax.psum_scatter(kv_terms.astype(jnp.bfloat16), "ctx", scatter_dimension=0, tiled=True)
        .astype(jnp.float32)
        .reshape(local_rows, 2 * model_width)
    )
    grad_projected = jnp.concatenate(
        [grad_queries.reshape(local_rows, model_width), own_grad], axis=1
    ).astype(jnp.bfloat16)
    grad_qkv_w = contract_rows(normed_low, grad_projected)
    grad_q_b = jnp.sum(grad_projected[:, :model_width].astype(jnp.float32), axis=0)
    grad_v_b = jnp.sum(grad_projected[:, 2 * model_width :].astype(jnp.float32), axis=0)
    grad_normed = contract_cols(grad_projected, w_qkv)
    _, norm_one_back = jax.vjp(layer_norm, inputs, gain_one, bias_one)
    grad_inputs_part, grad_gain_one, grad_bias_one = norm_one_back(grad_normed)
    grad_tokens = (grad_middle + grad_inputs_part).reshape(tokens.shape)
    (
        grad_qkv_w,
        grad_gain_one,
        grad_bias_one,
        grad_q_b,
        grad_v_b,
        grad_out_w,
        grad_out_b,
        grad_gain_two,
        grad_bias_two,
        grad_fc_w,
        grad_fc_b,
        grad_proj_w,
        grad_proj_b,
    ) = (
        lax.psum_scatter(
            grad_qkv_w.astype(jnp.bfloat16), "fsdp", scatter_dimension=0, tiled=True
        ).astype(jnp.float32),
        lax.psum_scatter(
            grad_gain_one.astype(jnp.bfloat16), "fsdp", scatter_dimension=0, tiled=True
        ).astype(jnp.float32),
        lax.psum_scatter(
            grad_bias_one.astype(jnp.bfloat16), "fsdp", scatter_dimension=0, tiled=True
        ).astype(jnp.float32),
        lax.psum_scatter(
            grad_q_b.astype(jnp.bfloat16), "fsdp", scatter_dimension=0, tiled=True
        ).astype(jnp.float32),
        lax.psum_scatter(
            grad_v_b.astype(jnp.bfloat16), "fsdp", scatter_dimension=0, tiled=True
        ).astype(jnp.float32),
        lax.psum_scatter(
            grad_out_w.astype(jnp.bfloat16), "fsdp", scatter_dimension=0, tiled=True
        ).astype(jnp.float32),
        lax.psum_scatter(
            grad_out_b.astype(jnp.bfloat16), "fsdp", scatter_dimension=0, tiled=True
        ).astype(jnp.float32),
        lax.psum_scatter(
            grad_gain_two.astype(jnp.bfloat16), "fsdp", scatter_dimension=0, tiled=True
        ).astype(jnp.float32),
        lax.psum_scatter(
            grad_bias_two.astype(jnp.bfloat16), "fsdp", scatter_dimension=0, tiled=True
        ).astype(jnp.float32),
        lax.psum_scatter(
            grad_fc_w.astype(jnp.bfloat16), "fsdp", scatter_dimension=0, tiled=True
        ).astype(jnp.float32),
        lax.psum_scatter(
            grad_fc_b.astype(jnp.bfloat16), "fsdp", scatter_dimension=0, tiled=True
        ).astype(jnp.float32),
        lax.psum_scatter(
            grad_proj_w.astype(jnp.bfloat16), "fsdp", scatter_dimension=0, tiled=True
        ).astype(jnp.float32),
        lax.psum_scatter(
            grad_proj_b.astype(jnp.bfloat16), "fsdp", scatter_dimension=0, tiled=True
        ).astype(jnp.float32),
    )
    summed = (
        lax.psum(grad_qkv_w.astype(jnp.bfloat16), "ctx").astype(jnp.float32),
        lax.psum(grad_gain_one.astype(jnp.bfloat16), "ctx").astype(jnp.float32),
        lax.psum(grad_bias_one.astype(jnp.bfloat16), "ctx").astype(jnp.float32),
        lax.psum(grad_q_b.astype(jnp.bfloat16), "ctx").astype(jnp.float32),
        lax.psum(grad_v_b.astype(jnp.bfloat16), "ctx").astype(jnp.float32),
        lax.psum(grad_out_w.astype(jnp.bfloat16), "ctx").astype(jnp.float32),
        lax.psum(grad_out_b.astype(jnp.bfloat16), "ctx").astype(jnp.float32),
        lax.psum(grad_gain_two.astype(jnp.bfloat16), "ctx").astype(jnp.float32),
        lax.psum(grad_bias_two.astype(jnp.bfloat16), "ctx").astype(jnp.float32),
        lax.psum(grad_fc_w.astype(jnp.bfloat16), "ctx").astype(jnp.float32),
        lax.psum(grad_fc_b.astype(jnp.bfloat16), "ctx").astype(jnp.float32),
        lax.psum(grad_proj_w.astype(jnp.bfloat16), "ctx").astype(jnp.float32),
        lax.psum(grad_proj_b.astype(jnp.bfloat16), "ctx").astype(jnp.float32),
    )
    return (
        outcome,
        grad_tokens,
        summed[0],
        summed[1],
        summed[2],
        summed[3],
        summed[4],
        summed[5],
        summed[6],
        summed[7],
        summed[8],
        summed[9],
        summed[10],
        summed[11],
        summed[12],
    )


def solution(mesh):
    placed = (
        P("fsdp", "ctx", None, None),
        P("fsdp", None),
        P("fsdp", None),
        P("fsdp"),
        P("fsdp"),
        P("fsdp"),
        P("fsdp"),
        P("fsdp", None),
        P("fsdp"),
        P("fsdp"),
        P("fsdp"),
        P("fsdp", None),
        P("fsdp"),
        P("fsdp", None),
        P("fsdp"),
        P("fsdp", "ctx", None, None),
    )
    return jax.shard_map(
        body,
        mesh=mesh,
        in_specs=placed,
        out_specs=(
            P("fsdp", "ctx", None, None),
            P("fsdp", "ctx", None, None),
            P("fsdp", None),
            P("fsdp"),
            P("fsdp"),
            P("fsdp"),
            P("fsdp"),
            P("fsdp", None),
            P("fsdp"),
            P("fsdp"),
            P("fsdp"),
            P("fsdp", None),
            P("fsdp"),
            P("fsdp", None),
            P("fsdp"),
        ),
        check_vma=False,
    )
```

profile of v0, /device:TPU:1, one launch (start us, length us, event | category | flops | bytes accessed | tf_op | source)
XLA Modules:
  0.0 776.3 jit_solution(6333738510427409305)
XLA Ops:
  8.7 1.3 fusion.55
  11.4 0.8 dynamic-update-slice
  12.2 0.8 dynamic-update-slice.1
  13.0 0.8 dynamic-update-slice.2
  13.9 0.8 dynamic-update-slice.3
  14.7 0.8 dynamic-update-slice.4
  15.5 0.8 dynamic-update-slice.5
  16.4 0.8 dynamic-update-slice.6
  17.2 0.8 dynamic-update-slice.7
  18.1 63.0 %all-reduce.19 = (bf16[768]{0:T(1024)(128)(2,1)S(1)}, bf16[768]{0:T(1024)(128)(2,1)S(1)}, bf16[768]{0:T(1024)(128)(2,1)S(1)}, bf16[768]{0:T(1024)(128)(2,1)S(1)}...) all-reduce(bf16[768]{0:T(1024)(128)(2,1)S(1)} %dynamic-update-slice, ...), channel_id=1, replica_groups=mesh['ctx'=8,'fsdp'=16] {'fsdp'}, use_global_device_ids=true, to_apply=%add.1 | all-reduce | flops 8448 | bytes 33792
  81.1 1.1 convert_reduce_fusion
  82.2 1.2 multiply_reduce_fusion.6
  84.6 1.3 add_convert_fusion.1
  85.9 3.2 fusion.58
  89.3 0.9 pad_maximum_fusion.2
  94.6 1.1 broadcast_compare_fusion
  95.7 0.9 copy.50
  96.7 21.6 %all-gather.14.cloned.1.call-done = bf16[3072,768]{1,0:T(8,128)(2,1)} async-done(((bf16[192,768]{1,0:T(8,128)(2,1)}), bf16[3072,768]{1,0:T(8,128)(2,1)}) %all-gather.14.cloned.1.call-update) | async-done | bytes 4718608 | tf_op jit(solution)/shard_map/all_gather | solution.py:83
  118.2 5.4 fusion.59
  123.6 37.8 %all-gather.8.cloned.1.call-done = bf16[16,128,1536]{2,1,0:T(8,128)(2,1)} async-done(((bf16[2,128,1536]{2,1,0:T(8,128)(2,1)}), bf16[16,128,1536]{2,1,0:T(8,128)(2,1)}) %all-gather.8.cloned.1.call-update) | async-done | bytes 6291472 | tf_op jit(solution)/shard_map/all_gather | solution.py:122
  161.4 5.9 fusion.54
  167.3 3.2 copy.64
  170.5 4.8 copy.63
  175.3 11.5 %fusion.4 = (f32[256,12]{0,1:T(8,128)S(1)}, f32[12,2048,256]{2,1,0:T(8,128)}) fusion(pred[256,2048]{0,1:T(8,128)(4,1)} %broadcast_compare_fusion, bf16[2048,12,64]{0,2,1:T(8,128)(2,1)S(1)} %bitcast.133, bf16[256,12,64]{0,2,1:T(8,128)(2,1)S(1)} %bitcast.143), kind=kOutput, calls=%fused_computation.8 | convolution fusion | flops 824177664 | bytes 29241344 | tf_op jit(solution)/shard_map/qhd,khd->qhk/dot_general | solution.py:114
  186.8 11.6 %fusion.6 = f32[256,12]{0,1:T(8,128)S(1)} fusion(f32[12,2048,256]{2,1,0:T(8,128)} %get-tuple-element.68, f32[256,12]{0,1:T(8,128)S(1)} %broadcast_maximum_fusion, pred[256,2048]{0,1:T(8,128)(4,1)S(1)} %copy-done.9), kind=kLoop, calls=%fused_computation.10 | loop fusion | flops 31454208 | bytes 25714688 | tf_op jit(solution)/shard_map/reduce_sum | solution.py:127
  199.1 12.4 %fusion.56 = (bf16[256,12,64]{0,2,1:T(8,128)(2,1)}, f32[256,12,64]{0,2,1:T(8,128)}) fusion(f32[256,12]{0,1:T(8,128)S(1)} %fusion.6, bf16[2048,12,64]{0,2,1:T(8,128)(2,1)S(1)} %bitcast.145, f32[12,2048,256]{2,1,0:T(8,128)} %get-tuple-element.68, f32[256,12]{0,1:T(8,128)S(1)} %broadcast_maximum_fusion, pred[256,2048]{0,1:T(8,128)(4,1)S(1)} %copy-done.9), kind=kOutput, calls=%fused_computation.103 | convolution fusion | flops 837156864 | bytes 30040064 | tf_op jit(solution)/shard_map/qhk,khd->qhd/dot_general | solution.py:128
  211.6 1.9 fusion.57
  213.5 0.9 copy-done.1
  215.9 45.8 %all-gather.12.cloned.1.call-done = bf16[3072,768]{1,0:T(8,128)(2,1)} async-done(((bf16[192,768]{1,0:T(8,128)(2,1)}), bf16[3072,768]{1,0:T(8,128)(2,1)}) %all-gather.12.cloned.1.call-update) | async-done | bytes 4718608 | tf_op jit(solution)/shard_map/all_gather | solution.py:82
  261.7 9.2 %fusion.49 = (bf16[3072]{0:T(1024)(128)(2,1)}, bf16[256,3072]{1,0:T(8,128)(2,1)S(1)}, f32[256,3072]{1,0:T(8,128)}) fusion(f32[256,3072]{1,0:T(8,128)} %fusion.59, f32[3072]{0:T(1024)} %convert_element_type.202, bf16[3072,768]{1,0:T(8,128)(2,1)} %all-gather.12.cloned.1.call-done, f32[256,768]{1,0:T(8,128)} %copy-done.1, f32[768]{0:T(1024)} %convert_element_type.200, ...), kind=kOutput, calls=%fused_computation.98 | convolution fusion | flops 1226241024 | bytes 13395968 | tf_op jit(solution)/shard_map/dot_general | solution.py:29
  270.9 2.1 multiply_reduce_fusion
  273.4 0.9 copy-done.4
  275.8 1.3 convolution_convert_fusion.4
  277.1 1.9 copy.52
  279.0 1.9 multiply_reduce_fusion.3
  280.9 12.4 %fusion.14 = bf16[12,64,2048]{2,1,0:T(8,128)(2,1)} fusion(bf16[256,12,64]{0,2,1:T(8,128)(2,1)} %bitcast.153, f32[12,2048,256]{2,1,0:T(8,128)} %get-tuple-element.68, f32[256,12]{0,1:T(8,128)} %log_add_fusion, pred[256,2048]{0,1:T(8,128)(4,1)} %broadcast_compare_fusion), kind=kOutput, calls=%fused_computation.24 | convolution fusion | flops 832045056 | bytes 29241344 | tf_op jit(solution)/shard_map/qhk,qhd->khd/dot_general | solution.py:167
  293.4 16.0 %fusion.1 = bf16[256,12,2048]{0,2,1:T(8,128)(2,1)} fusion(f32[12,2048,256]{2,1,0:T(8,128)} %get-tuple-element.68, f32[256,12]{0,1:T(8,128)} %multiply_reduce_fusion.3, f32[256,12]{0,1:T(8,128)} %log_add_fusion, pred[256,2048]{0,1:T(8,128)(4,1)} %broadcast_compare_fusion, bf16[2048,12,64]{0,2,1:T(8,128)(2,1)} %bitcast.144, bf16[256,12,64]{0,2,1:T(8,128)(2,1)} %bitcast.154), kind=kOutput, calls=%fused_computation.2 | convolution fusion | flops 843055104 | bytes 41836544 | tf_op jit(solution)/shard_map/qhd,khd->qhk/dot_general | solution.py:173
  309.4 8.6 %multiply_convert_fusion = bf16[12,64,2048]{2,1,0:T(8,128)(2,1)S(1)} fusion(bf16[256,12,64]{0,2,1:T(8,128)(2,1)} %bitcast.142, bf16[256,12,2048]{0,2,1:T(8,128)(2,1)} %fusion.1), kind=kOutput, calls=%fused_computation.17 | convolution fusion | flops 808452096 | bytes 16121856 | tf_op jit(solution)/shard_map/qhk,qhd->khd/dot_general | solution.py:182
  318.0 2.7 copy.65
  320.6 5.0 copy.56
  325.6 4.6 copy.66
  330.2 5.0 copy.57
  335.3 6.1 pad_maximum_fusion
  341.4 2.6 convolution_convert_fusion.3
  344.1 5.4 convolution_convert_fusion.1
  349.8 6.6 convolution_convert_fusion
  356.5 7.8 bitcast_reduce_fusion
  364.2 1.2 copy.58
  365.4 17.6 %reduce-scatter.6.cloned.1.call-done = bf16[2,128,1536]{2,1,0:T(8,128)(2,1)} async-done(((bf16[16,128,1536]{2,1,0:T(8,128)(2,1)}), bf16[2,128,1536]{2,1,0:T(8,128)(2,1)}) %reduce-scatter.6.cloned.1.call-update) | async-done | bytes 786448 | tf_op jit(solution)/shard_map/reduce_scatter | solution.py:192
  383.0 4.1 convolution_convert_fusion.2
  387.2 0.9 copy-done.8
  391.7 3.9 fusion.48
  396.0 60.8 %all-reduce.18 = (bf16[768]{0:T(1024)(128)(2,1)S(1)}, bf16[768]{0:T(1024)(128)(2,1)S(1)}, bf16[768]{0:T(1024)(128)(2,1)S(1)}, bf16[768]{0:T(1024)(128)(2,1)S(1)}...) all-reduce(bf16[768]{0:T(1024)(128)(2,1)} %copy-done.37, ...), channel_id=1, replica_groups=mesh['ctx'=8,'fsdp'=16] {'fsdp'}, use_global_device_ids=true, to_apply=%add.8 | all-reduce | flops 9984 | bytes 39936
  457.5 26.9 %all-reduce.20 = (bf16[48]{0:T(256)(128)(2,1)S(1)}, bf16[48]{0:T(256)(128)(2,1)S(1)}, bf16[48]{0:T(256)(128)(2,1)S(1)}, bf16[48]{0:T(256)(128)(2,1)S(1)}, bf16[4...) all-reduce(bf16[48]{0:T(256)(128)(2,1)S(1)} %dynamic-slice.11, ...), channel_id=1, replica_groups=mesh['ctx'=8,'fsdp'=16] {'ctx'}, use_global_device_ids=true, to_apply=%region_16.17 | all-reduce | flops 576 | bytes 2304 | tf_op jit(solution)/shard_map/psum | solution.py:263
  489.1 6.1 fusion.29
  495.2 44.3 %reduce-scatter.12.cloned.1.call-done = bf16[192,768]{1,0:T(8,128)(2,1)} async-done(((bf16[3072,768]{1,0:T(8,128)(2,1)}), bf16[192,768]{1,0:T(8,128)(2,1)}) %reduce-scatter.12.cloned.1.call-update) | async-done | bytes 294928 | tf_op jit(solution)/shard_map/reduce_scatter | solution.py:248
  539.5 81.2 %reduce-scatter.14.cloned.1.call-done = bf16[192,768]{1,0:T(8,128)(2,1)} async-done(((bf16[3072,768]{1,0:T(8,128)(2,1)}), bf16[192,768]{1,0:T(8,128)(2,1)}) %reduce-scatter.14.cloned.1.call-update) | async-done | bytes 294928 | tf_op jit(solution)/shard_map/reduce_scatter | solution.py:254
  620.8 78.9 %reduce-scatter.8.cloned.1.call-done = bf16[48,2304]{1,0:T(8,128)(2,1)} async-done(((bf16[768,2304]{1,0:T(8,128)(2,1)}), bf16[48,2304]{1,0:T(8,128)(2,1)}) %reduce-scatter.8.cloned.1.call-update) | async-done | bytes 221200 | tf_op jit(solution)/shard_map/reduce_scatter | solution.py:221
  699.7 1.3 add_add_fusion.2
  701.0 61.7 %all-reduce.24.cloned.1.call-done = (bf16[48,2304]{1,0:T(8,128)(2,1)}, bf16[48,768]{1,0:T(8,128)(2,1)}, bf16[192,768]{1,0:T(8,128)(2,1)}, bf16[192,768]{1,0:T(8,128)(2,1)}) async-done(((bf16[48,2304]{1,0:T(8,128)(2,1)}, bf16[48,768]{1,0:T(8,128)(2,1)}, bf16[192,768]{1,0:T(8,128)(2,1)}, bf16[192,768]{1,0:T(8,128)(2,1)}), (bf16[48,2304]{1,0:T(8,128)(2,1)}, bf16[48,768]{1,0:T(8,128)(2,1)}, ...) | async-done | bytes 884752 | tf_op jit(solution)/shard_map/psum | solution.py:262
  762.6 1.8 convert_element_type.229
  764.4 1.8 convert_element_type.232
  766.2 1.7 convert_element_type.214
  768.0 1.6 convert_element_type.222
  (164 shorter events, 19.8 us)
Async XLA Ops:
  7.2 78.7 %all-gather.6.cloned.1.call-start = ((), (), s32[]{:S(2)}) async-start(), calls=%async_computation.5 | async-start | bytes 3760128 | tf_op jit(solution)/shard_map/all_gather | solution.py:61
  7.9 110.3 %all-gather.14.cloned.1.call-start = ((), (), s32[]{:S(2)}) async-start(), calls=%async_computation.9 | async-start | bytes 5013504 | tf_op jit(solution)/shard_map/all_gather | solution.py:83
  8.7 152.7 %all-gather.8.cloned.1.call-start = ((), (), s32[]{:S(2)}) async-start(), calls=%async_computation.6 | async-start | bytes 7077888 | tf_op jit(solution)/shard_map/all_gather | solution.py:122
  81.1 2.9 copy-start.17
  82.2 1.8 copy-start.23
  83.5 0.5 copy-start.30
  84.0 0.6 copy-start.25
  85.8 3.3 copy-start.11
  89.1 5.3 copy-start.39
  89.2 29.1 %copy-start.6 = (bf16[1,2,128,768]{3,2,1,0:T(8,128)(2,1)S(1)}, bf16[1,2,128,768]{3,2,1,0:T(8,128)(2,1)}, u32[]{:S(2)}) copy-start(bf16[1,2,128,768]{3,2,1,0:T(8,128)(2,1)} %param.31) | copy-start | bytes 1179652
  90.2 121.3 %all-gather.10.cloned.1.call-start = ((), (), s32[]{:S(2)}) async-start(), calls=%async_computation.7 | async-start | bytes 1253376 | tf_op jit(solution)/shard_map/all_gather | solution.py:62
  90.8 170.9 %all-gather.12.cloned.1.call-start = ((), (), s32[]{:S(2)}) async-start(), calls=%async_computation.8 | async-start | bytes 5013504 | tf_op jit(solution)/shard_map/all_gather | solution.py:82
  91.4 291.6 %reduce-scatter.6.cloned.1.call-start = ((), (), s32[]{:S(2)}) async-start(), calls=%async_computation.10 | async-start | bytes 7077888 | tf_op jit(solution)/shard_map/reduce_scatter | solution.py:192
  170.5 4.8 copy-start.13
  175.3 11.5 %copy-start.9 = (pred[256,2048]{0,1:T(8,128)(4,1)S(1)}, pred[256,2048]{0,1:T(8,128)(4,1)}, u32[]{:S(2)}) copy-start(pred[256,2048]{0,1:T(8,128)(4,1)} %broadcast_compare_fusion) | copy-start | bytes 1572868
  186.8 12.3 %copy-start.15 = (bf16[2048,768]{0,1:T(8,128)(2,1)S(1)}, bf16[2048,768]{0,1:T(8,128)(2,1)}, u32[]{:S(2)}) copy-start(bf16[2048,768]{0,1:T(8,128)(2,1)} %copy.63) | copy-start | bytes 9437188
  198.5 0.6 copy-start.19
  199.1 12.5 %copy-start = (bf16[1,2,128,768]{3,2,1,0:T(8,128)(2,1)S(1)}, bf16[1,2,128,768]{3,2,1,0:T(8,128)(2,1)}, u32[]{:S(2)}) copy-start(bf16[1,2,128,768]{3,2,1,0:T(8,128)(2,1)} %param.16) | copy-start | bytes 1179652
  211.6 3.7 copy-start.20
  213.5 0.9 copy-start.1
  213.5 1.7 copy-start.27
  214.6 0.6 copy-start.32
  215.9 55.0 %copy-start.21 = (f32[768]{0:T(1024)S(1)}, f32[768]{0:T(1024)}, u32[]{:S(2)}) copy-start(f32[768]{0:T(1024)} %convert_element_type.199) | copy-start | bytes 9220
  215.9 55.0 %copy-start.28 = (f32[256]{0:T(256)S(1)}, f32[256]{0:T(256)}, u32[]{:S(2)}) copy-start(f32[256]{0:T(256)} %copy-done.27) | copy-start | bytes 3076
  215.9 55.0 %copy-start.29 = (f32[256]{0:T(256)S(1)}, f32[256]{0:T(256)}, u32[]{:S(2)}) copy-start(f32[256]{0:T(256)} %fusion.38) | copy-start | bytes 3076
  261.7 9.2 %copy-start.2 = (f32[256,768]{1,0:T(8,128)S(1)}, f32[256,768]{1,0:T(8,128)}, u32[]{:S(2)}) copy-start(f32[256,768]{1,0:T(8,128)} %copy-done.1) | copy-start | bytes 2359300
  261.7 9.2 %copy-start.38 = (bf16[3072,768]{1,0:T(8,128)(2,1)S(1)}, bf16[3072,768]{1,0:T(8,128)(2,1)}, u32[]{:S(2)}) copy-start(bf16[3072,768]{1,0:T(8,128)(2,1)} %all-gather.12.cloned.1.call-done) | copy-start | bytes 14155780
  270.9 2.1 copy-start.12
  270.9 2.1 copy-start.33
  270.9 3.3 copy-start.7
  273.0 2.8 copy-start.10
  273.4 0.9 copy-start.4
  273.4 20.0 %copy-start.34 = (f32[256]{0:T(256)}, f32[256]{0:T(256)S(1)}, u32[]{:S(2)}) copy-start(f32[256]{0:T(256)S(1)} %negate_multiply_fusion.1) | copy-start | bytes 3076
  275.0 0.8 copy-start.14
  341.3 2.7 copy-start.22
  341.4 153.9 %reduce-scatter.10.cloned.1.call-start = ((), (), s32[]{:S(2)}) async-start(), calls=%async_computation.12 | async-start | bytes 1253376 | tf_op jit(solution)/shard_map/reduce_scatter | solution.py:236
  344.0 195.5 %reduce-scatter.12.cloned.1.call-start = ((), (), s32[]{:S(2)}) async-start(), calls=%async_computation.13 | async-start | bytes 5013504 | tf_op jit(solution)/shard_map/reduce_scatter | solution.py:248
  349.5 271.3 %reduce-scatter.14.cloned.1.call-start = ((), (), s32[]{:S(2)}) async-start(), calls=%async_computation.14 | async-start | bytes 5013504 | tf_op jit(solution)/shard_map/reduce_scatter | solution.py:254
  356.4 343.2 %reduce-scatter.8.cloned.1.call-start = ((), (), s32[]{:S(2)}) async-start(), calls=%async_computation.11 | async-start | bytes 3760128 | tf_op jit(solution)/shard_map/reduce_scatter | solution.py:221
  387.1 1.0 copy-start.8
  387.1 3.0 copy-start.40
  387.1 3.9 copy-start.16
  387.1 4.5 copy-start.18
  387.1 4.5 copy-start.24
  387.1 375.5 %all-reduce.24.cloned.1.call-start = ((), (), s32[]{:S(2)}) async-start(), calls=%async_computation.15 | async-start | bytes 1769472 | tf_op jit(solution)/shard_map/psum | solution.py:262
  390.3 0.7 copy-start.37
  391.6 3.9 copy-start.31
  391.6 3.9 copy-start.26
  391.6 4.3 copy-start.36
  391.7 97.4 %copy-start.3 = (f32[256,768]{1,0:T(8,128)S(1)}, f32[256,768]{1,0:T(8,128)}, u32[]{:S(2)}) copy-start(f32[256,768]{1,0:T(8,128)} %copy-done.1) | copy-start | bytes 2359300
  489.1 210.6 %copy-start.5 = (f32[256,768]{1,0:T(8,128)S(1)}, f32[256,768]{1,0:T(8,128)}, u32[]{:S(2)}) copy-start(f32[256,768]{1,0:T(8,128)} %copy-done.4) | copy-start | bytes 2359300
  489.1 210.6 %copy-start.35 = (f32[256]{0:T(256)S(1)}, f32[256]{0:T(256)}, u32[]{:S(2)}) copy-start(f32[256]{0:T(256)} %copy-done.34) | copy-start | bytes 3076
Sparse Core Ops, SparseCore 0:
  10.1 52.5 all-gather.5
  64.8 53.3 all-gather.13
  120.5 40.8 all-gather.7
  163.4 42.0 all-gather.9
  207.4 54.2 all-gather.11
  341.5 41.4 reduce-scatter.5
  386.2 72.2 reduce-scatter.9
  461.8 77.7 reduce-scatter.11
  542.9 77.8 reduce-scatter.13
  624.0 75.5 reduce-scatter.7
  702.3 60.3 all-reduce.23
where the time goes:
time: 783 us; the launch traced here: 776 us
  waiting for transfers between devices  391 us (50%)
  blocking collectives  151 us (19%)
  matrix products  120 us (15%)
  local copies, waits for them, and re-layouts  50.1 us (6%)
  other arithmetic  45.2 us (6%)
  between operations  17.2 us (2%)
    unnamed x2, blocking collectives  124 us
    reduce_scatter x1, waiting for transfers between devices, body(): lax.psum_scatter(grad_proj_w.astype(jnp.bfloat16), 'fsdp', scatter_dimens...  81.2 us
    reduce_scatter x1, waiting for transfers between devices, body(): lax.psum_scatter(grad_qkv_w.astype(jnp.bfloat16), 'fsdp', scatter_dimensi...  78.9 us
    psum x1, waiting for transfers between devices, body(): lax.psum(grad_qkv_w.astype(jnp.bfloat16), 'ctx').astype(jnp.float32)  61.7 us
    all_gather x1, waiting for transfers between devices, body(): lax.all_gather(fc_weight, 'fsdp', axis=0, tiled=True)  45.8 us
    reduce_scatter x1, waiting for transfers between devices, body(): lax.psum_scatter(grad_fc_w.astype(jnp.bfloat16), 'fsdp', scatter_dimensio...  44.3 us
    all_gather x1, waiting for transfers between devices, body(): lax.all_gather(own_kv, 'ctx', axis=0, tiled=True)  37.8 us
    unnamed x114, local copies, waits for them, and re-layouts  29.4 us
  transfers between devices with their start and end apart: 11, of which 8 were waited for; matrix products, arithmetic and copies ran while one was open for 16% of the time, Pallas kernels for 0%

commit v1 on v0

v1 whole, which is shorter than its diff:
```python
import jax
import jax.numpy as jnp
from jax import lax
from jax.experimental import pallas as pl
from jax.experimental.pallas import tpu as pltpu
from jax.sharding import Mesh, PartitionSpec as P

D = 768
FF = 3072
HC = 3
HD = 64
CH = HC * HD
BT = 128
SEQ = 2048
ROWS = 256
KC = 512
EPS = 1e-05
NEG = -1e30
F32 = jnp.float32
BF16 = jnp.bfloat16

NT = (((1,), (1,)), ((), ()))
TN = (((0,), (0,)), ((), ()))


def dot(a, b):
    return jnp.dot(a, b, preferred_element_type=F32)


def dot_nt(a, b):
    return lax.dot_general(a, b, NT, preferred_element_type=F32)


def dot_tn(a, b):
    return lax.dot_general(a, b, TN, preferred_element_type=F32)


def standardize(v):
    centre = v - jnp.mean(v, axis=-1, keepdims=True)
    spread = jnp.mean(centre * centre, axis=-1, keepdims=True)
    root = lax.rsqrt(spread + EPS)
    return centre * root, root


def rel(a, b):
    return lax.rem(a - b + 4, 4)


def forward_kernel(meta, *refs):
    toks = refs[0:8]
    wrel = refs[8:12]
    vec, qvb = refs[12:14]
    (atts, attt_ref, lse_ref, q_ref, k_ref, kt_ref, v_ref, normed_ref, w_ref) = (
        refs[14:18],
        *refs[18:26],
    )
    vt_ref = refs[26]
    z, y = meta[2], meta[3]
    for ky in range(4):
        for kz in range(4):
            shard = rel(z, kz) * 4 + rel(y, ky)
            w_ref[pl.ds(pl.multiple_of(shard * 48, 16), 48), :] = wrel[ky][kz * 64 : kz * 64 + 48, :]
    gain = vec[0:1, :]
    bias = vec[1:2, :]
    qb = qvb[0:1, :]
    vb = qvb[1:2, :]
    w = w_ref[...]
    for k in range(8):
        own = k < 4
        xhat, _ = standardize(toks[k][...].astype(F32))
        normed = (xhat * gain + bias).astype(BF16)
        if own:
            normed_ref[k * ROWS : (k + 1) * ROWS, :] = normed
            proj = dot(normed, w)
            q = (proj[:, :CH] + qb).astype(BF16) * jnp.asarray(HD**-0.5, BF16)
            for h in range(HC):
                q_ref[h, k * ROWS : (k + 1) * ROWS, :] = q[:, h * HD : (h + 1) * HD]
            kv = proj[:, CH:]
        else:
            kv = dot(normed, w[:, CH:])
        for r in range(2):
            place = pl.multiple_of(meta[4 + 2 * k + r] * BT, BT)
            kk = kv[r * BT : (r + 1) * BT, :CH]
            vv = kv[r * BT : (r + 1) * BT, CH:] + vb
            kb = kk.astype(BF16)
            vbl = vv.astype(BF16)
            for h in range(HC):
                cols = slice(h * HD, (h + 1) * HD)
                k_ref[h, pl.ds(place, BT), :] = kb[:, cols]
                v_ref[h, pl.ds(place, BT), :] = vbl[:, cols]
                kt_ref[h, :, pl.ds(place, BT)] = kk[:, cols].T.astype(BF16)
                vt_ref[h, :, pl.ds(place, BT)] = vv[:, cols].T.astype(BF16)

    key_iota = lax.broadcasted_iota(jnp.int32, (KC, BT), 0)
    query_iota = lax.broadcasted_iota(jnp.int32, (KC, BT), 1)
    for i in range(8):
        pos = meta[4 + i]
        queries = [q_ref[h, i * BT : (i + 1) * BT, :] for h in range(HC)]

        def step(j, carry, masked, pos=pos, queries=queries):
            base = pl.multiple_of(j * KC, KC)
            out = []
            if masked:
                keep = key_iota + base <= query_iota + pos * BT
            for h in range(HC):
                m, total, acc = carry[h]
                s = dot_nt(k_ref[h, pl.ds(base, KC), :], queries[h])
                if masked:
                    s = jnp.where(keep, s, NEG)
                m_new = jnp.maximum(m, jnp.max(s, axis=0, keepdims=True))
                e = jnp.exp(s - m_new)
                a = jnp.exp(m - m_new)
                total = total * a + jnp.sum(e, axis=0, keepdims=True)
                acc = acc * a + dot(vt_ref[h, :, pl.ds(base, KC)], e.astype(BF16))
                out.append((m_new, total, acc))
            return tuple(out)

        full = lax.div(pos * BT, KC)
        carry = tuple(
            (jnp.full((1, BT), NEG, F32), jnp.zeros((1, BT), F32), jnp.zeros((HD, BT), F32))
            for _ in range(HC)
        )
        carry = lax.fori_loop(0, full, lambda j, c: step(j, c, False), carry)
        carry = step(full, carry, True)
        parts = []
        for h in range(HC):
            m, total, acc = carry[h]
            att = acc / total
            attt_ref[i, h] = att
            lse_ref[i, h : h + 1, :] = m + jnp.log(total)
            parts.append(att.T.astype(BF16))
        for h in range(HC):
            atts[i // 2][(i % 2) * BT : (i % 2 + 1) * BT, h * HD : (h + 1) * HD] = parts[h]


def gelu_parts(v):
    c = 0.7978845608028654
    t = jnp.tanh(c * (v + 0.044715 * (v * v * v)))
    act = 0.5 * v * (1.0 + t)
    slope = 0.5 * (1.0 + t) + (0.5 * c) * v * (1.0 - t * t) * (1.0 + (3 * 0.044715) * v * v)
    return act, slope


def mlp_kernel(
    meta,
    a0,
    a1,
    a2,
    a3,
    tok,
    cot,
    wout,
    vec,
    fcb,
    wblk,
    out_ref,
    gm_ref,
    d0,
    d1,
    d2,
    d3,
    own_a,
    own_b,
    oth_a,
    oth_b,
    vg_ref,
    fcg_ref,
    middle_s,
    xhat_s,
    root_s,
    n2_s,
    ffn_s,
    dn_s,
    dout_s,
):
    j = pl.program_id(0)
    x, c, z, y = meta[0], meta[1], meta[2], meta[3]
    atts = (a0, a1, a2, a3)

    def head_rows(k):
        return pl.ds(pl.multiple_of(lax.rem(x + k, 4) * CH, 64), CH)

    @pl.when(j == 0)
    def _():
        branch = vec[4:5, :]
        middle = tok[...].astype(F32)
        for k in range(4):
            middle = middle + dot(atts[k][...], wout[head_rows(k), :])
        middle = middle + branch
        xhat, root = standardize(middle)
        middle_s[...] = middle
        xhat_s[...] = xhat
        root_s[...] = root
        n2_s[...] = (xhat * vec[5:6, :] + vec[6:7, :]).astype(BF16)
        ffn_s[...] = jnp.zeros_like(ffn_s)
        dn_s[...] = jnp.zeros_like(dn_s)

    fc = wblk[:, 64:256, :].reshape(D, D)
    proj = wblk[:, 256:448, :].reshape(D, D)
    cols = pl.ds(pl.multiple_of(j * D, D), D)
    n2 = n2_s[...]
    ct = cot[...]
    hidden = dot_nt(n2, fc) + fcb[:, cols]
    act, slope = gelu_parts(hidden)
    act = act.astype(BF16)
    ffn_s[...] += dot(act, proj)
    gh = dot_nt(ct, proj) * slope
    gh = gh.astype(BF16)
    dn_s[...] += dot(gh, fc)
    fcg_ref[:, cols] = jnp.sum(gh.astype(F32), axis=0, keepdims=True)
    dproj = dot_tn(act, ct).astype(BF16)
    dfc = dot_tn(gh, n2).astype(BF16)
    kz = rel(j, z)
    for yy in range(4):
        ky = rel(yy, y)
        first = slice(yy * 192, yy * 192 + 96)
        second = slice(yy * 192 + 96, (yy + 1) * 192)

        @pl.when(c == 0)
        def _():
            own_a[kz, ky, 0:96, :] = dfc[first]
            own_b[ky, kz, 0:96, :] = dfc[second]
            oth_a[kz, ky, 0:96, :] = dproj[first]
            oth_b[ky, kz, 0:96, :] = dproj[second]

        @pl.when(c == 1)
        def _():
            oth_a[kz, ky, 0:96, :] = dfc[first]
            oth_b[ky, kz, 0:96, :] = dfc[second]
            own_a[kz, ky, 0:96, :] = dproj[first]
            own_b[ky, kz, 0:96, :] = dproj[second]

    @pl.when(j == 3)
    def _():
        ctf = ct.astype(F32)
        out_ref[...] = (middle_s[...] + ffn_s[...] + vec[7:8, :]).astype(BF16)
        dn = dn_s[...]
        xhat = xhat_s[...]
        e = dn * vec[5:6, :]
        part = e - jnp.mean(e, axis=-1, keepdims=True)
        part = part - xhat * jnp.mean(e * xhat, axis=-1, keepdims=True)
        gm = ctf + part * root_s[...]
        gm_ref[...] = gm
        gb = gm.astype(BF16)
        zero = jnp.zeros((4, D), F32)
        vg_ref[...] = jnp.concatenate(
            [
                jnp.sum(gb.astype(F32), axis=0, keepdims=True),
                jnp.sum(dn * xhat, axis=0, keepdims=True),
                jnp.sum(dn, axis=0, keepdims=True),
                jnp.sum(ctf, axis=0, keepdims=True),
                zero,
            ],
            axis=0,
        )
        for k, d in enumerate((d0, d1, d2, d3)):
            d[...] = dot_nt(gb, wout[head_rows(k), :]).astype(BF16)
            dout_s[head_rows(k), :] = dot_tn(atts[k][...], gb).astype(BF16)
        blank = jnp.zeros((16, D), BF16)
        for s in range(16):
            sz, sy = rel(s // 4, z), rel(s % 4, y)
            u = [dout_s[s * 48 + 16 * t : s * 48 + 16 * (t + 1), :] for t in range(3)]

            @pl.when(c == 0)
            def _():
                own_a[sz, sy, 96:112, :] = u[0]
                own_b[sy, sz, 96:112, :] = u[1]
                oth_a[sz, sy, 96:112, :] = u[2]
                oth_b[sy, sz, 96:112, :] = blank

            @pl.when(c == 1)
            def _():
                oth_a[sz, sy, 96:112, :] = u[0]
                oth_b[sy, sz, 96:112, :] = u[1]
                own_a[sz, sy, 96:112, :] = u[2]
                own_b[sy, sz, 96:112, :] = blank


def backward_kernel(meta, *refs):
    dos = refs[0:4]
    q_ref, k_ref, kt_ref, v_ref, attt_ref, lse_ref = refs[4:10]
    dq_ref, own_ref, oth_ref = refs[10:13]
    dk_s, dv_s, do_s = refs[13:16]
    dk_s[...] = jnp.zeros_like(dk_s)
    dv_s[...] = jnp.zeros_like(dv_s)
    for k in range(4):
        do = dos[k][...]
        for h in range(HC):
            do_s[h, k * ROWS : (k + 1) * ROWS, :] = do[:, h * HD : (h + 1) * HD]
    key_iota = lax.broadcasted_iota(jnp.int32, (KC, BT), 0)
    query_iota = lax.broadcasted_iota(jnp.int32, (KC, BT), 1)
    for i in range(8):
        pos = meta[4 + i]
        queries = [q_ref[h, i * BT : (i + 1) * BT, :] for h in range(HC)]
        grads = [do_s[h, i * BT : (i + 1) * BT, :] for h in range(HC)]
        lses = [lse_ref[i, h : h + 1, :] for h in range(HC)]
        corrs = [
            jnp.sum(grads[h].astype(F32).T * attt_ref[i, h], axis=0, keepdims=True)
            for h in range(HC)
        ]

        def step(j, carry, masked, pos=pos, queries=queries, grads=grads, lses=lses, corrs=corrs):
            base = pl.multiple_of(j * KC, KC)
            keys = pl.ds(base, KC)
            if masked:
                keep = key_iota + base <= query_iota + pos * BT
            out = []
            for h in range(HC):
                s = dot_nt(k_ref[h, keys, :], queries[h])
                p = jnp.exp(s - lses[h])
                if masked:
                    p = jnp.where(keep, p, 0.0)
                dp = dot_nt(v_ref[h, keys, :], grads[h])
                ds = (p * (dp - corrs[h])).astype(BF16)
                dv_s[h, keys, :] += dot(p.astype(BF16), grads[h])
                dk_s[h, keys, :] += dot(ds, queries[h])
                out.append(carry[h] + dot(kt_ref[h, :, keys], ds))
            return tuple(out)

        full = lax.div(pos * BT, KC)
        carry = tuple(jnp.zeros((HD, BT), F32) for _ in range(HC))
        carry = lax.fori_loop(0, full, lambda j, c: step(j, c, False), carry)
        carry = step(full, carry, True)
        for h in range(HC):
            dq_ref[i * BT : (i + 1) * BT, h * HD : (h + 1) * HD] = (
                (carry[h] * HD**-0.5).T.astype(BF16)
            )
    for i in range(8):
        here = pl.ds(pl.multiple_of(meta[4 + i] * BT, BT), BT)
        there = pl.ds(pl.multiple_of(meta[12 + i] * BT, BT), BT)
        rows = slice(i * BT, (i + 1) * BT)
        for h in range(HC):
            own_ref[rows, h * HD : (h + 1) * HD] = dk_s[h, here, :]
            own_ref[rows, CH + h * HD : CH + (h + 1) * HD] = dv_s[h, here, :]
            oth_ref[rows, h * HD : (h + 1) * HD] = dk_s[h, there, :].astype(BF16)
            oth_ref[rows, CH + h * HD : CH + (h + 1) * HD] = dv_s[h, there, :].astype(BF16)


def input_grad_kernel(dq_ref, own_ref, recv_ref, w_ref, n0, n1, n2, n3, g_ref):
    g_ref[:, :CH] = dq_ref[...]
    g_ref[:, CH:] = (own_ref[...] + recv_ref[...].astype(F32)).astype(BF16)
    w = w_ref[...]
    for k, n in enumerate((n0, n1, n2, n3)):
        n[...] = dot_nt(g_ref[k * ROWS : (k + 1) * ROWS, :], w).astype(BF16)


def weight_grad_kernel(
    meta, normed_ref, g_ref, t0, t1, t2, t3, n0, n1, n2, n3, own_ref, oth_ref, vg_ref, qv_ref, dw_s
):
    c, z, y = meta[1], meta[2], meta[3]
    g = g_ref[...]
    dw_s[...] = dot_tn(normed_ref[...], g).astype(BF16)
    blank = jnp.zeros((16, HC * CH), BF16)
    for s in range(16):
        sz, sy = rel(s // 4, z), rel(s % 4, y)
        first = dw_s[s * 48 : s * 48 + 32, :]
        second = dw_s[s * 48 + 32 : s * 48 + 48, :]

        @pl.when(c == 0)
        def _():
            own_ref[sz, sy] = first
            oth_ref[sz, sy, 0:16, :] = second
            oth_ref[sz, sy, 16:32, :] = blank

        @pl.when(c == 1)
        def _():
            oth_ref[sz, sy] = first
            own_ref[sz, sy, 0:16, :] = second
            own_ref[sz, sy, 16:32, :] = blank

    gain = jnp.zeros((1, D), F32)
    bias = jnp.zeros((1, D), F32)
    for t, n in zip((t0, t1, t2, t3), (n0, n1, n2, n3)):
        xhat, _ = standardize(t[...].astype(F32))
        ng = n[...].astype(F32)
        gain = gain + jnp.sum(ng * xhat, axis=0, keepdims=True)
        bias = bias + jnp.sum(ng, axis=0, keepdims=True)
    vg_ref[0:1, :] = gain
    vg_ref[1:2, :] = bias
    qv_ref[...] = jnp.sum(g.astype(F32), axis=0, keepdims=True)


def token_grad_kernel(tok, gm, vec, n0, n1, n2, n3, out_ref):
    ng = n0[...].astype(F32) + n1[...].astype(F32) + n2[...].astype(F32) + n3[...].astype(F32)
    xhat, root = standardize(tok[...].astype(F32))
    e = ng * vec[0:1, :]
    part = e - jnp.mean(e, axis=-1, keepdims=True)
    part = part - xhat * jnp.mean(e * xhat, axis=-1, keepdims=True)
    out_ref[...] = gm[...] + part * root


def shift(v, axis, k):
    return lax.ppermute(v, axis, [(i, (i + k) % 4) for i in range(4)])


def swap(v):
    return lax.ppermute(v, "core", [(0, 1), (1, 0)])


def gather4(v, axis):
    return [v] + [shift(v, axis, k) for k in (1, 2, 3)]


def scatter4(pieces, axis):
    total = pieces[0].astype(F32)
    for k in (1, 2, 3):
        total = total + shift(pieces[k], axis, k).astype(F32)
    return total.astype(BF16)


def in_order(pieces, index):
    up = [pieces[0], pieces[3], pieces[2], pieces[1]]
    twice = jnp.stack(up + up)
    return lax.dynamic_slice_in_dim(twice, rel(0, index), 4, axis=0)


def call(kernel, outs, scratch=(), smem=True, **kw):
    specs = [pl.BlockSpec(memory_space=pltpu.VMEM)]

    def run(*args):
        first = [pl.BlockSpec(memory_space=pltpu.SMEM)] if smem else specs
        return pl.pallas_call(
            kernel,
            out_shape=outs,
            in_specs=first + specs * (len(args) - 1),
            out_specs=jax.tree.map(lambda _: specs[0], outs),
            scratch_shapes=list(scratch),
            compiler_params=pltpu.CompilerParams(vmem_limit_bytes=56 * 2**20),
            **kw,
        )(*args)

    return run


def shp(*dims, dtype=BF16):
    return jax.ShapeDtypeStruct(dims, dtype)


def body(
    tokens,
    dealing,
    qkv_weight,
    ln1_gain,
    ln1_bias,
    q_bias,
    v_bias,
    out_weight,
    out_bias,
    ln2_gain,
    ln2_bias,
    fc_weight,
    fc_bias,
    proj_weight,
    proj_bias,
    cotangent,
):
    x = lax.axis_index("x")
    c = lax.axis_index("core")
    z = lax.axis_index("z")
    y = lax.axis_index("y")
    deal = dealing[0].reshape(4, 2, 2)
    deal_rel = in_order([deal[0], deal[3], deal[2], deal[1]], rel(0, x))
    deal_rel = jnp.stack([deal_rel[0], deal_rel[3], deal_rel[2], deal_rel[1]])
    deal_own = jnp.where(c == 0, deal_rel[:, 0], deal_rel[:, 1]).reshape(8)
    deal_oth = jnp.where(c == 0, deal_rel[:, 1], deal_rel[:, 0]).reshape(8)
    meta = jnp.concatenate([jnp.stack([x, c, z, y]).astype(jnp.int32), deal_own, deal_oth])

    tok = tokens.reshape(ROWS, D)
    cot = cotangent.reshape(ROWS, D)
    tok_own = gather4(tok, "x")
    tok_oth = [swap(t) for t in tok_own]

    wcols = lax.dynamic_index_in_dim(qkv_weight.reshape(48, 3, 4, CH), x, axis=2, keepdims=False)
    wcols = wcols.reshape(48, 3 * CH)
    row = jnp.concatenate(
        [ln1_gain, ln1_bias, q_bias, v_bias, out_bias, ln2_gain, ln2_bias, proj_bias, fc_bias]
    )
    mine = lax.broadcasted_iota(jnp.int32, (16, 1), 0) == z * 4 + y
    wbuf = jnp.concatenate([wcols, jnp.where(mine, row[None, :], jnp.zeros((), BF16))], axis=0)
    by_z = jnp.concatenate(gather4(wbuf, "z"), axis=0)
    wrel = gather4(by_z, "y")
    rows16 = sum(
        w.reshape(4, 64, 3 * CH)[k, 48:, :].astype(F32) for w in wrel for k in range(4)
    )
    vec = rows16[:, :384].reshape(16, 8, 48).transpose(1, 0, 2).reshape(8, D)
    fcb = rows16[:, 384:].reshape(1, FF)
    qvb = lax.dynamic_index_in_dim(vec[2:4].reshape(2, 4, CH), x, axis=1, keepdims=False)
    qvb = jnp.concatenate([qvb, jnp.zeros((6, CH), F32)], axis=0)

    shard = jnp.concatenate(
        [out_weight, jnp.zeros((16, D), BF16), fc_weight, proj_weight], axis=0
    )
    part = lax.dynamic_slice_in_dim(shard, (x * 2 + c) * 56, 56, axis=0)
    wall = lax.all_gather(part, ("z", "y", "x", "core"), axis=0, tiled=True).reshape(16, 448, D)
    wout = wall[:, :48].reshape(D, D)

    fwd = call(
        forward_kernel,
        [shp(ROWS, CH)] * 4
        + [
            shp(8, HC, HD, BT, dtype=F32),
            shp(8, 8, BT, dtype=F32),
            shp(HC, 1024, HD),
            shp(HC, SEQ, HD),
            shp(HC, HD, SEQ),
            shp(HC, SEQ, HD),
            shp(1024, D),
            shp(D, 3 * CH),
        ],
        [pltpu.VMEM((HC, HD, SEQ), BF16)],
        name="attention_forward",
    )(meta, *tok_own, *tok_oth, *wrel, vec, qvb)
    att, (attt, lse, q, kk, kt, v, normed, w) = fwd[:4], fwd[4:]
    att_rel = [att[0]] + [shift(att[k], "x", -k) for k in (1, 2, 3)]

    whole = lambda *dims: pl.BlockSpec(dims, lambda j: (0,) * len(dims))
    mlp_outs = (
        [shp(ROWS, D), shp(ROWS, D, dtype=F32)]
        + [shp(ROWS, CH)] * 4
        + [shp(4, 4, 112, D)] * 4
        + [shp(8, D, dtype=F32), shp(1, FF, dtype=F32)]
    )
    mlp = pl.pallas_call(
        mlp_kernel,
        grid=(4,),
        out_shape=mlp_outs,
        in_specs=[pl.BlockSpec(memory_space=pltpu.SMEM)]
        + [whole(ROWS, CH)] * 4
        + [whole(ROWS, D), whole(ROWS, D), whole(D, D), whole(8, D), whole(1, FF)]
        + [pl.BlockSpec((4, 448, D), lambda j: (j, 0, 0))],
        out_specs=[whole(*o.shape) for o in mlp_outs],
        scratch_shapes=[
            pltpu.VMEM((ROWS, D), F32),
            pltpu.VMEM((ROWS, D), F32),
            pltpu.VMEM((ROWS, 1), F32),
            pltpu.VMEM((ROWS, D), BF16),
            pltpu.VMEM((ROWS, D), F32),
            pltpu.VMEM((ROWS, D), F32),
            pltpu.VMEM((D, D), BF16),
        ],
        compiler_params=pltpu.CompilerParams(vmem_limit_bytes=56 * 2**20),
        name="feed_forward",
    )(meta, *att_rel, tok, cot, wout, vec, fcb, wall)
    outcome, gm = mlp[0], mlp[1]
    datt, (own_a, own_b, oth_a, oth_b), (vg2, fcg) = mlp[2:6], mlp[6:10], mlp[10:12]

    datt_rel = [datt[0]] + [shift(datt[k], "x", k) for k in (1, 2, 3)]
    recv_a, recv_b = swap(oth_a), swap(oth_b)

    dq, dkv_own, dkv_oth = call(
        backward_kernel,
        [shp(1024, CH), shp(1024, 2 * CH, dtype=F32), shp(1024, 2 * CH)],
        [
            pltpu.VMEM((HC, SEQ, HD), F32),
            pltpu.VMEM((HC, SEQ, HD), F32),
            pltpu.VMEM((HC, 1024, HD), BF16),
        ],
        name="attention_backward",
    )(meta, *datt_rel, q, kk, kt, v, attt, lse)
    dkv_recv = swap(dkv_oth)

    sum_a = [(own_a[k].astype(F32) + recv_a[k].astype(F32)).astype(BF16) for k in range(4)]
    sum_b = [(own_b[k].astype(F32) + recv_b[k].astype(F32)).astype(BF16) for k in range(4)]
    za = scatter4(sum_a, "z")
    yb = scatter4(sum_b, "y")
    fa = scatter4([za[k] for k in range(4)], "y")
    fb = scatter4([yb[k] for k in range(4)], "z")
    quarters = jnp.concatenate([fa, fb], axis=0).reshape(4, 56, D)
    quarters = lax.dynamic_slice_in_dim(jnp.concatenate([quarters, quarters]), x, 4, axis=0)
    quarter = scatter4([quarters[k] for k in range(4)], "x")
    half = in_order(gather4(quarter, "x"), x).reshape(224, D)
    half_oth = swap(half)
    low = jnp.where(c == 0, half, half_oth).astype(F32)
    high = jnp.where(c == 0, half_oth, half).astype(F32)
    grad_fc_w = jnp.concatenate([low[0:96], low[112:208]], axis=0)
    grad_proj_w = jnp.concatenate([high[0:96], high[112:208]], axis=0)
    grad_out_w = jnp.concatenate([low[96:112], low[208:224], high[96:112]], axis=0)

    ng0, ng1, ng2, ng3, g = call(
        input_grad_kernel,
        [shp(ROWS, D)] * 4 + [shp(1024, 3 * CH)],
        smem=False,
        name="input_grad",
    )(dq, dkv_own, dkv_recv, w)
    ng_rel = [ng0] + [shift(n, "x", -k) for k, n in ((1, ng1), (2, ng2), (3, ng3))]
    wq_own, wq_oth, vg1, qvg = call(
        weight_grad_kernel,
        [
            shp(4, 4, 32, 3 * CH),
            shp(4, 4, 32, 3 * CH),
            shp(8, D, dtype=F32),
            shp(1, 3 * CH, dtype=F32),
        ],
        [pltpu.VMEM((D, 3 * CH), BF16)],
        name="weight_grad",
    )(meta, normed, g, *tok_own, ng0, ng1, ng2, ng3)
    token_grad = call(
        token_grad_kernel, shp(ROWS, D, dtype=F32), smem=False, name="token_grad"
    )(tok, gm, vec, *ng_rel)

    place = lambda part: lax.dynamic_update_slice(jnp.zeros((1, D), F32), part, (0, x * CH))
    vg = jnp.concatenate(
        [vg1[0:2], place(qvg[:, :CH]), place(qvg[:, 2 * CH :]), vg2[0:4]], axis=0
    )
    vrows = jnp.concatenate(
        [vg.reshape(8, 16, 48).transpose(1, 0, 2).reshape(16, 384), fcg.reshape(16, 192)], axis=1
    )
    vrows = vrows + swap(vrows)
    vrows = sum(gather4(vrows, "z"))
    vrows = sum(gather4(vrows, "y"))
    vrow = lax.dynamic_slice_in_dim(vrows, z * 4 + y, 1, axis=0)
    vrow = in_order(gather4(vrow, "x"), x)
    vrow = (vrow[0] + vrow[1] + vrow[2] + vrow[3])[0]

    wq_recv = swap(wq_oth)
    wq = [(wq_own[k].astype(F32) + wq_recv[k].astype(F32)).astype(BF16) for k in range(4)]
    wq = scatter4(wq, "z")
    wq = scatter4([wq[k] for k in range(4)], "y")
    wq_x = in_order(gather4(wq, "x"), x)
    wq_x_oth = swap(wq_x)
    grad_qkv = jnp.concatenate(
        [jnp.where(c == 0, wq_x, wq_x_oth), jnp.where(c == 0, wq_x_oth, wq_x)[:, :16]], axis=1
    )
    grad_qkv = (
        grad_qkv.reshape(4, 48, 3, CH).transpose(1, 2, 0, 3).reshape(48, 3 * D).astype(F32)
    )

    vecs = [vrow[k * 48 : (k + 1) * 48] for k in range(8)]
    return (
        outcome.reshape(tokens.shape),
        token_grad.reshape(tokens.shape),
        grad_qkv,
        vecs[0],
        vecs[1],
        vecs[2],
        vecs[3],
        grad_out_w,
        vecs[4],
        vecs[5],
        vecs[6],
        grad_fc_w,
        vrow[384:],
        grad_proj_w,
        vecs[7],
    )


def solution(mesh):
    split = Mesh(mesh.devices.reshape(4, 2, 4, 4), ("x", "core", "z", "y"))
    fsdp = ("z", "y")
    ctx = ("x", "core")
    act = P(fsdp, ctx, None, None)
    mat = P(fsdp, None)
    one = P(fsdp)
    return jax.shard_map(
        body,
        mesh=split,
        in_specs=(act, mat, mat, one, one, one, one, mat, one, one, one, mat, one, mat, one, act),
        out_specs=(act, act, mat, one, one, one, one, mat, one, one, one, mat, one, mat, one),
        check_vma=False,
    )
```

time: 783 us -> 348 us (0.44)
  waiting for transfers between devices: 391 us -> 112 us
  blocking collectives: 151 us -> 0 us
  matrix products: 120 us -> 0 us
  starting transfers between devices: 1.22 us -> 92.6 us
  Pallas kernels: 0 us -> 91.2 us
  other arithmetic: 45.2 us -> 10.4 us
  local copies, waits for them, and re-layouts: 50.1 us -> 21.2 us
    reduce_scatter x5 -> x0, waiting for transfers between devices: 222 us -> none  [the longest x1 81.2 us: body(): lax.psum_scatter(grad_proj_w.astype(jnp.bfloat16), 'fsdp', scatter_dimens...]
    unnamed x2 -> x0, blocking collectives: 124 us -> none
    dot_general x18 -> x0, matrix products: 120 us -> none  [the longest x4 19.7 us: contract_cols(): lax.dot_general(left_side, right_side, (((1,), (1,)), ((), ())), preferre...]
    ppermute x0 -> x65, waiting for transfers between devices: none -> 95.8 us  [the longest x54 88.2 us: shift(): return lax.ppermute(v, axis, [(i, (i + k) % 4) for i in range(4)])]
    ppermute x0 -> x65, starting transfers between devices: none -> 92.6 us  [the longest x54 73.1 us: shift(): return lax.ppermute(v, axis, [(i, (i + k) % 4) for i in range(4)])]
    pallas_call x0 -> x6, Pallas kernels: none -> 91.2 us  [the longest x5 71.1 us: run(): pl.pallas_call(kernel, out_shape=outs, in_specs=first + specs * (len(args...]
    all_gather x5 -> x1, waiting for transfers between devices: 105 us -> 16.6 us  [body(): lax.all_gather(part, ('z', 'y', 'x', 'core'), axis=0, tiled=True)]
    psum x1 -> x0, waiting for transfers between devices: 61.7 us -> none  [body(): lax.psum(grad_qkv_w.astype(jnp.bfloat16), 'ctx').astype(jnp.float32)]
  transfers between devices with their start and end apart: 11 -> 66, of which waited for: 8 -> 30; matrix products, arithmetic and copies ran while one was open for 16% -> 6% of each run, Pallas kernels for 0% -> 10%
where the time goes in v1:
time: 348 us; the launch traced here: 343 us
  waiting for transfers between devices  112 us (32%)
  starting transfers between devices  92.6 us (27%)
  Pallas kernels  91.2 us (26%)
  local copies, waits for them, and re-layouts  21.2 us (6%)
  between operations  15.1 us (4%)
  other arithmetic  10.4 us (3%)
    ppermute x54, waiting for transfers between devices, shift(): return lax.ppermute(v, axis, [(i, (i + k) % 4) for i in range(4)])  88.2 us
    ppermute x54, starting transfers between devices, shift(): return lax.ppermute(v, axis, [(i, (i + k) % 4) for i in range(4)])  73.1 us
    pallas_call x5, Pallas kernels, run(): pl.pallas_call(kernel, out_shape=outs, in_specs=first + specs * (len(args...  71.1 us
    pallas_call x1, Pallas kernels, body(): pl.pallas_call(mlp_kernel, grid=(4,), out_shape=mlp_outs, in_specs=[pl.Bl...  20.1 us
    ppermute x11, starting transfers between devices, swap(): return lax.ppermute(v, 'core', [(0, 1), (1, 0)])  19.5 us
    all_gather x1, waiting for transfers between devices, body(): lax.all_gather(part, ('z', 'y', 'x', 'core'), axis=0, tiled=True)  16.6 us
    ppermute x11, waiting for transfers between devices, swap(): return lax.ppermute(v, 'core', [(0, 1), (1, 0)])  7.59 us
    unnamed x97, local copies, waits for them, and re-layouts  7.15 us
  transfers between devices with their start and end apart: 66, of which 30 were waited for; matrix products, arithmetic and copies ran while one was open for 6% of the time, Pallas kernels for 10%

profile of v1, /device:TPU:1, one launch (start us, length us, event | category | flops | bytes accessed | tf_op | source)
XLA Modules:
  0.0 342.9 jit_solution(5788069393062098623)
XLA Ops:
  7.5 1.6 fusion.32
  9.1 1.2 reshape.284
  11.3 2.5 collective-permute-start.7
  13.8 3.3 collective-permute-start.8
  18.1 2.3 collective-permute-done.8
  20.5 1.4 collective-permute-start.10
  21.8 1.2 collective-permute-start
  23.0 2.5 collective-permute-start.1
  25.5 1.2 collective-permute-start.2
  26.7 2.6 collective-permute-start.11
  30.0 1.1 collective-permute-start.12
  31.2 7.3 %collective-permute-done.11.refs_10_ = bf16[256,576]{1,0:T(8,128)(2,1)S(1)} collective-permute-done((bf16[256,576]{1,0:T(8,128)(2,1)S(1)}, bf16[256,576]{1,0:T(8,128)(2,1)S(1)}, u32[]{:S(2)}, u32[]{:S(2)}) %collective-permute-start.11) | collective-permute-done | bytes 294944 | tf_op jit(solution)/shard_map/ppermute | solution.py:393
  38.4 2.5 collective-permute-start.3
  41.6 3.4 collective-permute-start.5
  48.6 29.6 %attention_forward.1 = (bf16[256,192]{1,0:T(8,128)(2,1)}, bf16[256,192]{1,0:T(8,128)(2,1)}, bf16[256,192]{1,0:T(8,128)(2,1)}, bf16[256,192]{1,0:T(8,128)(2,1)}, ...) custom-call(s32[20]{0:T(128)} %concatenate.43.meta, ...), custom_call_target="tpu_custom_call" | custom-call | tf_op jit(solution)/shard_map/attention_forward/pallas_call | solution.py:422
  78.2 1.9 collective-permute-start.13
  82.1 16.6 %all-gather.2.cloned.1.call-done = bf16[7168,768]{1,0:T(8,128)(2,1)} async-done(((bf16[56,768]{1,0:T(8,128)(2,1)}), bf16[7168,768]{1,0:T(8,128)(2,1)}) %all-gather.2.cloned.1.call-update) | async-done | bytes 11010064 | tf_op jit(solution)/shard_map/all_gather | solution.py:494
  98.7 2.4 slice.459
  101.9 20.1 %feed_forward.1 = (bf16[256,768]{1,0:T(8,128)(2,1)}, f32[256,768]{1,0:T(8,128)}, bf16[256,192]{1,0:T(8,128)(2,1)}, bf16[256,192]{1,0:T(8,128)(2,1)}, bf16[256,19...) custom-call(s32[20]{0:T(128)} %concatenate.43.meta, ...), custom_call_target="tpu_custom_call" | custom-call | tf_op jit(solution)/shard_map/feed_forward/pallas_call | solution.py:523
  123.1 1.6 collective-permute-start.18
  124.7 6.5 %collective-permute-done.16.refs_1_ = bf16[256,192]{1,0:T(8,128)(2,1)S(1)} collective-permute-done((bf16[256,192]{1,0:T(8,128)(2,1)}, bf16[256,192]{1,0:T(8,128)(2,1)S(1)}, u32[]{:S(2)}, u32[]{:S(2)}) %collective-permute-start.16) | collective-permute-done | bytes 98336 | tf_op jit(solution)/shard_map/ppermute | solution.py:393
  132.1 26.7 %attention_backward.1 = (bf16[1024,192]{1,0:T(8,128)(2,1)}, f32[1024,384]{1,0:T(8,128)}, bf16[1024,384]{1,0:T(8,128)(2,1)}) custom-call(s32[20]{0:T(128)} %concatenate.43.meta, bf16[256,192]{1,0:T(8,128)(2,1)} %get-tuple-element.57.refs_0_, bf16[256,192]{1,0:T(8,128)(2,1)} %copy-done.22, bf16[256,192]{1,0:T(8,128)(2,1)} %copy-done.23, ...), custom_call_target="tpu_custom_call" | custom-call | tf_op jit(solution)/shard_map/attention_backward/pallas_call | solution.py:422
  160.0 1.2 collective-permute-done.19.recv_ref
  162.1 4.7 %input_grad.1 = (bf16[256,768]{1,0:T(8,128)(2,1)}, bf16[256,768]{1,0:T(8,128)(2,1)}, bf16[256,768]{1,0:T(8,128)(2,1)}, bf16[256,768]{1,0:T(8,128)(2,1)}, bf16[1024,576]{1,0:T(8,128)(2,1)}) custom-call(bf16[1024,192]{1,0:T(8,128)(2,1)} %get-tuple-element.67.dq_ref, f32[1024,384]{1,0:T(8,128)} %get-tuple-element.68.own_ref, bf16[1024,384]{1,0:T(8,128)(2,1)} %copy-done.6, ...), custom_call_target="tpu_custom_call" | custom-call | tf_op jit(solution)/shard_map/input_grad/pallas_call | solution.py:422
  166.8 6.8 %weight_grad.1 = (bf16[4,4,32,576]{3,2,1,0:T(8,128)(2,1)}, bf16[4,4,32,576]{3,2,1,0:T(8,128)(2,1)}, f32[8,768]{1,0:T(8,128)}, f32[1,576]{1,0:T(1,128)}) custom-call(s32[20]{0:T(128)} %concatenate.43.meta, bf16[1024,768]{1,0:T(8,128)(2,1)} %get-tuple-element.75.normed_ref, bf16[1024,576]{1,0:T(8,128)(2,1)} %get-tuple-element.76.g_ref, ...), custom_call_target="tpu_custom_call" | custom-call | tf_op jit(solution)/shard_map/weight_grad/pallas_call | solution.py:422
  176.9 1.6 collective-permute-start.35
  178.5 2.6 collective-permute-start.36
  181.7 1.5 collective-permute-done.36
  184.7 2.8 collective-permute-start.39
  187.6 1.9 collective-permute-start.40
  189.5 1.2 collective-permute-done.40
  190.7 3.5 %collective-permute-start.41 = (f32[1,576]{1,0:T(1,128)S(1)}, f32[1,576]{1,0:T(1,128)S(1)}, u32[]{:S(2)}, u32[]{:S(2)}) collective-permute-start(f32[1,576]{1,0:T(1,128)S(1)} %get-tuple-element.94), channel_id=1, source_target_pairs={{0,96},{32,0},{64,32},{96,64},{1,97},{33,1},{65,33},{97,65},{2,98}... | collective-permute-start | bytes 6920 | tf_op jit(solution)/shard_map/ppermute | solution.py:393
  194.2 3.3 collective-permute-start.44
  198.4 3.5 %collective-permute-done.42 = f32[1,576]{1,0:T(1,128)S(1)} collective-permute-done((f32[1,576]{1,0:T(1,128)S(1)}, f32[1,576]{1,0:T(1,128)S(1)}, u32[]{:S(2)}, u32[]{:S(2)}) %collective-permute-start.42) | collective-permute-done | bytes 2336 | tf_op jit(solution)/shard_map/ppermute | solution.py:393
  202.0 5.3 %collective-permute-done.23 = bf16[4,4,32,576]{3,2,1,0:T(8,128)(2,1)S(1)} collective-permute-done((bf16[4,4,32,576]{3,2,1,0:T(8,128)(2,1)}, bf16[4,4,32,576]{3,2,1,0:T(8,128)(2,1)S(1)}, u32[]{:S(2)}, u32[]{:S(2)}) %collective-permute-start.23) | collective-permute-done | bytes 589856 | tf_op jit(solution)/shard_map/ppermute | solution.py:397
  207.3 1.2 fusion.28
  209.4 3.6 %collective-permute-start.25 = (bf16[4,32,576]{2,1,0:T(8,128)(2,1)S(1)}, bf16[4,32,576]{2,1,0:T(8,128)(2,1)S(1)}, u32[]{:S(2)}, u32[]{:S(2)}) collective-permute-start(bf16[4,32,576]{2,1,0:T(8,128)(2,1)S(1)} %get-tuple-element.105), channel_id=1, source_target_pairs={{0,8},{4,12},{8,0},{12,4},{1,9},{5,13},{9,1},{13,5},{2,10},{6,14},... | collective-permute-start | bytes 442376 | tf_op jit(solution)/shard_map/ppermute | solution.py:393
  213.0 2.9 collective-permute-done.24
  215.8 4.6 %collective-permute-done.25 = bf16[4,32,576]{2,1,0:T(8,128)(2,1)S(1)} collective-permute-done((bf16[4,32,576]{2,1,0:T(8,128)(2,1)S(1)}, bf16[4,32,576]{2,1,0:T(8,128)(2,1)S(1)}, u32[]{:S(2)}, u32[]{:S(2)}) %collective-permute-start.25) | collective-permute-done | bytes 147488 | tf_op jit(solution)/shard_map/ppermute | solution.py:393
  222.4 3.6 %collective-permute-start.28 = (bf16[32,576]{1,0:T(8,128)(2,1)S(1)}, bf16[32,576]{1,0:T(8,128)(2,1)S(1)}, u32[]{:S(2)}, u32[]{:S(2)}) collective-permute-start(bf16[32,576]{1,0:T(8,128)(2,1)S(1)} %get-tuple-element.125), channel_id=1, source_target_pairs={{0,2},{1,3},{2,0},{3,1},{4,6},{5,7},{6,4},{7,5},{8,10},{9,11},{10,... | collective-permute-start | bytes 110600 | tf_op jit(solution)/shard_map/ppermute | solution.py:393
  226.2 1.8 collective-permute-start.29
  228.0 1.3 collective-permute-done.29
  230.0 2.7 collective-permute-start.30
  233.8 4.0 %collective-permute-done.21.n2 = bf16[256,768]{1,0:T(8,128)(2,1)S(1)} collective-permute-done((bf16[256,768]{1,0:T(8,128)(2,1)S(1)}, bf16[256,768]{1,0:T(8,128)(2,1)S(1)}, u32[]{:S(2)}, u32[]{:S(2)}) %collective-permute-start.21) | collective-permute-done | bytes 393248 | tf_op jit(solution)/shard_map/ppermute | solution.py:393
  237.9 11.1 %collective-permute-done.22.n3 = bf16[256,768]{1,0:T(8,128)(2,1)S(1)} collective-permute-done((bf16[256,768]{1,0:T(8,128)(2,1)S(1)}, bf16[256,768]{1,0:T(8,128)(2,1)S(1)}, u32[]{:S(2)}, u32[]{:S(2)}) %collective-permute-start.22) | collective-permute-done | bytes 393248 | tf_op jit(solution)/shard_map/ppermute | solution.py:393
  249.8 3.4 token_grad.1
  253.8 4.0 %collective-permute-done.31 = bf16[32,576]{1,0:T(8,128)(2,1)S(1)} collective-permute-done((bf16[32,576]{1,0:T(8,128)(2,1)}, bf16[32,576]{1,0:T(8,128)(2,1)S(1)}, u32[]{:S(2)}, u32[]{:S(2)}) %collective-permute-start.31) | collective-permute-done | bytes 36896 | tf_op jit(solution)/shard_map/ppermute | solution.py:393
  259.1 1.4 constant_dynamic-update-slice_fusion.8
  261.9 3.0 collective-permute-start.46
  265.6 2.4 collective-permute-start.53
  268.0 9.6 %collective-permute-done.45 = bf16[4,112,768]{2,1,0:T(8,128)(2,1)S(1)} collective-permute-done((bf16[4,112,768]{2,1,0:T(8,128)(2,1)S(1)}, bf16[4,112,768]{2,1,0:T(8,128)(2,1)S(1)}, u32[]{:S(2)}, u32[]{:S(2)}) %collective-permute-start.45) | collective-permute-done | bytes 688160 | tf_op jit(solution)/shard_map/ppermute | solution.py:393
  278.6 14.8 %collective-permute-done.46 = bf16[4,112,768]{2,1,0:T(8,128)(2,1)S(1)} collective-permute-done((bf16[4,112,768]{2,1,0:T(8,128)(2,1)S(1)}, bf16[4,112,768]{2,1,0:T(8,128)(2,1)S(1)}, u32[]{:S(2)}, u32[]{:S(2)}) %collective-permute-start.46) | collective-permute-done | bytes 688160 | tf_op jit(solution)/shard_map/ppermute | solution.py:393
  294.9 2.4 collective-permute-start.49
  297.2 1.7 collective-permute-start.50
  299.5 1.7 collective-permute-start.55
  301.2 2.9 collective-permute-start.56
  306.1 4.6 %collective-permute-done.56 = bf16[112,768]{1,0:T(8,128)(2,1)S(1)} collective-permute-done((bf16[112,768]{1,0:T(8,128)(2,1)S(1)}, bf16[112,768]{1,0:T(8,128)(2,1)S(1)}, u32[]{:S(2)}, u32[]{:S(2)}) %collective-permute-start.56) | collective-permute-done | bytes 172064 | tf_op jit(solution)/shard_map/ppermute | solution.py:393
  311.0 1.6 collective-permute-start.59
  312.6 1.5 collective-permute-start.60
  314.1 3.5 %collective-permute-start.33 = (bf16[4,32,576]{2,1,0:T(8,128)(2,1)S(1)}, bf16[4,32,576]{2,1,0:T(8,128)(2,1)S(1)}, u32[]{:S(2)}, u32[]{:S(2)}) collective-permute-start(bf16[4,32,576]{2,1,0:T(8,128)(2,1)S(1)} %constant_dynamic-slice_fusion.12), channel_id=1, source_target_pairs={{0,16},{16,0},{1,17},{17,1},{2,18},{18,2},{3,19},{19,3},{4,20},{20... | collective-permute-start | bytes 442376 | tf_op jit(solution)/shard_map/ppermute | solution.py:397
  317.7 2.0 collective-permute-start.61
  321.4 3.3 collective-permute-done.62
  325.7 5.6 %collective-permute-start.64 = (bf16[224,768]{1,0:T(8,128)(2,1)S(1)}, bf16[224,768]{1,0:T(8,128)(2,1)S(1)}, u32[]{:S(2)}, u32[]{:S(2)}) collective-permute-start(bf16[224,768]{1,0:T(8,128)(2,1)S(1)} %bitcast.184), channel_id=1, source_target_pairs={{0,16},{16,0},{1,17},{17,1},{2,18},{18,2},{3,19},{19,3},{4,20},{20... | collective-permute-start | bytes 1032200 | tf_op jit(solution)/shard_map/ppermute | solution.py:397
  332.1 1.1 reshape.318
  (265 shorter events, 41.2 us)
Async XLA Ops:
  7.3 91.4 %all-gather.2.cloned.1.call-start = ((), (), s32[]{:S(2)}) async-start(), calls=%async_computation | async-start | bytes 11096064 | tf_op jit(solution)/shard_map/all_gather | solution.py:494
  11.3 6.8 %collective-permute-start.7 = (bf16[64,576]{1,0:T(8,128)(2,1)S(1)}, bf16[64,576]{1,0:T(8,128)(2,1)S(1)}, u32[]{:S(2)}, u32[]{:S(2)}) collective-permute-start(bf16[64,576]{1,0:T(8,128)(2,1)S(1)} %pad_maximum_fusion.4), channel_id=1, source_target_pairs={{0,4},{4,8},{8,12},{12,0},{1,5},{5,9},{9,13},{13,1},{2,6},{6,10},{... | collective-permute-start | bytes 221192 | tf_op jit(solution)/shard_map/ppermute | solution.py:393
  13.8 6.6 %collective-permute-start.8 = (bf16[64,576]{1,0:T(8,128)(2,1)S(1)}, bf16[64,576]{1,0:T(8,128)(2,1)S(1)}, u32[]{:S(2)}, u32[]{:S(2)}) collective-permute-start(bf16[64,576]{1,0:T(8,128)(2,1)S(1)} %pad_maximum_fusion.4), channel_id=1, source_target_pairs={{0,8},{4,12},{8,0},{12,4},{1,9},{5,13},{9,1},{13,5},{2,10},{6,14},... | collective-permute-start | bytes 221192 | tf_op jit(solution)/shard_map/ppermute | solution.py:393
  17.1 3.3 collective-permute-start.9
  20.5 9.5 %collective-permute-start.10 = (bf16[256,576]{1,0:T(8,128)(2,1)S(1)}, bf16[256,576]{1,0:T(8,128)(2,1)S(1)}, u32[]{:S(2)}, u32[]{:S(2)}) collective-permute-start(bf16[256,576]{1,0:T(8,128)(2,1)S(1)} %constant_dynamic-update-slice_fusion.refs_8_), channel_id=1, source_target_pairs={{0,1},{1,2},{2,3},{3,0},{4,5},{5,6},{6,7},{7,4},{8,9},{9,10},{10,1... | collective-permute-start | bytes 884744 | tf_op jit(solution)/shard_map/ppermute | solution.py:393
  21.8 19.1 %collective-permute-start = (bf16[256,768]{1,0:T(8,128)(2,1)S(1)}, bf16[256,768]{1,0:T(8,128)(2,1)S(1)}, u32[]{:S(2)}, u32[]{:S(2)}) collective-permute-start(bf16[256,768]{1,0:T(8,128)(2,1)S(1)} %bitcast.177), channel_id=1, source_target_pairs={{0,32},{32,64},{64,96},{96,0},{1,33},{33,65},{65,97},{97,1},{2,34}... | collective-permute-start | bytes 1179656 | tf_op jit(solution)/shard_map/ppermute | solution.py:393
  23.0 18.5 %collective-permute-start.1 = (bf16[256,768]{1,0:T(8,128)(2,1)S(1)}, bf16[256,768]{1,0:T(8,128)(2,1)S(1)}, u32[]{:S(2)}, u32[]{:S(2)}) collective-permute-start(bf16[256,768]{1,0:T(8,128)(2,1)S(1)} %bitcast.178), channel_id=1, source_target_pairs={{0,64},{32,96},{64,0},{96,32},{1,65},{33,97},{65,1},{97,33},{2,66}... | collective-permute-start | bytes 1179656 | tf_op jit(solution)/shard_map/ppermute | solution.py:393
  25.5 19.4 %collective-permute-start.2 = (bf16[256,768]{1,0:T(8,128)(2,1)S(1)}, bf16[256,768]{1,0:T(8,128)(2,1)S(1)}, u32[]{:S(2)}, u32[]{:S(2)}) collective-permute-start(bf16[256,768]{1,0:T(8,128)(2,1)S(1)} %bitcast.179), channel_id=1, source_target_pairs={{0,96},{32,0},{64,32},{96,64},{1,97},{33,1},{65,33},{97,65},{2,98}... | collective-permute-start | bytes 1179656 | tf_op jit(solution)/shard_map/ppermute | solution.py:393
  26.7 11.7 %collective-permute-start.11 = (bf16[256,576]{1,0:T(8,128)(2,1)S(1)}, bf16[256,576]{1,0:T(8,128)(2,1)S(1)}, u32[]{:S(2)}, u32[]{:S(2)}) collective-permute-start(bf16[256,576]{1,0:T(8,128)(2,1)S(1)} %constant_dynamic-update-slice_fusion.refs_8_), channel_id=1, source_target_pairs={{0,2},{1,3},{2,0},{3,1},{4,6},{5,7},{6,4},{7,5},{8,10},{9,11},{10,... | collective-permute-start | bytes 884744 | tf_op jit(solution)/shard_map/ppermute | solution.py:393
  30.0 16.3 %collective-permute-start.12 = (bf16[256,576]{1,0:T(8,128)(2,1)S(1)}, bf16[256,576]{1,0:T(8,128)(2,1)S(1)}, u32[]{:S(2)}, u32[]{:S(2)}) collective-permute-start(bf16[256,576]{1,0:T(8,128)(2,1)S(1)} %constant_dynamic-update-slice_fusion.refs_8_), channel_id=1, source_target_pairs={{0,3},{1,0},{2,1},{3,2},{4,7},{5,4},{6,5},{7,6},{8,11},{9,8},{10,9... | collective-permute-start | bytes 884744 | tf_op jit(solution)/shard_map/ppermute | solution.py:393
  38.4 9.4 %collective-permute-start.3 = (bf16[256,768]{1,0:T(8,128)(2,1)S(1)}, bf16[256,768]{1,0:T(8,128)(2,1)S(1)}, u32[]{:S(2)}, u32[]{:S(2)}) collective-permute-start(bf16[256,768]{1,0:T(8,128)(2,1)S(1)} %bitcast.180), channel_id=1, source_target_pairs={{0,16},{16,0},{1,17},{17,1},{2,18},{18,2},{3,19},{19,3},{4,20},{20... | collective-permute-start | bytes 1179656 | tf_op jit(solution)/shard_map/ppermute | solution.py:397
  41.0 6.9 %collective-permute-start.4 = (bf16[256,768]{1,0:T(8,128)(2,1)S(1)}, bf16[256,768]{1,0:T(8,128)(2,1)}, u32[]{:S(2)}, u32[]{:S(2)}) collective-permute-start(bf16[256,768]{1,0:T(8,128)(2,1)S(1)} %collective-permute-done.refs_1_.t1), channel_id=1, source_target_pairs={{0,16},{16,0},{1,17},{17,1},{2,18},{18,2},{3,19},{19,3},{4,20},{20... | collective-permute-start | bytes 1179656 | tf_op jit(solution)/shard_map/ppermute | solution.py:397
  41.6 6.3 %collective-permute-start.5 = (bf16[256,768]{1,0:T(8,128)(2,1)S(1)}, bf16[256,768]{1,0:T(8,128)(2,1)}, u32[]{:S(2)}, u32[]{:S(2)}) collective-permute-start(bf16[256,768]{1,0:T(8,128)(2,1)S(1)} %collective-permute-done.1.refs_2_.t2), channel_id=1, source_target_pairs={{0,16},{16,0},{1,17},{17,1},{2,18},{18,2},{3,19},{19,3},{4,20},{20... | collective-permute-start | bytes 1179656 | tf_op jit(solution)/shard_map/ppermute | solution.py:397
  44.9 3.0 collective-permute-start.6
  78.2 23.0 %collective-permute-start.13 = (bf16[256,192]{1,0:T(8,128)(2,1)}, bf16[256,192]{1,0:T(8,128)(2,1)S(1)}, u32[]{:S(2)}, u32[]{:S(2)}) collective-permute-start(bf16[256,192]{1,0:T(8,128)(2,1)} %get-tuple-element.52), channel_id=1, source_target_pairs={{0,96},{32,0},{64,32},{96,64},{1,97},{33,1},{65,33},{97,65},{2,98}... | collective-permute-start | bytes 294920 | tf_op jit(solution)/shard_map/ppermute | solution.py:393
  80.1 21.0 %collective-permute-start.14 = (bf16[256,192]{1,0:T(8,128)(2,1)}, bf16[256,192]{1,0:T(8,128)(2,1)S(1)}, u32[]{:S(2)}, u32[]{:S(2)}) collective-permute-start(bf16[256,192]{1,0:T(8,128)(2,1)} %get-tuple-element.53), channel_id=1, source_target_pairs={{0,64},{32,96},{64,0},{96,32},{1,65},{33,97},{65,1},{97,33},{2,66}... | collective-permute-start | bytes 294920 | tf_op jit(solution)/shard_map/ppermute | solution.py:393
  81.0 20.2 %collective-permute-start.15 = (bf16[256,192]{1,0:T(8,128)(2,1)}, bf16[256,192]{1,0:T(8,128)(2,1)S(1)}, u32[]{:S(2)}, u32[]{:S(2)}) collective-permute-start(bf16[256,192]{1,0:T(8,128)(2,1)} %get-tuple-element.54), channel_id=1, source_target_pairs={{0,32},{32,64},{64,96},{96,0},{1,33},{33,65},{65,97},{97,1},{2,34}... | collective-permute-start | bytes 294920 | tf_op jit(solution)/shard_map/ppermute | solution.py:393
  121.9 9.2 %collective-permute-start.16 = (bf16[256,192]{1,0:T(8,128)(2,1)}, bf16[256,192]{1,0:T(8,128)(2,1)S(1)}, u32[]{:S(2)}, u32[]{:S(2)}) collective-permute-start(bf16[256,192]{1,0:T(8,128)(2,1)} %get-tuple-element.58), channel_id=1, source_target_pairs={{0,32},{32,64},{64,96},{96,0},{1,33},{33,65},{65,97},{97,1},{2,34}... | collective-permute-start | bytes 294920 | tf_op jit(solution)/shard_map/ppermute | solution.py:393
  122.0 9.1 %collective-permute-start.17 = (bf16[256,192]{1,0:T(8,128)(2,1)}, bf16[256,192]{1,0:T(8,128)(2,1)S(1)}, u32[]{:S(2)}, u32[]{:S(2)}) collective-permute-start(bf16[256,192]{1,0:T(8,128)(2,1)} %get-tuple-element.59), channel_id=1, source_target_pairs={{0,64},{32,96},{64,0},{96,32},{1,65},{33,97},{65,1},{97,33},{2,66}... | collective-permute-start | bytes 294920 | tf_op jit(solution)/shard_map/ppermute | solution.py:393
  123.1 8.3 %collective-permute-start.18 = (bf16[256,192]{1,0:T(8,128)(2,1)}, bf16[256,192]{1,0:T(8,128)(2,1)S(1)}, u32[]{:S(2)}, u32[]{:S(2)}) collective-permute-start(bf16[256,192]{1,0:T(8,128)(2,1)} %get-tuple-element.60), channel_id=1, source_target_pairs={{0,96},{32,0},{64,32},{96,64},{1,97},{33,1},{65,33},{97,65},{2,98}... | collective-permute-start | bytes 294920 | tf_op jit(solution)/shard_map/ppermute | solution.py:393
  176.9 4.8 %collective-permute-start.35 = (f32[16,576]{1,0:T(8,128)S(1)}, f32[16,576]{1,0:T(8,128)S(1)}, u32[]{:S(2)}, u32[]{:S(2)}) collective-permute-start(f32[16,576]{1,0:T(8,128)S(1)} %add.302), channel_id=1, source_target_pairs={{0,4},{4,8},{8,12},{12,0},{1,5},{5,9},{9,13},{13,1},{2,6},{6,10},{... | collective-permute-start | bytes 110600 | tf_op jit(solution)/shard_map/ppermute | solution.py:393
  178.5 4.7 %collective-permute-start.36 = (f32[16,576]{1,0:T(8,128)S(1)}, f32[16,576]{1,0:T(8,128)S(1)}, u32[]{:S(2)}, u32[]{:S(2)}) collective-permute-start(f32[16,576]{1,0:T(8,128)S(1)} %add.302), channel_id=1, source_target_pairs={{0,8},{4,12},{8,0},{12,4},{1,9},{5,13},{9,1},{13,5},{2,10},{6,14},... | collective-permute-start | bytes 110600 | tf_op jit(solution)/shard_map/ppermute | solution.py:393
  181.2 3.0 collective-permute-start.37
  184.2 5.3 %collective-permute-start.38 = (f32[16,576]{1,0:T(8,128)S(1)}, f32[16,576]{1,0:T(8,128)S(1)}, u32[]{:S(2)}, u32[]{:S(2)}) collective-permute-start(f32[16,576]{1,0:T(8,128)S(1)} %add_add_fusion), channel_id=1, source_target_pairs={{0,1},{1,2},{2,3},{3,0},{4,5},{5,6},{6,7},{7,4},{8,9},{9,10},{10,1... | collective-permute-start | bytes 110600 | tf_op jit(solution)/shard_map/ppermute | solution.py:393
  184.7 4.8 %collective-permute-start.39 = (f32[16,576]{1,0:T(8,128)S(1)}, f32[16,576]{1,0:T(8,128)S(1)}, u32[]{:S(2)}, u32[]{:S(2)}) collective-permute-start(f32[16,576]{1,0:T(8,128)S(1)} %add_add_fusion), channel_id=1, source_target_pairs={{0,2},{1,3},{2,0},{3,1},{4,6},{5,7},{6,4},{7,5},{8,10},{9,11},{10,... | collective-permute-start | bytes 110600 | tf_op jit(solution)/shard_map/ppermute | solution.py:393
  187.6 3.1 collective-permute-start.40
  190.7 7.3 %collective-permute-start.41 = (f32[1,576]{1,0:T(1,128)S(1)}, f32[1,576]{1,0:T(1,128)S(1)}, u32[]{:S(2)}, u32[]{:S(2)}) collective-permute-start(f32[1,576]{1,0:T(1,128)S(1)} %get-tuple-element.94), channel_id=1, source_target_pairs={{0,96},{32,0},{64,32},{96,64},{1,97},{33,1},{65,33},{97,65},{2,98}... | collective-permute-start | bytes 6920 | tf_op jit(solution)/shard_map/ppermute | solution.py:393
  194.2 66.3 %collective-permute-start.44 = (bf16[4,4,112,768]{3,2,1,0:T(8,128)(2,1)}, bf16[4,4,112,768]{3,2,1,0:T(8,128)(2,1)S(1)}, u32[]{:S(2)}, u32[]{:S(2)}) collective-permute-start(bf16[4,4,112,768]{3,2,1,0:T(8,128)(2,1)} %get-tuple-element.84), channel_id=1, source_target_pairs={{0,16},{16,0},{1,17},{17,1},{2,18},{18,2},{3,19},{19,3},{4,20},{20... | collective-permute-start | bytes 8257544 | tf_op jit(solution)/shard_map/ppermute | solution.py:397
  197.5 67.4 %collective-permute-start.51 = (bf16[4,4,112,768]{3,2,1,0:T(8,128)(2,1)}, bf16[4,4,112,768]{3,2,1,0:T(8,128)(2,1)S(1)}, u32[]{:S(2)}, u32[]{:S(2)}) collective-permute-start(bf16[4,4,112,768]{3,2,1,0:T(8,128)(2,1)} %get-tuple-element.86), channel_id=1, source_target_pairs={{0,16},{16,0},{1,17},{17,1},{2,18},{18,2},{3,19},{19,3},{4,20},{20... | collective-permute-start | bytes 8257544 | tf_op jit(solution)/shard_map/ppermute | solution.py:397
  197.5 9.8 %collective-permute-start.23 = (bf16[4,4,32,576]{3,2,1,0:T(8,128)(2,1)}, bf16[4,4,32,576]{3,2,1,0:T(8,128)(2,1)S(1)}, u32[]{:S(2)}, u32[]{:S(2)}) collective-permute-start(bf16[4,4,32,576]{3,2,1,0:T(8,128)(2,1)} %get-tuple-element.78), channel_id=1, source_target_pairs={{0,16},{16,0},{1,17},{17,1},{2,18},{18,2},{3,19},{19,3},{4,20},{20... | collective-permute-start | bytes 1769480 | tf_op jit(solution)/shard_map/ppermute | solution.py:397
  198.0 3.9 %collective-permute-start.42 = (f32[1,576]{1,0:T(1,128)S(1)}, f32[1,576]{1,0:T(1,128)S(1)}, u32[]{:S(2)}, u32[]{:S(2)}) collective-permute-start(f32[1,576]{1,0:T(1,128)S(1)} %get-tuple-element.94), channel_id=1, source_target_pairs={{0,64},{32,96},{64,0},{96,32},{1,65},{33,97},{65,1},{97,33},{2,66}... | collective-permute-start | bytes 6920 | tf_op jit(solution)/shard_map/ppermute | solution.py:393
  198.0 4.0 %collective-permute-start.43 = (f32[1,576]{1,0:T(1,128)S(1)}, f32[1,576]{1,0:T(1,128)S(1)}, u32[]{:S(2)}, u32[]{:S(2)}) collective-permute-start(f32[1,576]{1,0:T(1,128)S(1)} %get-tuple-element.94), channel_id=1, source_target_pairs={{0,32},{32,64},{64,96},{96,0},{1,33},{33,65},{65,97},{97,1},{2,34}... | collective-permute-start | bytes 6920 | tf_op jit(solution)/shard_map/ppermute | solution.py:393
  208.5 7.3 %collective-permute-start.24 = (bf16[4,32,576]{2,1,0:T(8,128)(2,1)S(1)}, bf16[4,32,576]{2,1,0:T(8,128)(2,1)S(1)}, u32[]{:S(2)}, u32[]{:S(2)}) collective-permute-start(bf16[4,32,576]{2,1,0:T(8,128)(2,1)S(1)} %get-tuple-element.103), channel_id=1, source_target_pairs={{0,4},{4,8},{8,12},{12,0},{1,5},{5,9},{9,13},{13,1},{2,6},{6,10},{... | collective-permute-start | bytes 442376 | tf_op jit(solution)/shard_map/ppermute | solution.py:393
  209.4 11.0 %collective-permute-start.25 = (bf16[4,32,576]{2,1,0:T(8,128)(2,1)S(1)}, bf16[4,32,576]{2,1,0:T(8,128)(2,1)S(1)}, u32[]{:S(2)}, u32[]{:S(2)}) collective-permute-start(bf16[4,32,576]{2,1,0:T(8,128)(2,1)S(1)} %get-tuple-element.105), channel_id=1, source_target_pairs={{0,8},{4,12},{8,0},{12,4},{1,9},{5,13},{9,1},{13,5},{2,10},{6,14},... | collective-permute-start | bytes 442376 | tf_op jit(solution)/shard_map/ppermute | solution.py:393
  212.9 7.5 %collective-permute-start.26 = (bf16[4,32,576]{2,1,0:T(8,128)(2,1)S(1)}, bf16[4,32,576]{2,1,0:T(8,128)(2,1)S(1)}, u32[]{:S(2)}, u32[]{:S(2)}) collective-permute-start(bf16[4,32,576]{2,1,0:T(8,128)(2,1)S(1)} %get-tuple-element.104), channel_id=1, source_target_pairs={{0,12},{4,0},{8,4},{12,8},{1,13},{5,1},{9,5},{13,9},{2,14},{6,2},{... | collective-permute-start | bytes 442376 | tf_op jit(solution)/shard_map/ppermute | solution.py:393
  215.8 14.1 %collective-permute-start.20 = (bf16[256,768]{1,0:T(8,128)(2,1)S(1)}, bf16[256,768]{1,0:T(8,128)(2,1)S(1)}, u32[]{:S(2)}, u32[]{:S(2)}) collective-permute-start(bf16[256,768]{1,0:T(8,128)(2,1)S(1)} %copy-done.14), channel_id=1, source_target_pairs={{0,96},{32,0},{64,32},{96,64},{1,97},{33,1},{65,33},{97,65},{2,98}... | collective-permute-start | bytes 1179656 | tf_op jit(solution)/shard_map/ppermute | solution.py:393
  221.5 4.7 %collective-permute-start.27 = (bf16[32,576]{1,0:T(8,128)(2,1)S(1)}, bf16[32,576]{1,0:T(8,128)(2,1)S(1)}, u32[]{:S(2)}, u32[]{:S(2)}) collective-permute-start(bf16[32,576]{1,0:T(8,128)(2,1)S(1)} %get-tuple-element.123), channel_id=1, source_target_pairs={{0,1},{1,2},{2,3},{3,0},{4,5},{5,6},{6,7},{7,4},{8,9},{9,10},{10,1... | collective-permute-start | bytes 110600 | tf_op jit(solution)/shard_map/ppermute | solution.py:393
  222.4 5.5 %collective-permute-start.28 = (bf16[32,576]{1,0:T(8,128)(2,1)S(1)}, bf16[32,576]{1,0:T(8,128)(2,1)S(1)}, u32[]{:S(2)}, u32[]{:S(2)}) collective-permute-start(bf16[32,576]{1,0:T(8,128)(2,1)S(1)} %get-tuple-element.125), channel_id=1, source_target_pairs={{0,2},{1,3},{2,0},{3,1},{4,6},{5,7},{6,4},{7,5},{8,10},{9,11},{10,... | collective-permute-start | bytes 110600 | tf_op jit(solution)/shard_map/ppermute | solution.py:393
  226.2 3.1 collective-permute-start.29
  228.0 9.9 %collective-permute-start.21 = (bf16[256,768]{1,0:T(8,128)(2,1)S(1)}, bf16[256,768]{1,0:T(8,128)(2,1)S(1)}, u32[]{:S(2)}, u32[]{:S(2)}) collective-permute-start(bf16[256,768]{1,0:T(8,128)(2,1)S(1)} %copy-done.13), channel_id=1, source_target_pairs={{0,64},{32,96},{64,0},{96,32},{1,65},{33,97},{65,1},{97,33},{2,66}... | collective-permute-start | bytes 1179656 | tf_op jit(solution)/shard_map/ppermute | solution.py:393
  229.3 19.7 %collective-permute-start.22 = (bf16[256,768]{1,0:T(8,128)(2,1)S(1)}, bf16[256,768]{1,0:T(8,128)(2,1)S(1)}, u32[]{:S(2)}, u32[]{:S(2)}) collective-permute-start(bf16[256,768]{1,0:T(8,128)(2,1)S(1)} %copy-done.12), channel_id=1, source_target_pairs={{0,32},{32,64},{64,96},{96,0},{1,33},{33,65},{65,97},{97,1},{2,34}... | collective-permute-start | bytes 1179656 | tf_op jit(solution)/shard_map/ppermute | solution.py:393
  230.0 23.2 %collective-permute-start.30 = (bf16[32,576]{1,0:T(8,128)(2,1)}, bf16[32,576]{1,0:T(8,128)(2,1)S(1)}, u32[]{:S(2)}, u32[]{:S(2)}) collective-permute-start(bf16[32,576]{1,0:T(8,128)(2,1)} %get-tuple-element.96), channel_id=1, source_target_pairs={{0,96},{32,0},{64,32},{96,64},{1,97},{33,1},{65,33},{97,65},{2,98}... | collective-permute-start | bytes 110600 | tf_op jit(solution)/shard_map/ppermute | solution.py:393
  253.2 4.7 %collective-permute-start.31 = (bf16[32,576]{1,0:T(8,128)(2,1)}, bf16[32,576]{1,0:T(8,128)(2,1)S(1)}, u32[]{:S(2)}, u32[]{:S(2)}) collective-permute-start(bf16[32,576]{1,0:T(8,128)(2,1)} %get-tuple-element.96), channel_id=1, source_target_pairs={{0,64},{32,96},{64,0},{96,32},{1,65},{33,97},{65,1},{97,33},{2,66}... | collective-permute-start | bytes 110600 | tf_op jit(solution)/shard_map/ppermute | solution.py:393
  253.2 5.3 %collective-permute-start.32 = (bf16[32,576]{1,0:T(8,128)(2,1)}, bf16[32,576]{1,0:T(8,128)(2,1)S(1)}, u32[]{:S(2)}, u32[]{:S(2)}) collective-permute-start(bf16[32,576]{1,0:T(8,128)(2,1)} %get-tuple-element.96), channel_id=1, source_target_pairs={{0,32},{32,64},{64,96},{96,0},{1,33},{33,65},{65,97},{97,1},{2,34}... | collective-permute-start | bytes 110600 | tf_op jit(solution)/shard_map/ppermute | solution.py:393
  261.0 16.6 %collective-permute-start.45 = (bf16[4,112,768]{2,1,0:T(8,128)(2,1)S(1)}, bf16[4,112,768]{2,1,0:T(8,128)(2,1)S(1)}, u32[]{:S(2)}, u32[]{:S(2)}) collective-permute-start(bf16[4,112,768]{2,1,0:T(8,128)(2,1)S(1)} %get-tuple-element.97), channel_id=1, source_target_pairs={{0,4},{4,8},{8,12},{12,0},{1,5},{5,9},{9,13},{13,1},{2,6},{6,10},{... | collective-permute-start | bytes 2064392 | tf_op jit(solution)/shard_map/ppermute | solution.py:393
  261.9 31.5 %collective-permute-start.46 = (bf16[4,112,768]{2,1,0:T(8,128)(2,1)S(1)}, bf16[4,112,768]{2,1,0:T(8,128)(2,1)S(1)}, u32[]{:S(2)}, u32[]{:S(2)}) collective-permute-start(bf16[4,112,768]{2,1,0:T(8,128)(2,1)S(1)} %get-tuple-element.99), channel_id=1, source_target_pairs={{0,8},{4,12},{8,0},{12,4},{1,9},{5,13},{9,1},{13,5},{2,10},{6,14},... | collective-permute-start | bytes 2064392 | tf_op jit(solution)/shard_map/ppermute | solution.py:393
  264.9 29.3 %collective-permute-start.47 = (bf16[4,112,768]{2,1,0:T(8,128)(2,1)S(1)}, bf16[4,112,768]{2,1,0:T(8,128)(2,1)S(1)}, u32[]{:S(2)}, u32[]{:S(2)}) collective-permute-start(bf16[4,112,768]{2,1,0:T(8,128)(2,1)S(1)} %get-tuple-element.98), channel_id=1, source_target_pairs={{0,12},{4,0},{8,4},{12,8},{1,13},{5,1},{9,5},{13,9},{2,14},{6,2},{... | collective-permute-start | bytes 2064392 | tf_op jit(solution)/shard_map/ppermute | solution.py:393
  265.5 31.7 %collective-permute-start.52 = (bf16[4,112,768]{2,1,0:T(8,128)(2,1)S(1)}, bf16[4,112,768]{2,1,0:T(8,128)(2,1)S(1)}, u32[]{:S(2)}, u32[]{:S(2)}) collective-permute-start(bf16[4,112,768]{2,1,0:T(8,128)(2,1)S(1)} %get-tuple-element.100), channel_id=1, source_target_pairs={{0,1},{1,2},{2,3},{3,0},{4,5},{5,6},{6,7},{7,4},{8,9},{9,10},{10,1... | collective-permute-start | bytes 2064392 | tf_op jit(solution)/shard_map/ppermute | solution.py:393
  265.6 33.4 %collective-permute-start.53 = (bf16[4,112,768]{2,1,0:T(8,128)(2,1)S(1)}, bf16[4,112,768]{2,1,0:T(8,128)(2,1)S(1)}, u32[]{:S(2)}, u32[]{:S(2)}) collective-permute-start(bf16[4,112,768]{2,1,0:T(8,128)(2,1)S(1)} %get-tuple-element.102), channel_id=1, source_target_pairs={{0,2},{1,3},{2,0},{3,1},{4,6},{5,7},{6,4},{7,5},{8,10},{9,11},{10,... | collective-permute-start | bytes 2064392 | tf_op jit(solution)/shard_map/ppermute | solution.py:393
  277.6 21.4 %collective-permute-start.54 = (bf16[4,112,768]{2,1,0:T(8,128)(2,1)S(1)}, bf16[4,112,768]{2,1,0:T(8,128)(2,1)S(1)}, u32[]{:S(2)}, u32[]{:S(2)}) collective-permute-start(bf16[4,112,768]{2,1,0:T(8,128)(2,1)S(1)} %get-tuple-element.101), channel_id=1, source_target_pairs={{0,3},{1,0},{2,1},{3,2},{4,7},{5,4},{6,5},{7,6},{8,11},{9,8},{10,9... | collective-permute-start | bytes 2064392 | tf_op jit(solution)/shard_map/ppermute | solution.py:393
  294.8 9.4 %collective-permute-start.48 = (bf16[112,768]{1,0:T(8,128)(2,1)S(1)}, bf16[112,768]{1,0:T(8,128)(2,1)S(1)}, u32[]{:S(2)}, u32[]{:S(2)}) collective-permute-start(bf16[112,768]{1,0:T(8,128)(2,1)S(1)} %get-tuple-element.114), channel_id=1, source_target_pairs={{0,1},{1,2},{2,3},{3,0},{4,5},{5,6},{6,7},{7,4},{8,9},{9,10},{10,1... | collective-permute-start | bytes 516104 | tf_op jit(solution)/shard_map/ppermute | solution.py:393
  294.9 10.3 %collective-permute-start.49 = (bf16[112,768]{1,0:T(8,128)(2,1)S(1)}, bf16[112,768]{1,0:T(8,128)(2,1)S(1)}, u32[]{:S(2)}, u32[]{:S(2)}) collective-permute-start(bf16[112,768]{1,0:T(8,128)(2,1)S(1)} %get-tuple-element.116), channel_id=1, source_target_pairs={{0,2},{1,3},{2,0},{3,1},{4,6},{5,7},{6,4},{7,5},{8,10},{9,11},{10,... | collective-permute-start | bytes 516104 | tf_op jit(solution)/shard_map/ppermute | solution.py:393
  297.2 8.0 %collective-permute-start.50 = (bf16[112,768]{1,0:T(8,128)(2,1)S(1)}, bf16[112,768]{1,0:T(8,128)(2,1)S(1)}, u32[]{:S(2)}, u32[]{:S(2)}) collective-permute-start(bf16[112,768]{1,0:T(8,128)(2,1)S(1)} %get-tuple-element.115), channel_id=1, source_target_pairs={{0,3},{1,0},{2,1},{3,2},{4,7},{5,4},{6,5},{7,6},{8,11},{9,8},{10,9... | collective-permute-start | bytes 516104 | tf_op jit(solution)/shard_map/ppermute | solution.py:393
  299.5 6.6 %collective-permute-start.55 = (bf16[112,768]{1,0:T(8,128)(2,1)S(1)}, bf16[112,768]{1,0:T(8,128)(2,1)S(1)}, u32[]{:S(2)}, u32[]{:S(2)}) collective-permute-start(bf16[112,768]{1,0:T(8,128)(2,1)S(1)} %get-tuple-element.117), channel_id=1, source_target_pairs={{0,4},{4,8},{8,12},{12,0},{1,5},{5,9},{9,13},{13,1},{2,6},{6,10},{... | collective-permute-start | bytes 516104 | tf_op jit(solution)/shard_map/ppermute | solution.py:393
  301.2 9.4 %collective-permute-start.56 = (bf16[112,768]{1,0:T(8,128)(2,1)S(1)}, bf16[112,768]{1,0:T(8,128)(2,1)S(1)}, u32[]{:S(2)}, u32[]{:S(2)}) collective-permute-start(bf16[112,768]{1,0:T(8,128)(2,1)S(1)} %get-tuple-element.119), channel_id=1, source_target_pairs={{0,8},{4,12},{8,0},{12,4},{1,9},{5,13},{9,1},{13,5},{2,10},{6,14},... | collective-permute-start | bytes 516104 | tf_op jit(solution)/shard_map/ppermute | solution.py:393
  304.2 6.5 %collective-permute-start.57 = (bf16[112,768]{1,0:T(8,128)(2,1)S(1)}, bf16[112,768]{1,0:T(8,128)(2,1)S(1)}, u32[]{:S(2)}, u32[]{:S(2)}) collective-permute-start(bf16[112,768]{1,0:T(8,128)(2,1)S(1)} %get-tuple-element.118), channel_id=1, source_target_pairs={{0,12},{4,0},{8,4},{12,8},{1,13},{5,1},{9,5},{13,9},{2,14},{6,2},{... | collective-permute-start | bytes 516104 | tf_op jit(solution)/shard_map/ppermute | solution.py:393
  310.9 6.7 %collective-permute-start.58 = (bf16[56,768]{1,0:T(8,128)(2,1)S(1)}, bf16[56,768]{1,0:T(8,128)(2,1)S(1)}, u32[]{:S(2)}, u32[]{:S(2)}) collective-permute-start(bf16[56,768]{1,0:T(8,128)(2,1)S(1)} %get-tuple-element.120), channel_id=1, source_target_pairs={{0,32},{32,64},{64,96},{96,0},{1,33},{33,65},{65,97},{97,1},{2,34}... | collective-permute-start | bytes 258056 | tf_op jit(solution)/shard_map/ppermute | solution.py:393
  311.0 6.6 %collective-permute-start.59 = (bf16[56,768]{1,0:T(8,128)(2,1)S(1)}, bf16[56,768]{1,0:T(8,128)(2,1)S(1)}, u32[]{:S(2)}, u32[]{:S(2)}) collective-permute-start(bf16[56,768]{1,0:T(8,128)(2,1)S(1)} %get-tuple-element.121), channel_id=1, source_target_pairs={{0,64},{32,96},{64,0},{96,32},{1,65},{33,97},{65,1},{97,33},{2,66}... | collective-permute-start | bytes 258056 | tf_op jit(solution)/shard_map/ppermute | solution.py:393
  312.6 5.0 %collective-permute-start.60 = (bf16[56,768]{1,0:T(8,128)(2,1)S(1)}, bf16[56,768]{1,0:T(8,128)(2,1)S(1)}, u32[]{:S(2)}, u32[]{:S(2)}) collective-permute-start(bf16[56,768]{1,0:T(8,128)(2,1)S(1)} %get-tuple-element.122), channel_id=1, source_target_pairs={{0,96},{32,0},{64,32},{96,64},{1,97},{33,1},{65,33},{97,65},{2,98}... | collective-permute-start | bytes 258056 | tf_op jit(solution)/shard_map/ppermute | solution.py:393
  314.1 5.6 %collective-permute-start.33 = (bf16[4,32,576]{2,1,0:T(8,128)(2,1)S(1)}, bf16[4,32,576]{2,1,0:T(8,128)(2,1)S(1)}, u32[]{:S(2)}, u32[]{:S(2)}) collective-permute-start(bf16[4,32,576]{2,1,0:T(8,128)(2,1)S(1)} %constant_dynamic-slice_fusion.12), channel_id=1, source_target_pairs={{0,16},{16,0},{1,17},{17,1},{2,18},{18,2},{3,19},{19,3},{4,20},{20... | collective-permute-start | bytes 442376 | tf_op jit(solution)/shard_map/ppermute | solution.py:397
  317.7 3.7 %collective-permute-start.61 = (bf16[56,768]{1,0:T(8,128)(2,1)S(1)}, bf16[56,768]{1,0:T(8,128)(2,1)S(1)}, u32[]{:S(2)}, u32[]{:S(2)}) collective-permute-start(bf16[56,768]{1,0:T(8,128)(2,1)S(1)} %get-tuple-element.92), channel_id=1, source_target_pairs={{0,96},{32,0},{64,32},{96,64},{1,97},{33,1},{65,33},{97,65},{2,98}... | collective-permute-start | bytes 258056 | tf_op jit(solution)/shard_map/ppermute | solution.py:393
  319.7 4.9 %collective-permute-start.62 = (bf16[56,768]{1,0:T(8,128)(2,1)S(1)}, bf16[56,768]{1,0:T(8,128)(2,1)S(1)}, u32[]{:S(2)}, u32[]{:S(2)}) collective-permute-start(bf16[56,768]{1,0:T(8,128)(2,1)S(1)} %get-tuple-element.92), channel_id=1, source_target_pairs={{0,64},{32,96},{64,0},{96,32},{1,65},{33,97},{65,1},{97,33},{2,66}... | collective-permute-start | bytes 258056 | tf_op jit(solution)/shard_map/ppermute | solution.py:393
  320.8 4.8 %collective-permute-start.63 = (bf16[56,768]{1,0:T(8,128)(2,1)S(1)}, bf16[56,768]{1,0:T(8,128)(2,1)S(1)}, u32[]{:S(2)}, u32[]{:S(2)}) collective-permute-start(bf16[56,768]{1,0:T(8,128)(2,1)S(1)} %get-tuple-element.92), channel_id=1, source_target_pairs={{0,32},{32,64},{64,96},{96,0},{1,33},{33,65},{65,97},{97,1},{2,34}... | collective-permute-start | bytes 258056 | tf_op jit(solution)/shard_map/ppermute | solution.py:393
  325.7 7.5 %collective-permute-start.64 = (bf16[224,768]{1,0:T(8,128)(2,1)S(1)}, bf16[224,768]{1,0:T(8,128)(2,1)S(1)}, u32[]{:S(2)}, u32[]{:S(2)}) collective-permute-start(bf16[224,768]{1,0:T(8,128)(2,1)S(1)} %bitcast.184), channel_id=1, source_target_pairs={{0,16},{16,0},{1,17},{17,1},{2,18},{18,2},{3,19},{19,3},{4,20},{20... | collective-permute-start | bytes 1032200 | tf_op jit(solution)/shard_map/ppermute | solution.py:397
  (39 other events, 349.8 us)
Sparse Core Ops, SparseCore 0:
  11.2 87.5 all-gather.1

commit v2 on v1

--- a/solution.py
+++ b/solution.py
@@ -141,139 +141,105 @@
     return act, slope
 
 
+def head_rows(x, k):
+    return pl.ds(pl.multiple_of(lax.rem(x + k, 4) * CH, 64), CH)
+
+
+def middle_kernel(meta, a0, a1, a2, a3, tok, wout, vec, middle_ref, xhat_ref, root_ref, n2_ref):
+    middle = tok[...].astype(F32)
+    for k, a in enumerate((a0, a1, a2, a3)):
+        middle = middle + dot(a[...], wout[head_rows(meta[0], k), :])
+    middle = middle + vec[4:5, :]
+    xhat, root = standardize(middle)
+    middle_ref[...] = middle
+    xhat_ref[...] = xhat
+    root_ref[...] = root
+    n2_ref[...] = (xhat * vec[5:6, :] + vec[6:7, :]).astype(BF16)
+
+
 def mlp_kernel(
+    n2_own, n2_oth, cot_own, cot_oth, fcb, wblk, ffn_own, ffn_oth, dn_own, dn_oth, dw_ref, fcg_ref, ffn_s, dn_s
+):
+    j = pl.program_id(0)
+    fc = wblk[:, 0:96, :].reshape(D, D)
+    proj = wblk[:, 96:192, :].reshape(D, D)
+    n2 = jnp.concatenate([n2_own[...], n2_oth[...]], axis=0)
+    ct = jnp.concatenate([cot_own[...], cot_oth[...]], axis=0)
+    act, slope = gelu_parts(dot_nt(n2, fc) + fcb[j])
+    act = act.astype(BF16)
+    gh = (dot_nt(ct, proj) * slope).astype(BF16)
+    ffn = dot(act, proj)
+    dn = dot(gh, fc)
+    fcg_ref[j] = jnp.sum(gh.astype(F32), axis=0, keepdims=True)
+    dw_ref[:, 0:96, :] = dot_tn(gh, n2).astype(BF16).reshape(8, 96, D)
+    dw_ref[:, 96:192, :] = dot_tn(act, ct).astype(BF16).reshape(8, 96, D)
+
+    @pl.when(j == 0)
+    def _():
+        ffn_s[...] = ffn
+        dn_s[...] = dn
+
+    @pl.when(j == 1)
+    def _():
+        ffn_own[...] = ffn_s[:ROWS] + ffn[:ROWS]
+        ffn_oth[...] = (ffn_s[ROWS:] + ffn[ROWS:]).astype(BF16)
+        dn_own[...] = dn_s[:ROWS] + dn[:ROWS]
+        dn_oth[...] = (dn_s[ROWS:] + dn[ROWS:]).astype(BF16)
+
+
+def middle_grad_kernel(
     meta,
+    dw_in,
     a0,
     a1,
     a2,
     a3,
-    tok,
     cot,
     wout,
     vec,
-    fcb,
-    wblk,
-    out_ref,
+    xhat_ref,
+    root_ref,
+    dn_own,
+    dn_recv,
     gm_ref,
     d0,
     d1,
     d2,
     d3,
-    own_a,
-    own_b,
-    oth_a,
-    oth_b,
     vg_ref,
-    fcg_ref,
-    middle_s,
-    xhat_s,
-    root_s,
-    n2_s,
-    ffn_s,
-    dn_s,
+    dw_out,
     dout_s,
+    sem,
 ):
-    j = pl.program_id(0)
-    x, c, z, y = meta[0], meta[1], meta[2], meta[3]
-    atts = (a0, a1, a2, a3)
-
-    def head_rows(k):
-        return pl.ds(pl.multiple_of(lax.rem(x + k, 4) * CH, 64), CH)
-
-    @pl.when(j == 0)
-    def _():
-        branch = vec[4:5, :]
-        middle = tok[...].astype(F32)
-        for k in range(4):
-            middle = middle + dot(atts[k][...], wout[head_rows(k), :])
-        middle = middle + branch
-        xhat, root = standardize(middle)
-        middle_s[...] = middle
-        xhat_s[...] = xhat
-        root_s[...] = root
-        n2_s[...] = (xhat * vec[5:6, :] + vec[6:7, :]).astype(BF16)
-        ffn_s[...] = jnp.zeros_like(ffn_s)
-        dn_s[...] = jnp.zeros_like(dn_s)
-
-    fc = wblk[:, 64:256, :].reshape(D, D)
-    proj = wblk[:, 256:448, :].reshape(D, D)
-    cols = pl.ds(pl.multiple_of(j * D, D), D)
-    n2 = n2_s[...]
-    ct = cot[...]
-    hidden = dot_nt(n2, fc) + fcb[:, cols]
-    act, slope = gelu_parts(hidden)
-    act = act.astype(BF16)
-    ffn_s[...] += dot(act, proj)
-    gh = dot_nt(ct, proj) * slope
-    gh = gh.astype(BF16)
-    dn_s[...] += dot(gh, fc)
-    fcg_ref[:, cols] = jnp.sum(gh.astype(F32), axis=0, keepdims=True)
-    dproj = dot_tn(act, ct).astype(BF16)
-    dfc = dot_tn(gh, n2).astype(BF16)
-    kz = rel(j, z)
-    for yy in range(4):
-        ky = rel(yy, y)
-        first = slice(yy * 192, yy * 192 + 96)
-        second = slice(yy * 192 + 96, (yy + 1) * 192)
-
-        @pl.when(c == 0)
-        def _():
-            own_a[kz, ky, 0:96, :] = dfc[first]
-            own_b[ky, kz, 0:96, :] = dfc[second]
-            oth_a[kz, ky, 0:96, :] = dproj[first]
-            oth_b[ky, kz, 0:96, :] = dproj[second]
-
-        @pl.when(c == 1)
-        def _():
-            oth_a[kz, ky, 0:96, :] = dfc[first]
-            oth_b[ky, kz, 0:96, :] = dfc[second]
-            own_a[kz, ky, 0:96, :] = dproj[first]
-            own_b[ky, kz, 0:96, :] = dproj[second]
-
-    @pl.when(j == 3)
-    def _():
-        ctf = ct.astype(F32)
-        out_ref[...] = (middle_s[...] + ffn_s[...] + vec[7:8, :]).astype(BF16)
-        dn = dn_s[...]
-        xhat = xhat_s[...]
-        e = dn * vec[5:6, :]
-        part = e - jnp.mean(e, axis=-1, keepdims=True)
-        part = part - xhat * jnp.mean(e * xhat, axis=-1, keepdims=True)
-        gm = ctf + part * root_s[...]
-        gm_ref[...] = gm
-        gb = gm.astype(BF16)
-        zero = jnp.zeros((4, D), F32)
-        vg_ref[...] = jnp.concatenate(
-            [
-                jnp.sum(gb.astype(F32), axis=0, keepdims=True),
-                jnp.sum(dn * xhat, axis=0, keepdims=True),
-                jnp.sum(dn, axis=0, keepdims=True),
-                jnp.sum(ctf, axis=0, keepdims=True),
-                zero,
-            ],
-            axis=0,
-        )
-        for k, d in enumerate((d0, d1, d2, d3)):
-            d[...] = dot_nt(gb, wout[head_rows(k), :]).astype(BF16)
-            dout_s[head_rows(k), :] = dot_tn(atts[k][...], gb).astype(BF16)
-        blank = jnp.zeros((16, D), BF16)
-        for s in range(16):
-            sz, sy = rel(s // 4, z), rel(s % 4, y)
-            u = [dout_s[s * 48 + 16 * t : s * 48 + 16 * (t + 1), :] for t in range(3)]
-
-            @pl.when(c == 0)
-            def _():
-                own_a[sz, sy, 96:112, :] = u[0]
-                own_b[sy, sz, 96:112, :] = u[1]
-                oth_a[sz, sy, 96:112, :] = u[2]
-                oth_b[sy, sz, 96:112, :] = blank
-
-            @pl.when(c == 1)
-            def _():
-                oth_a[sz, sy, 96:112, :] = u[0]
-                oth_b[sy, sz, 96:112, :] = u[1]
-                own_a[sz, sy, 96:112, :] = u[2]
-                own_b[sy, sz, 96:112, :] = blank
+    x = meta[0]
+    ctf = cot[...].astype(F32)
+    dn = dn_own[...] + dn_recv[...].astype(F32)
+    xhat = xhat_ref[...]
+    e = dn * vec[5:6, :]
+    part = e - jnp.mean(e, axis=-1, keepdims=True)
+    part = part - xhat * jnp.mean(e * xhat, axis=-1, keepdims=True)
+    gm = ctf + part * root_ref[...]
+    gm_ref[...] = gm
+    gb = gm.astype(BF16)
+    for k, (a, d) in enumerate(zip((a0, a1, a2, a3), (d0, d1, d2, d3))):
+        d[...] = dot_nt(gb, wout[head_rows(x, k), :]).astype(BF16)
+        g = dot_tn(a[...], gb).astype(BF16)
+        first = lax.rem(x + k, 4) * 4
+        for t in range(4):
+            dout_s[first + t] = g[t * 48 : (t + 1) * 48, :]
+    copy = pltpu.make_async_copy(dout_s, dw_out.at[:, 192:240, :], sem)
+    copy.start()
+    vg_ref[...] = jnp.concatenate(
+        [
+            jnp.sum(gb.astype(F32), axis=0, keepdims=True),
+            jnp.sum(dn * xhat, axis=0, keepdims=True),
+            jnp.sum(dn, axis=0, keepdims=True),
+            jnp.sum(ctf, axis=0, keepdims=True),
+            jnp.zeros((4, D), F32),
+        ],
+        axis=0,
+    )
+    copy.wait()
 
 
 def backward_kernel(meta, *refs):
@@ -345,29 +311,11 @@
 
 
 def weight_grad_kernel(
-    meta, normed_ref, g_ref, t0, t1, t2, t3, n0, n1, n2, n3, own_ref, oth_ref, vg_ref, qv_ref, dw_s
+    meta, normed_ref, g_ref, t0, t1, t2, t3, n0, n1, n2, n3, vg2, fcg, own_ref, oth_ref, dw_s, vec_s, row_s
 ):
-    c, z, y = meta[1], meta[2], meta[3]
+    x, c, z, y = meta[0], meta[1], meta[2], meta[3]
     g = g_ref[...]
     dw_s[...] = dot_tn(normed_ref[...], g).astype(BF16)
-    blank = jnp.zeros((16, HC * CH), BF16)
-    for s in range(16):
-        sz, sy = rel(s // 4, z), rel(s % 4, y)
-        first = dw_s[s * 48 : s * 48 + 32, :]
-        second = dw_s[s * 48 + 32 : s * 48 + 48, :]
-
-        @pl.when(c == 0)
-        def _():
-            own_ref[sz, sy] = first
-            oth_ref[sz, sy, 0:16, :] = second
-            oth_ref[sz, sy, 16:32, :] = blank
-
-        @pl.when(c == 1)
-        def _():
-            oth_ref[sz, sy] = first
-            own_ref[sz, sy, 0:16, :] = second
-            own_ref[sz, sy, 16:32, :] = blank
-
     gain = jnp.zeros((1, D), F32)
     bias = jnp.zeros((1, D), F32)
     for t, n in zip((t0, t1, t2, t3), (n0, n1, n2, n3)):
@@ -375,9 +323,51 @@
         ng = n[...].astype(F32)
         gain = gain + jnp.sum(ng * xhat, axis=0, keepdims=True)
         bias = bias + jnp.sum(ng, axis=0, keepdims=True)
-    vg_ref[0:1, :] = gain
-    vg_ref[1:2, :] = bias
-    qv_ref[...] = jnp.sum(g.astype(F32), axis=0, keepdims=True)
+    sums = jnp.sum(g.astype(F32), axis=0, keepdims=True)
+    vec_s[0:1, :] = gain
+    vec_s[1:2, :] = bias
+    vec_s[2:4, :] = jnp.zeros((2, D), F32)
+    for i in range(4):
+
+        @pl.when(x == i)
+        def _():
+            vec_s[2:3, i * CH : (i + 1) * CH] = sums[:, :CH]
+            vec_s[3:4, i * CH : (i + 1) * CH] = sums[:, 2 * CH :]
+
+    vec_s[4:8, :] = vg2[0:4, :]
+    row_s[...] = jnp.zeros_like(row_s)
+    for s in range(16):
+        for v in range(8):
+            row_s[s, 0:1, v * 48 : (v + 1) * 48] = vec_s[v : v + 1, s * 48 : (s + 1) * 48]
+
+        @pl.when(c == 0)
+        def _():
+            row_s[s, 0:1, 384:480] = fcg[s // 8, :, (s % 8) * 96 : (s % 8 + 1) * 96]
+
+        @pl.when(c == 1)
+        def _():
+            row_s[s, 0:1, 480:576] = fcg[s // 8, :, (s % 8) * 96 : (s % 8 + 1) * 96]
+
+    blank = jnp.zeros((16, HC * CH), BF16)
+    for s in range(16):
+        sz, sy = rel(s // 4, z), rel(s % 4, y)
+        first = dw_s[s * 48 : s * 48 + 32, :]
+        second = dw_s[s * 48 + 32 : s * 48 + 48, :]
+        row = row_s[s].astype(BF16)
+        own_ref[sz, sy, 32:48, :] = row
+        oth_ref[sz, sy, 32:48, :] = row
+
+        @pl.when(c == 0)
+        def _():
+            own_ref[sz, sy, 0:32, :] = first
+            oth_ref[sz, sy, 0:16, :] = second
+            oth_ref[sz, sy, 16:32, :] = blank
+
+        @pl.when(c == 1)
+        def _():
+            oth_ref[sz, sy, 0:32, :] = first
+            own_ref[sz, sy, 0:16, :] = second
+            own_ref[sz, sy, 16:32, :] = blank
 
 
 def token_grad_kernel(tok, gm, vec, n0, n1, n2, n3, out_ref):
@@ -408,13 +398,17 @@
     return total.astype(BF16)
 
 
+def sum4(pieces):
+    return (pieces[0] + pieces[2]) + (pieces[1] + pieces[3])
+
+
 def in_order(pieces, index):
     up = [pieces[0], pieces[3], pieces[2], pieces[1]]
     twice = jnp.stack(up + up)
     return lax.dynamic_slice_in_dim(twice, rel(0, index), 4, axis=0)
 
 
-def call(kernel, outs, scratch=(), smem=True, **kw):
+def call(kernel, outs, scratch=(), smem=True, us=0, **kw):
     specs = [pl.BlockSpec(memory_space=pltpu.VMEM)]
 
     def run(*args):
@@ -426,10 +420,15 @@
             out_specs=jax.tree.map(lambda _: specs[0], outs),
             scratch_shapes=list(scratch),
             compiler_params=pltpu.CompilerParams(vmem_limit_bytes=56 * 2**20),
+            cost_estimate=cost(us),
             **kw,
         )(*args)
 
     return run
+
+
+def cost(us):
+    return pl.CostEstimate(flops=us * 10**9, bytes_accessed=us * 10**6, transcendentals=0)
 
 
 def shp(*dims, dtype=BF16):
@@ -467,9 +466,6 @@
 
     tok = tokens.reshape(ROWS, D)
     cot = cotangent.reshape(ROWS, D)
-    tok_own = gather4(tok, "x")
-    tok_oth = [swap(t) for t in tok_own]
-
     wcols = lax.dynamic_index_in_dim(qkv_weight.reshape(48, 3, 4, CH), x, axis=2, keepdims=False)
     wcols = wcols.reshape(48, 3 * CH)
     row = jnp.concatenate(
@@ -478,6 +474,10 @@
     mine = lax.broadcasted_iota(jnp.int32, (16, 1), 0) == z * 4 + y
     wbuf = jnp.concatenate([wcols, jnp.where(mine, row[None, :], jnp.zeros((), BF16))], axis=0)
     by_z = jnp.concatenate(gather4(wbuf, "z"), axis=0)
+    by_z, tok_1, tok_3 = lax.optimization_barrier((by_z, shift(tok, "x", 1), shift(tok, "x", 3)))
+    tok_far, _ = lax.optimization_barrier((tok, by_z))
+    tok_own = [tok, tok_1, shift(tok_far, "x", 2), tok_3]
+    tok_oth = [swap(t) for t in tok_own]
     wrel = gather4(by_z, "y")
     rows16 = sum(
         w.reshape(4, 64, 3 * CH)[k, 48:, :].astype(F32) for w in wrel for k in range(4)
@@ -487,12 +487,15 @@
     qvb = lax.dynamic_index_in_dim(vec[2:4].reshape(2, 4, CH), x, axis=1, keepdims=False)
     qvb = jnp.concatenate([qvb, jnp.zeros((6, CH), F32)], axis=0)
 
-    shard = jnp.concatenate(
-        [out_weight, jnp.zeros((16, D), BF16), fc_weight, proj_weight], axis=0
-    )
-    part = lax.dynamic_slice_in_dim(shard, (x * 2 + c) * 56, 56, axis=0)
-    wall = lax.all_gather(part, ("z", "y", "x", "core"), axis=0, tiled=True).reshape(16, 448, D)
-    wout = wall[:, :48].reshape(D, D)
+    half = lambda w, n: lax.dynamic_slice_in_dim(w, c * n, n, axis=0)
+    part = jnp.concatenate(
+        [half(fc_weight, 96), half(proj_weight, 96), half(out_weight, 24), jnp.zeros((8, D), BF16)],
+        axis=0,
+    )
+    wall = lax.all_gather(part, ("z", "y"), axis=0, tiled=True).reshape(16, 224, D)
+    fcb = lax.dynamic_index_in_dim(fcb.reshape(16, 2, 96), c, axis=1, keepdims=False)
+    fcb = fcb.reshape(2, 1, D)
+    cot_oth = swap(cot)
 
     fwd = call(
         forward_kernel,
@@ -508,45 +511,74 @@
             shp(D, 3 * CH),
         ],
         [pltpu.VMEM((HC, HD, SEQ), BF16)],
+        us=25,
         name="attention_forward",
     )(meta, *tok_own, *tok_oth, *wrel, vec, qvb)
     att, (attt, lse, q, kk, kt, v, normed, w) = fwd[:4], fwd[4:]
+    wall, first = lax.optimization_barrier((wall, att[0]))
+    att = [first, *att[1:]]
+    out_half = wall[:, 192:216]
+    out_recv = swap(out_half)
+    wout = jnp.stack(
+        [jnp.where(c == 0, out_half, out_recv), jnp.where(c == 0, out_recv, out_half)], axis=1
+    ).reshape(D, D)
     att_rel = [att[0]] + [shift(att[k], "x", -k) for k in (1, 2, 3)]
 
+    middle, xhat, root, n2 = call(
+        middle_kernel,
+        [shp(ROWS, D, dtype=F32), shp(ROWS, D, dtype=F32), shp(ROWS, 1, dtype=F32), shp(ROWS, D)],
+        us=4,
+        name="middle",
+    )(meta, *att_rel, tok, wout, vec)
+    n2_oth = swap(n2)
+
     whole = lambda *dims: pl.BlockSpec(dims, lambda j: (0,) * len(dims))
-    mlp_outs = (
-        [shp(ROWS, D), shp(ROWS, D, dtype=F32)]
+    mlp_outs = [
+        shp(ROWS, D, dtype=F32),
+        shp(ROWS, D),
+        shp(ROWS, D, dtype=F32),
+        shp(ROWS, D),
+        shp(16, 240, D),
+        shp(2, 1, D, dtype=F32),
+    ]
+    mlp_specs = [whole(*o.shape) for o in mlp_outs]
+    mlp_specs[4] = pl.BlockSpec((8, 240, D), lambda j: (j, 0, 0))
+    ffn_own, ffn_oth, dn_own, dn_oth, dw, fcg = pl.pallas_call(
+        mlp_kernel,
+        grid=(2,),
+        out_shape=mlp_outs,
+        in_specs=[whole(ROWS, D)] * 4
+        + [whole(2, 1, D), pl.BlockSpec((8, 224, D), lambda j: (j, 0, 0))],
+        out_specs=mlp_specs,
+        scratch_shapes=[pltpu.VMEM((2 * ROWS, D), F32), pltpu.VMEM((2 * ROWS, D), F32)],
+        compiler_params=pltpu.CompilerParams(vmem_limit_bytes=56 * 2**20),
+        cost_estimate=cost(18),
+        name="feed_forward",
+    )(n2, n2_oth, cot, cot_oth, fcb, wall)
+    dn_recv = swap(dn_oth)
+    ffn_recv = swap(ffn_oth)
+    outcome = (middle + (ffn_own + ffn_recv.astype(F32)) + vec[7:8]).astype(BF16)
+
+    vmem = pl.BlockSpec(memory_space=pltpu.VMEM)
+    hbm = pl.BlockSpec(memory_space=pl.ANY)
+    gm, *datt, vg2, dw = pl.pallas_call(
+        middle_grad_kernel,
+        out_shape=[shp(ROWS, D, dtype=F32)]
         + [shp(ROWS, CH)] * 4
-        + [shp(4, 4, 112, D)] * 4
-        + [shp(8, D, dtype=F32), shp(1, FF, dtype=F32)]
-    )
-    mlp = pl.pallas_call(
-        mlp_kernel,
-        grid=(4,),
-        out_shape=mlp_outs,
-        in_specs=[pl.BlockSpec(memory_space=pltpu.SMEM)]
-        + [whole(ROWS, CH)] * 4
-        + [whole(ROWS, D), whole(ROWS, D), whole(D, D), whole(8, D), whole(1, FF)]
-        + [pl.BlockSpec((4, 448, D), lambda j: (j, 0, 0))],
-        out_specs=[whole(*o.shape) for o in mlp_outs],
-        scratch_shapes=[
-            pltpu.VMEM((ROWS, D), F32),
-            pltpu.VMEM((ROWS, D), F32),
-            pltpu.VMEM((ROWS, 1), F32),
-            pltpu.VMEM((ROWS, D), BF16),
-            pltpu.VMEM((ROWS, D), F32),
-            pltpu.VMEM((ROWS, D), F32),
-            pltpu.VMEM((D, D), BF16),
-        ],
+        + [shp(8, D, dtype=F32), shp(16, 240, D)],
+        in_specs=[pl.BlockSpec(memory_space=pltpu.SMEM), hbm] + [vmem] * 11,
+        out_specs=[vmem] * 6 + [hbm],
+        scratch_shapes=[pltpu.VMEM((16, 48, D), BF16), pltpu.SemaphoreType.DMA],
+        input_output_aliases={1: 6},
         compiler_params=pltpu.CompilerParams(vmem_limit_bytes=56 * 2**20),
-        name="feed_forward",
-    )(meta, *att_rel, tok, cot, wout, vec, fcb, wall)
-    outcome, gm = mlp[0], mlp[1]
-    datt, (own_a, own_b, oth_a, oth_b), (vg2, fcg) = mlp[2:6], mlp[6:10], mlp[10:12]
+        cost_estimate=cost(5),
+        name="middle_grad",
+    )(meta, dw, *att_rel, cot, wout, vec, xhat, root, dn_own, dn_recv)
+    shard_grad = lax.psum_scatter(
+        dw.reshape(16 * 240, D), ("z", "y"), scatter_dimension=0, tiled=True
+    )
 
     datt_rel = [datt[0]] + [shift(datt[k], "x", k) for k in (1, 2, 3)]
-    recv_a, recv_b = swap(oth_a), swap(oth_b)
-
     dq, dkv_own, dkv_oth = call(
         backward_kernel,
         [shp(1024, CH), shp(1024, 2 * CH, dtype=F32), shp(1024, 2 * CH)],
@@ -555,68 +587,42 @@
             pltpu.VMEM((HC, SEQ, HD), F32),
             pltpu.VMEM((HC, 1024, HD), BF16),
         ],
+        us=24,
         name="attention_backward",
     )(meta, *datt_rel, q, kk, kt, v, attt, lse)
     dkv_recv = swap(dkv_oth)
-
-    sum_a = [(own_a[k].astype(F32) + recv_a[k].astype(F32)).astype(BF16) for k in range(4)]
-    sum_b = [(own_b[k].astype(F32) + recv_b[k].astype(F32)).astype(BF16) for k in range(4)]
-    za = scatter4(sum_a, "z")
-    yb = scatter4(sum_b, "y")
-    fa = scatter4([za[k] for k in range(4)], "y")
-    fb = scatter4([yb[k] for k in range(4)], "z")
-    quarters = jnp.concatenate([fa, fb], axis=0).reshape(4, 56, D)
-    quarters = lax.dynamic_slice_in_dim(jnp.concatenate([quarters, quarters]), x, 4, axis=0)
-    quarter = scatter4([quarters[k] for k in range(4)], "x")
-    half = in_order(gather4(quarter, "x"), x).reshape(224, D)
-    half_oth = swap(half)
-    low = jnp.where(c == 0, half, half_oth).astype(F32)
-    high = jnp.where(c == 0, half_oth, half).astype(F32)
-    grad_fc_w = jnp.concatenate([low[0:96], low[112:208]], axis=0)
-    grad_proj_w = jnp.concatenate([high[0:96], high[112:208]], axis=0)
-    grad_out_w = jnp.concatenate([low[96:112], low[208:224], high[96:112]], axis=0)
 
     ng0, ng1, ng2, ng3, g = call(
         input_grad_kernel,
         [shp(ROWS, D)] * 4 + [shp(1024, 3 * CH)],
         smem=False,
+        us=5,
         name="input_grad",
     )(dq, dkv_own, dkv_recv, w)
     ng_rel = [ng0] + [shift(n, "x", -k) for k, n in ((1, ng1), (2, ng2), (3, ng3))]
-    wq_own, wq_oth, vg1, qvg = call(
+    wq_own, wq_oth = call(
         weight_grad_kernel,
+        [shp(4, 4, 48, 3 * CH)] * 2,
         [
-            shp(4, 4, 32, 3 * CH),
-            shp(4, 4, 32, 3 * CH),
-            shp(8, D, dtype=F32),
-            shp(1, 3 * CH, dtype=F32),
+            pltpu.VMEM((D, 3 * CH), BF16),
+            pltpu.VMEM((8, D), F32),
+            pltpu.VMEM((16, 16, 3 * CH), F32),
         ],
-        [pltpu.VMEM((D, 3 * CH), BF16)],
+        us=8,
         name="weight_grad",
-    )(meta, normed, g, *tok_own, ng0, ng1, ng2, ng3)
+    )(meta, normed, g, *tok_own, ng0, ng1, ng2, ng3, vg2, fcg)
     token_grad = call(
-        token_grad_kernel, shp(ROWS, D, dtype=F32), smem=False, name="token_grad"
+        token_grad_kernel, shp(ROWS, D, dtype=F32), smem=False, us=3, name="token_grad"
     )(tok, gm, vec, *ng_rel)
-
-    place = lambda part: lax.dynamic_update_slice(jnp.zeros((1, D), F32), part, (0, x * CH))
-    vg = jnp.concatenate(
-        [vg1[0:2], place(qvg[:, :CH]), place(qvg[:, 2 * CH :]), vg2[0:4]], axis=0
-    )
-    vrows = jnp.concatenate(
-        [vg.reshape(8, 16, 48).transpose(1, 0, 2).reshape(16, 384), fcg.reshape(16, 192)], axis=1
-    )
-    vrows = vrows + swap(vrows)
-    vrows = sum(gather4(vrows, "z"))
-    vrows = sum(gather4(vrows, "y"))
-    vrow = lax.dynamic_slice_in_dim(vrows, z * 4 + y, 1, axis=0)
-    vrow = in_order(gather4(vrow, "x"), x)
-    vrow = (vrow[0] + vrow[1] + vrow[2] + vrow[3])[0]
 
     wq_recv = swap(wq_oth)
     wq = [(wq_own[k].astype(F32) + wq_recv[k].astype(F32)).astype(BF16) for k in range(4)]
     wq = scatter4(wq, "z")
+    wq, token_grad = lax.optimization_barrier((wq, token_grad))
     wq = scatter4([wq[k] for k in range(4)], "y")
-    wq_x = in_order(gather4(wq, "x"), x)
+    wq_rel = gather4(wq, "x")
+    vrow = sum4([w[32].astype(F32) for w in wq_rel])
+    wq_x = in_order(wq_rel, x)[:, :32]
     wq_x_oth = swap(wq_x)
     grad_qkv = jnp.concatenate(
         [jnp.where(c == 0, wq_x, wq_x_oth), jnp.where(c == 0, wq_x_oth, wq_x)[:, :16]], axis=1
@@ -624,6 +630,15 @@
     grad_qkv = (
         grad_qkv.reshape(4, 48, 3, CH).transpose(1, 2, 0, 3).reshape(48, 3 * D).astype(F32)
     )
+
+    shard_grad = sum4([v.astype(F32) for v in gather4(shard_grad, "x")]).astype(BF16)
+    shard_oth = swap(shard_grad).astype(F32)
+    shard_grad = shard_grad.astype(F32)
+    low = jnp.where(c == 0, shard_grad, shard_oth)
+    high = jnp.where(c == 0, shard_oth, shard_grad)
+    grad_fc_w = jnp.concatenate([low[0:96], high[0:96]], axis=0)
+    grad_proj_w = jnp.concatenate([low[96:192], high[96:192]], axis=0)
+    grad_out_w = shard_grad[192:] + shard_oth[192:]
 
     vecs = [vrow[k * 48 : (k + 1) * 48] for k in range(8)]
     return (

time: 348 us -> 273 us (0.78)
  waiting for transfers between devices: 112 us -> 60 us
  starting transfers between devices: 92.6 us -> 72.4 us
  Pallas kernels: 91.2 us -> 95.9 us
  local copies, waits for them, and re-layouts: 21.2 us -> 16.9 us
    ppermute x54 -> x30, waiting for transfers between devices: 88.2 us -> 55 us  [shift(): return lax.ppermute(v, axis, [(i, (i + k) % 4) for i in range(4)])]
    ppermute x54 -> x30, starting transfers between devices: 73.1 us -> 51.2 us  [shift(): return lax.ppermute(v, axis, [(i, (i + k) % 4) for i in range(4)])]
    all_gather x1, waiting for transfers between devices: 16.6 us -> 0.02 us  [body(): lax.all_gather(part, ('z', 'y'), axis=0, tiled=True).reshape(16, 224, D)]
    pallas_call x5 -> x6, Pallas kernels: 71.1 us -> 76.6 us  [run(): pl.pallas_call(kernel, out_shape=outs, in_specs=first + specs * (len(args...]
    ppermute x11 -> x13, waiting for transfers between devices: 7.59 us -> 4.87 us  [swap(): return lax.ppermute(v, 'core', [(0, 1), (1, 0)])]
    unnamed x97 -> x88, local copies, waits for them, and re-layouts: 7.15 us -> 5.43 us
    ppermute x11 -> x13, starting transfers between devices: 19.5 us -> 21.1 us  [swap(): return lax.ppermute(v, 'core', [(0, 1), (1, 0)])]
    pallas_call x1 -> x2, Pallas kernels: 20.1 us -> 19.3 us  [the longest x1 13.4 us: body(): pl.pallas_call(mlp_kernel, grid=(2,), out_shape=mlp_outs, in_specs=[whole...]
  transfers between devices with their start and end apart: 66 -> 45, of which waited for: 30 -> 21; matrix products, arithmetic and copies ran while one was open for 6% -> 6% of each run, Pallas kernels for 10% -> 28%
where the time goes in v2:
time: 273 us; the launch traced here: 270 us
  Pallas kernels  95.9 us (35%)
  starting transfers between devices  72.4 us (27%)
  waiting for transfers between devices  60 us (22%)
  local copies, waits for them, and re-layouts  16.9 us (6%)
  between operations  14.9 us (5%)
  other arithmetic  9.53 us (3%)
    pallas_call x6, Pallas kernels, run(): pl.pallas_call(kernel, out_shape=outs, in_specs=first + specs * (len(args...  76.6 us
    ppermute x30, waiting for transfers between devices, shift(): return lax.ppermute(v, axis, [(i, (i + k) % 4) for i in range(4)])  55 us
    ppermute x30, starting transfers between devices, shift(): return lax.ppermute(v, axis, [(i, (i + k) % 4) for i in range(4)])  51.2 us
    ppermute x13, starting transfers between devices, swap(): return lax.ppermute(v, 'core', [(0, 1), (1, 0)])  21.1 us
    pallas_call x1, Pallas kernels, body(): pl.pallas_call(mlp_kernel, grid=(2,), out_shape=mlp_outs, in_specs=[whole...  13.4 us
    pallas_call x1, Pallas kernels, body(): pl.pallas_call(middle_grad_kernel, out_shape=[shp(ROWS, D, dtype=F32)] +...  5.82 us
  transfers between devices with their start and end apart: 45, of which 21 were waited for; matrix products, arithmetic and copies ran while one was open for 6% of the time, Pallas kernels for 28%

profile of v2, /device:TPU:1, one launch (start us, length us, event | category | flops | bytes accessed | tf_op | source)
XLA Modules:
  0.0 269.6 jit_solution(2075509874343807772)
XLA Ops:
  8.1 1.0 constant_dynamic-slice_fusion.6
  9.1 0.9 maximum_maximum_fusion
  11.3 2.5 collective-permute-start
  13.8 2.5 collective-permute-start.4
  16.3 2.2 collective-permute-start.2
  18.5 1.2 collective-permute-start.1
  19.7 3.6 %collective-permute-done.1 = bf16[64,576]{1,0:T(8,128)(2,1)S(1)} collective-permute-done((bf16[64,576]{1,0:T(8,128)(2,1)S(1)}, bf16[64,576]{1,0:T(8,128)(2,1)S(1)}, u32[]{:S(2)}, u32[]{:S(2)}) %collective-permute-start.1) | collective-permute-done | bytes 73760 | tf_op jit(solution)/shard_map/ppermute | solution.py:383
  23.8 3.1 %collective-permute-done.3.refs_1_.t1 = bf16[256,768]{1,0:T(8,128)(2,1)S(1)} collective-permute-done((bf16[256,768]{1,0:T(8,128)(2,1)S(1)}, bf16[256,768]{1,0:T(8,128)(2,1)S(1)}, u32[]{:S(2)}, u32[]{:S(2)}) %collective-permute-start.3) | collective-permute-done | bytes 393248 | tf_op jit(solution)/shard_map/ppermute | solution.py:383
  26.9 2.2 collective-permute-start.6
  29.0 2.7 %collective-permute-start.12 = (bf16[256,576]{1,0:T(8,128)(2,1)S(1)}, bf16[256,576]{1,0:T(8,128)(2,1)S(1)}, u32[]{:S(2)}, u32[]{:S(2)}) collective-permute-start(bf16[256,576]{1,0:T(8,128)(2,1)S(1)} %constant_dynamic-update-slice_fusion.refs_8_), channel_id=1, source_target_pairs={{0,3},{1,0},{2,1},{3,2},{4,7},{5,4},{6,5},{7,6},{8,11},{9,8},{10,9... | collective-permute-start | bytes 884744 | tf_op jit(solution)/shard_map/ppermute | solution.py:383
  33.5 7.9 %collective-permute-done.12.refs_11_ = bf16[256,576]{1,0:T(8,128)(2,1)S(1)} collective-permute-done((bf16[256,576]{1,0:T(8,128)(2,1)S(1)}, bf16[256,576]{1,0:T(8,128)(2,1)S(1)}, u32[]{:S(2)}, u32[]{:S(2)}) %collective-permute-start.12) | collective-permute-done | bytes 294944 | tf_op jit(solution)/shard_map/ppermute | solution.py:383
  41.5 1.1 collective-permute-start.7
  42.6 1.0 collective-permute-done.11.refs_10_
  43.6 1.5 collective-permute-start.9
  46.7 4.5 %collective-permute-done.10.refs_9_ = bf16[256,576]{1,0:T(8,128)(2,1)S(1)} collective-permute-done((bf16[256,576]{1,0:T(8,128)(2,1)S(1)}, bf16[256,576]{1,0:T(8,128)(2,1)S(1)}, u32[]{:S(2)}, u32[]{:S(2)}) %collective-permute-start.10) | collective-permute-done | bytes 294944 | tf_op jit(solution)/shard_map/ppermute | solution.py:383
  52.8 29.4 %attention_forward.1 = (bf16[256,192]{1,0:T(8,128)(2,1)}, bf16[256,192]{1,0:T(8,128)(2,1)}, bf16[256,192]{1,0:T(8,128)(2,1)}, bf16[256,192]{1,0:T(8,128)(2,1)}, ...) custom-call(s32[20]{0:T(128)} %concatenate.28.meta, ...), custom_call_target="tpu_custom_call" | custom-call | flops 24999999488 | bytes 25000000 | tf_op jit(solution)/shard_map/attention_forward/pallas_call | solution.py:416
  82.2 1.1 slice.267
  83.9 2.2 collective-permute-start.13
  86.1 0.8 collective-permute-start.14
  86.9 0.9 collective-permute-start.15
  87.8 1.1 select_bitcast_fusion.1
  89.0 1.1 copy.57
  90.2 1.8 collective-permute-done.13.a1
  92.6 3.5 %collective-permute-done.15.a3 = bf16[256,192]{1,0:T(8,128)(2,1)S(1)} collective-permute-done((bf16[256,192]{1,0:T(8,128)(2,1)}, bf16[256,192]{1,0:T(8,128)(2,1)S(1)}, u32[]{:S(2)}, u32[]{:S(2)}) %collective-permute-start.15) | collective-permute-done | bytes 98336 | tf_op jit(solution)/shard_map/ppermute | solution.py:383
  96.7 3.5 %middle.1 = (f32[256,768]{1,0:T(8,128)}, f32[256,768]{1,0:T(8,128)}, f32[256,1]{1,0:T(8,128)}, bf16[256,768]{1,0:T(8,128)(2,1)}) custom-call(s32[20]{0:T(128)} %concatenate.28.meta, bf16[256,192]{1,0:T(8,128)(2,1)} %get-tuple-element.67.a0, bf16[256,192]{1,0:T(8,128)(2,1)} %copy-done.30, bf16[256,192]{1,0:T(8,128)(2,1)} %copy-done.31, ...), custom_call_target="tpu_custom_call" | custom-call | flops 4000000000 | bytes 4000000 | tf_op jit(solution)/shard_map/middle/pallas_call | solution.py:416
  103.0 13.4 %feed_forward.1 = (f32[256,768]{1,0:T(8,128)}, bf16[256,768]{1,0:T(8,128)(2,1)}, f32[256,768]{1,0:T(8,128)}, bf16[256,768]{1,0:T(8,128)(2,1)}, bf16[16,240,768]{2,1,0:T(8,128)(2,1)}, /*index=5*/f32[2,1,768]{2,1,0:T(1,128)}) custom-call(bf16[256,768]{1,0:T(8,128)(2,1)} %get-tuple-element.73.n2_own, bf16[256,768]{1,0:T(8,128)(2,1)} %copy-done.28, ...), custom_call_target="tpu_custom_call" | custom-call | flops 17999998976 | bytes 18000000 | tf_op jit(solution)/shard_map/feed_forward/pallas_call | solution.py:546
  116.8 1.6 collective-permute-done.20.dn_recv
  119.1 5.8 %middle_grad.1 = (f32[256,768]{1,0:T(8,128)}, bf16[256,192]{1,0:T(8,128)(2,1)}, bf16[256,192]{1,0:T(8,128)(2,1)}, bf16[256,192]{1,0:T(8,128)(2,1)}, bf16[256,192...) custom-call(s32[20]{0:T(128)} %concatenate.28.meta, ...), custom_call_target="tpu_custom_call", output_to_operand_aliasing={{6}: (1, {})} | custom-call | flops 5000000000 | bytes 5000000 | tf_op jit(solution)/shard_map/middle_grad/pallas_call | solution.py:564
  125.0 0.9 copy-done.35
  126.1 1.5 collective-permute-start.22
  127.6 1.4 collective-permute-start.23
  128.9 5.9 %collective-permute-done.21.refs_1_ = bf16[256,192]{1,0:T(8,128)(2,1)S(1)} collective-permute-done((bf16[256,192]{1,0:T(8,128)(2,1)S(1)}, bf16[256,192]{1,0:T(8,128)(2,1)S(1)}, u32[]{:S(2)}, u32[]{:S(2)}) %collective-permute-start.21) | collective-permute-done | bytes 98336 | tf_op jit(solution)/shard_map/ppermute | solution.py:383
  135.8 26.7 %attention_backward.1 = (bf16[1024,192]{1,0:T(8,128)(2,1)}, f32[1024,384]{1,0:T(8,128)}, bf16[1024,384]{1,0:T(8,128)(2,1)}) custom-call(s32[20]{0:T(128)} %concatenate.28.meta, bf16[256,192]{1,0:T(8,128)(2,1)} %get-tuple-element.82.refs_0_, bf16[256,192]{1,0:T(8,128)(2,1)} %copy-done.36, bf16[256,192]{1,0:T(8,128)(2,1)} %copy-done.37, ...), custom_call_target="tpu_custom_call" | custom-call | flops 24000000000 | bytes 24000000 | tf_op jit(solution)/shard_map/attention_backward/pallas_call | solution.py:416
  162.5 2.5 collective-permute-done.24.recv_ref
  165.0 0.9 copy-done.18
  165.9 4.9 %input_grad.1 = (bf16[256,768]{1,0:T(8,128)(2,1)}, bf16[256,768]{1,0:T(8,128)(2,1)}, bf16[256,768]{1,0:T(8,128)(2,1)}, bf16[256,768]{1,0:T(8,128)(2,1)}, bf16[1024,576]{1,0:T(8,128)(2,1)}) custom-call(bf16[1024,192]{1,0:T(8,128)(2,1)} %get-tuple-element.92.dq_ref, f32[1024,384]{1,0:T(8,128)} %get-tuple-element.93.own_ref, bf16[1024,384]{1,0:T(8,128)(2,1)} %copy-done.18, ...), custom_call_target="tpu_custom_call" | custom-call | flops 5000000000 | bytes 5000000 | tf_op jit(solution)/shard_map/input_grad/pallas_call | solution.py:416
  170.8 8.9 %weight_grad.1 = (bf16[4,4,48,576]{3,2,1,0:T(8,128)(2,1)}, bf16[4,4,48,576]{3,2,1,0:T(8,128)(2,1)}) custom-call(s32[20]{0:T(128)} %concatenate.28.meta, bf16[1024,768]{1,0:T(8,128)(2,1)} %get-tuple-element.76.normed_ref, bf16[1024,576]{1,0:T(8,128)(2,1)} %get-tuple-element.96.g_ref, bf16[256,768]{1,0:T(8,128)(2,1)} %bitcast.107, ...), custom_call_target="tpu_custom_call" | custom-call | flops 8000000000 | bytes 8000000 | tf_op jit(solution)/shard_map/weight_grad/pallas_call | solution.py:416
  179.7 3.2 %collective-permute-start.29 = (bf16[256,768]{1,0:T(8,128)(2,1)S(1)}, bf16[256,768]{1,0:T(8,128)(2,1)S(1)}, u32[]{:S(2)}, u32[]{:S(2)}) collective-permute-start(bf16[256,768]{1,0:T(8,128)(2,1)S(1)} %copy-done.26), channel_id=1, source_target_pairs={{0,96},{32,0},{64,32},{96,64},{1,97},{33,1},{65,33},{97,65},{2,98}... | collective-permute-start | bytes 1179656 | tf_op jit(solution)/shard_map/ppermute | solution.py:383
  183.6 1.0 collective-permute-start.19
  184.6 1.4 fusion.4
  186.0 3.1 %collective-permute-start.26 = (bf16[4,48,576]{2,1,0:T(8,128)(2,1)S(1)}, bf16[4,48,576]{2,1,0:T(8,128)(2,1)S(1)}, u32[]{:S(2)}, u32[]{:S(2)}) collective-permute-start(bf16[4,48,576]{2,1,0:T(8,128)(2,1)S(1)} %get-tuple-element.119), channel_id=1, source_target_pairs={{0,4},{4,8},{8,12},{12,0},{1,5},{5,9},{9,13},{13,1},{2,6},{6,10},{... | collective-permute-start | bytes 663560 | tf_op jit(solution)/shard_map/ppermute | solution.py:383
  189.1 10.2 %collective-permute-done.29.n1 = bf16[256,768]{1,0:T(8,128)(2,1)S(1)} collective-permute-done((bf16[256,768]{1,0:T(8,128)(2,1)S(1)}, bf16[256,768]{1,0:T(8,128)(2,1)S(1)}, u32[]{:S(2)}, u32[]{:S(2)}) %collective-permute-start.29) | collective-permute-done | bytes 393248 | tf_op jit(solution)/shard_map/ppermute | solution.py:383
  199.3 4.8 %collective-permute-start.27 = (bf16[4,48,576]{2,1,0:T(8,128)(2,1)S(1)}, bf16[4,48,576]{2,1,0:T(8,128)(2,1)S(1)}, u32[]{:S(2)}, u32[]{:S(2)}) collective-permute-start(bf16[4,48,576]{2,1,0:T(8,128)(2,1)S(1)} %get-tuple-element.121), channel_id=1, source_target_pairs={{0,8},{4,12},{8,0},{12,4},{1,9},{5,13},{9,1},{13,5},{2,10},{6,14},... | collective-permute-start | bytes 663560 | tf_op jit(solution)/shard_map/ppermute | solution.py:383
  204.1 3.3 %token_grad.1 = f32[256,768]{1,0:T(8,128)} custom-call(bf16[256,768]{1,0:T(8,128)(2,1)} %bitcast.108, f32[256,768]{1,0:T(8,128)} %get-tuple-element.105.gm, f32[8,768]{1,0:T(8,128)} %reshape.201.refs_12_.vec, bf16[256,768]{1,0:T(8,128)(2,1)} %get-tuple-element.97.n0, bf16[256,768]{1,0:T(8,128)(2,1)} %copy-done.27, ...), custom_call_target="tpu_custom_call" | custom-call | flops 3000000000 | bytes 3000000 | tf_op jit(solution)/shard_map/token_grad/pallas_call | solution.py:416
  207.4 1.2 collective-permute-done.28
  208.7 1.1 fusion.2
  209.8 1.6 collective-permute-start.32
  211.4 8.5 %collective-permute-start.34 = (bf16[48,576]{1,0:T(8,128)(2,1)S(1)}, bf16[48,576]{1,0:T(8,128)(2,1)S(1)}, u32[]{:S(2)}, u32[]{:S(2)}) collective-permute-start(bf16[48,576]{1,0:T(8,128)(2,1)S(1)} %get-tuple-element.129), channel_id=1, source_target_pairs={{0,3},{1,0},{2,1},{3,2},{4,7},{5,4},{6,5},{7,6},{8,11},{9,8},{10,9... | collective-permute-start | bytes 165896 | tf_op jit(solution)/shard_map/ppermute | solution.py:383
  219.9 2.0 collective-permute-start.33
  222.0 2.6 collective-permute-done.33
  224.7 3.3 %collective-permute-start.35 = (bf16[48,576]{1,0:T(8,128)(2,1)S(1)}, bf16[48,576]{1,0:T(8,128)(2,1)S(1)}, u32[]{:S(2)}, u32[]{:S(2)}) collective-permute-start(bf16[48,576]{1,0:T(8,128)(2,1)S(1)} %get-tuple-element.116), channel_id=1, source_target_pairs={{0,96},{32,0},{64,32},{96,64},{1,97},{33,1},{65,33},{97,65},{2,98}... | collective-permute-start | bytes 165896 | tf_op jit(solution)/shard_map/ppermute | solution.py:383
  228.0 0.9 add_convert_fusion
  228.9 1.2 collective-permute-start.36
  230.1 3.5 %collective-permute-done.36 = bf16[48,576]{1,0:T(8,128)(2,1)S(1)} collective-permute-done((bf16[48,576]{1,0:T(8,128)(2,1)S(1)}, bf16[48,576]{1,0:T(8,128)(2,1)S(1)}, u32[]{:S(2)}, u32[]{:S(2)}) %collective-permute-start.36) | collective-permute-done | bytes 55328 | tf_op jit(solution)/shard_map/ppermute | solution.py:383
  233.9 2.4 collective-permute-start.41
  236.3 1.3 collective-permute-start.39
  238.2 5.7 %collective-permute-start.38 = (bf16[4,32,576]{2,1,0:T(8,128)(2,1)S(1)}, bf16[4,32,576]{2,1,0:T(8,128)(2,1)S(1)}, u32[]{:S(2)}, u32[]{:S(2)}) collective-permute-start(bf16[4,32,576]{2,1,0:T(8,128)(2,1)S(1)} %constant_dynamic-slice_fusion.3), channel_id=1, source_target_pairs={{0,16},{16,0},{1,17},{17,1},{2,18},{18,2},{3,19},{19,3},{4,20},{20... | collective-permute-start | bytes 442376 | tf_op jit(solution)/shard_map/ppermute | solution.py:387
  244.5 3.8 %collective-permute-done.40 = bf16[240,768]{1,0:T(8,128)(2,1)S(1)} collective-permute-done((bf16[240,768]{1,0:T(8,128)(2,1)}, bf16[240,768]{1,0:T(8,128)(2,1)S(1)}, u32[]{:S(2)}, u32[]{:S(2)}) %collective-permute-start.40) | collective-permute-done | bytes 368672 | tf_op jit(solution)/shard_map/ppermute | solution.py:383
  248.3 0.8 collective-permute-done.39
  249.1 1.2 fusion.13
  250.3 7.7 %collective-permute-start.42 = (bf16[240,768]{1,0:T(8,128)(2,1)S(1)}, bf16[240,768]{1,0:T(8,128)(2,1)S(1)}, u32[]{:S(2)}, u32[]{:S(2)}) collective-permute-start(bf16[240,768]{1,0:T(8,128)(2,1)S(1)} %get-tuple-element.114), channel_id=1, source_target_pairs={{0,16},{16,0},{1,17},{17,1},{2,18},{18,2},{3,19},{19,3},{4,20},{20... | collective-permute-start | bytes 1105928 | tf_op jit(solution)/shard_map/ppermute | solution.py:387
  258.8 1.1 reshape.223
  260.8 0.9 pad_maximum_fusion.2
  261.7 0.9 pad_maximum_fusion.1
  (195 shorter events, 18.6 us)
Async XLA Ops:
  7.2 3.8 %copy-start.16 = (bf16[48]{0:T(256)(128)(2,1)S(1)}, bf16[48]{0:T(256)(128)(2,1)}, u32[]{:S(2)}) copy-start(bf16[48]{0:T(256)(128)(2,1)} %param.30) | copy-start | bytes 292
  7.2 3.8 %copy-start.17 = (bf16[192]{0:T(256)(128)(2,1)S(1)}, bf16[192]{0:T(256)(128)(2,1)}, u32[]{:S(2)}) copy-start(bf16[192]{0:T(256)(128)(2,1)} %param.28) | copy-start | bytes 1156
  7.2 3.8 %copy-start.15 = (bf16[48]{0:T(256)(128)(2,1)S(1)}, bf16[48]{0:T(256)(128)(2,1)}, u32[]{:S(2)}) copy-start(bf16[48]{0:T(256)(128)(2,1)} %param.26) | copy-start | bytes 292
  7.2 3.8 %copy-start.14 = (bf16[48]{0:T(256)(128)(2,1)S(1)}, bf16[48]{0:T(256)(128)(2,1)}, u32[]{:S(2)}) copy-start(bf16[48]{0:T(256)(128)(2,1)} %param.25) | copy-start | bytes 292
  7.3 6.5 %copy-start.20 = (bf16[1,2,128,768]{3,2,1,0:T(8,128)(2,1)S(1)}, bf16[1,2,128,768]{3,2,1,0:T(8,128)(2,1)}, u32[]{:S(2)}) copy-start(bf16[1,2,128,768]{3,2,1,0:T(8,128)(2,1)} %param.16) | copy-start | bytes 1179652
  7.3 74.9 %all-gather.2.cloned.1.call-start = ((), (), s32[]{:S(2)}) async-start(), calls=%async_computation.1 | async-start | bytes 5849088 | tf_op jit(solution)/shard_map/all_gather | solution.py:495
  9.1 23.1 %copy-start.8 = (s32[1,16]{1,0:T(1,128)S(1)}, s32[1,16]{1,0:T(1,128)}, u32[]{:S(2)}) copy-start(s32[1,16]{1,0:T(1,128)} %param.17) | copy-start | bytes 196
  10.0 223.9 %reduce-scatter.2.cloned.1.call-start = ((), (), s32[]{:S(2)}) async-start(), calls=%async_computation.2 | async-start | bytes 6266880 | tf_op jit(solution)/shard_map/reduce_scatter | solution.py:577
  11.3 8.4 %collective-permute-start = (bf16[64,576]{1,0:T(8,128)(2,1)S(1)}, bf16[64,576]{1,0:T(8,128)(2,1)S(1)}, u32[]{:S(2)}, u32[]{:S(2)}) collective-permute-start(bf16[64,576]{1,0:T(8,128)(2,1)S(1)} %pad_maximum_fusion.3), channel_id=1, source_target_pairs={{0,4},{4,8},{8,12},{12,0},{1,5},{5,9},{9,13},{13,1},{2,6},{6,10},{... | collective-permute-start | bytes 221192 | tf_op jit(solution)/shard_map/ppermute | solution.py:383
  13.8 9.9 %collective-permute-start.4 = (bf16[256,768]{1,0:T(8,128)(2,1)S(1)}, bf16[256,768]{1,0:T(8,128)(2,1)S(1)}, u32[]{:S(2)}, u32[]{:S(2)}) collective-permute-start(bf16[256,768]{1,0:T(8,128)(2,1)S(1)} %bitcast.109), channel_id=1, source_target_pairs={{0,96},{32,0},{64,32},{96,64},{1,97},{33,1},{65,33},{97,65},{2,98}... | collective-permute-start | bytes 1179656 | tf_op jit(solution)/shard_map/ppermute | solution.py:383
  16.3 10.6 %collective-permute-start.3 = (bf16[256,768]{1,0:T(8,128)(2,1)S(1)}, bf16[256,768]{1,0:T(8,128)(2,1)S(1)}, u32[]{:S(2)}, u32[]{:S(2)}) collective-permute-start(bf16[256,768]{1,0:T(8,128)(2,1)S(1)} %bitcast.110), channel_id=1, source_target_pairs={{0,32},{32,64},{64,96},{96,0},{1,33},{33,65},{65,97},{97,1},{2,34}... | collective-permute-start | bytes 1179656 | tf_op jit(solution)/shard_map/ppermute | solution.py:383
  16.3 7.0 %collective-permute-start.2 = (bf16[64,576]{1,0:T(8,128)(2,1)S(1)}, bf16[64,576]{1,0:T(8,128)(2,1)S(1)}, u32[]{:S(2)}, u32[]{:S(2)}) collective-permute-start(bf16[64,576]{1,0:T(8,128)(2,1)S(1)} %pad_maximum_fusion.3), channel_id=1, source_target_pairs={{0,12},{4,0},{8,4},{12,8},{1,13},{5,1},{9,5},{13,9},{2,14},{6,2},{... | collective-permute-start | bytes 221192 | tf_op jit(solution)/shard_map/ppermute | solution.py:383
  18.5 4.8 %collective-permute-start.1 = (bf16[64,576]{1,0:T(8,128)(2,1)S(1)}, bf16[64,576]{1,0:T(8,128)(2,1)S(1)}, u32[]{:S(2)}, u32[]{:S(2)}) collective-permute-start(bf16[64,576]{1,0:T(8,128)(2,1)S(1)} %pad_maximum_fusion.3), channel_id=1, source_target_pairs={{0,8},{4,12},{8,0},{12,4},{1,9},{5,13},{9,1},{13,5},{2,10},{6,14},... | collective-permute-start | bytes 221192 | tf_op jit(solution)/shard_map/ppermute | solution.py:383
  23.3 29.4 %copy-start.4 = (bf16[256,576]{1,0:T(8,128)(2,1)}, bf16[256,576]{1,0:T(8,128)(2,1)S(1)}, u32[]{:S(2)}) copy-start(bf16[256,576]{1,0:T(8,128)(2,1)S(1)} %constant_dynamic-update-slice_fusion.refs_8_) | copy-start | bytes 884740
  23.8 29.0 %copy-start.21 = (bf16[256,768]{1,0:T(8,128)(2,1)}, bf16[256,768]{1,0:T(8,128)(2,1)S(1)}, u32[]{:S(2)}) copy-start(bf16[256,768]{1,0:T(8,128)(2,1)S(1)} %collective-permute-done.4.refs_3_.t3) | copy-start | bytes 1179652
  26.9 25.9 %copy-start.22 = (bf16[256,768]{1,0:T(8,128)(2,1)}, bf16[256,768]{1,0:T(8,128)(2,1)S(1)}, u32[]{:S(2)}) copy-start(bf16[256,768]{1,0:T(8,128)(2,1)S(1)} %collective-permute-done.3.refs_1_.t1) | copy-start | bytes 1179652
  26.9 18.3 %collective-permute-start.5 = (bf16[256,768]{1,0:T(8,128)(2,1)S(1)}, bf16[256,768]{1,0:T(8,128)(2,1)}, u32[]{:S(2)}, u32[]{:S(2)}) collective-permute-start(bf16[256,768]{1,0:T(8,128)(2,1)S(1)} %bitcast.111), channel_id=1, source_target_pairs={{0,64},{32,96},{64,0},{96,32},{1,65},{33,97},{65,1},{97,33},{2,66}... | collective-permute-start | bytes 1179656 | tf_op jit(solution)/shard_map/ppermute | solution.py:383
  26.9 25.9 %collective-permute-start.6 = (bf16[256,768]{1,0:T(8,128)(2,1)S(1)}, bf16[256,768]{1,0:T(8,128)(2,1)}, u32[]{:S(2)}, u32[]{:S(2)}) collective-permute-start(bf16[256,768]{1,0:T(8,128)(2,1)S(1)} %bitcast.112), channel_id=1, source_target_pairs={{0,16},{16,0},{1,17},{17,1},{2,18},{18,2},{3,19},{19,3},{4,20},{20... | collective-permute-start | bytes 1179656 | tf_op jit(solution)/shard_map/ppermute | solution.py:387
  29.0 12.4 %collective-permute-start.12 = (bf16[256,576]{1,0:T(8,128)(2,1)S(1)}, bf16[256,576]{1,0:T(8,128)(2,1)S(1)}, u32[]{:S(2)}, u32[]{:S(2)}) collective-permute-start(bf16[256,576]{1,0:T(8,128)(2,1)S(1)} %constant_dynamic-update-slice_fusion.refs_8_), channel_id=1, source_target_pairs={{0,3},{1,0},{2,1},{3,2},{4,7},{5,4},{6,5},{7,6},{8,11},{9,8},{10,9... | collective-permute-start | bytes 884744 | tf_op jit(solution)/shard_map/ppermute | solution.py:383
  31.8 11.8 %collective-permute-start.11 = (bf16[256,576]{1,0:T(8,128)(2,1)S(1)}, bf16[256,576]{1,0:T(8,128)(2,1)S(1)}, u32[]{:S(2)}, u32[]{:S(2)}) collective-permute-start(bf16[256,576]{1,0:T(8,128)(2,1)S(1)} %constant_dynamic-update-slice_fusion.refs_8_), channel_id=1, source_target_pairs={{0,2},{1,3},{2,0},{3,1},{4,6},{5,7},{6,4},{7,5},{8,10},{9,11},{10,... | collective-permute-start | bytes 884744 | tf_op jit(solution)/shard_map/ppermute | solution.py:383
  32.7 18.4 %collective-permute-start.10 = (bf16[256,576]{1,0:T(8,128)(2,1)S(1)}, bf16[256,576]{1,0:T(8,128)(2,1)S(1)}, u32[]{:S(2)}, u32[]{:S(2)}) collective-permute-start(bf16[256,576]{1,0:T(8,128)(2,1)S(1)} %constant_dynamic-update-slice_fusion.refs_8_), channel_id=1, source_target_pairs={{0,1},{1,2},{2,3},{3,0},{4,5},{5,6},{6,7},{7,4},{8,9},{9,10},{10,1... | collective-permute-start | bytes 884744 | tf_op jit(solution)/shard_map/ppermute | solution.py:383
  41.5 11.3 %copy-start.5 = (bf16[256,576]{1,0:T(8,128)(2,1)}, bf16[256,576]{1,0:T(8,128)(2,1)S(1)}, u32[]{:S(2)}) copy-start(bf16[256,576]{1,0:T(8,128)(2,1)S(1)} %collective-permute-done.12.refs_11_) | copy-start | bytes 884740
  41.5 11.3 %collective-permute-start.7 = (bf16[256,768]{1,0:T(8,128)(2,1)S(1)}, bf16[256,768]{1,0:T(8,128)(2,1)}, u32[]{:S(2)}, u32[]{:S(2)}) collective-permute-start(bf16[256,768]{1,0:T(8,128)(2,1)S(1)} %collective-permute-done.3.refs_1_.t1), channel_id=1, source_target_pairs={{0,16},{16,0},{1,17},{17,1},{2,18},{18,2},{3,19},{19,3},{4,20},{20... | collective-permute-start | bytes 1179656 | tf_op jit(solution)/shard_map/ppermute | solution.py:387
  43.6 9.2 %copy-start.6 = (bf16[256,576]{1,0:T(8,128)(2,1)}, bf16[256,576]{1,0:T(8,128)(2,1)S(1)}, u32[]{:S(2)}) copy-start(bf16[256,576]{1,0:T(8,128)(2,1)S(1)} %collective-permute-done.11.refs_10_) | copy-start | bytes 884740
  43.6 9.1 %collective-permute-start.9 = (bf16[256,768]{1,0:T(8,128)(2,1)S(1)}, bf16[256,768]{1,0:T(8,128)(2,1)}, u32[]{:S(2)}, u32[]{:S(2)}) collective-permute-start(bf16[256,768]{1,0:T(8,128)(2,1)S(1)} %collective-permute-done.4.refs_3_.t3), channel_id=1, source_target_pairs={{0,16},{16,0},{1,17},{17,1},{2,18},{18,2},{3,19},{19,3},{4,20},{20... | collective-permute-start | bytes 1179656 | tf_op jit(solution)/shard_map/ppermute | solution.py:387
  45.1 7.6 %collective-permute-start.8 = (bf16[256,768]{1,0:T(8,128)(2,1)}, bf16[256,768]{1,0:T(8,128)(2,1)}, u32[]{:S(2)}, u32[]{:S(2)}) collective-permute-start(bf16[256,768]{1,0:T(8,128)(2,1)} %collective-permute-done.5.refs_2_.t2), channel_id=1, source_target_pairs={{0,16},{16,0},{1,17},{17,1},{2,18},{18,2},{3,19},{19,3},{4,20},{20... | collective-permute-start | bytes 1179656 | tf_op jit(solution)/shard_map/ppermute | solution.py:387
  52.7 30.7 %copy-start.19 = (bf16[1,2,128,768]{3,2,1,0:T(8,128)(2,1)S(1)}, bf16[1,2,128,768]{3,2,1,0:T(8,128)(2,1)}, u32[]{:S(2)}) copy-start(bf16[1,2,128,768]{3,2,1,0:T(8,128)(2,1)} %param.31) | copy-start | bytes 1179652
  83.3 4.4 %collective-permute-start.16 = (bf16[16,24,768]{2,1,0:T(8,128)(2,1)S(1)}, bf16[16,24,768]{2,1,0:T(8,128)(2,1)S(1)}, u32[]{:S(2)}, u32[]{:S(2)}) collective-permute-start(bf16[16,24,768]{2,1,0:T(8,128)(2,1)S(1)} %slice.267), channel_id=1, source_target_pairs={{0,16},{16,0},{1,17},{17,1},{2,18},{18,2},{3,19},{19,3},{4,20},{20... | collective-permute-start | bytes 1769480 | tf_op jit(solution)/shard_map/ppermute | solution.py:387
  83.5 18.0 %collective-permute-start.18 = (bf16[256,768]{1,0:T(8,128)(2,1)S(1)}, bf16[256,768]{1,0:T(8,128)(2,1)S(1)}, u32[]{:S(2)}, u32[]{:S(2)}) collective-permute-start(bf16[256,768]{1,0:T(8,128)(2,1)S(1)} %bitcast.104), channel_id=1, source_target_pairs={{0,16},{16,0},{1,17},{17,1},{2,18},{18,2},{3,19},{19,3},{4,20},{20... | collective-permute-start | bytes 1179656 | tf_op jit(solution)/shard_map/ppermute | solution.py:387
  83.9 8.0 %collective-permute-start.13 = (bf16[256,192]{1,0:T(8,128)(2,1)}, bf16[256,192]{1,0:T(8,128)(2,1)S(1)}, u32[]{:S(2)}, u32[]{:S(2)}) collective-permute-start(bf16[256,192]{1,0:T(8,128)(2,1)} %get-tuple-element.68), channel_id=1, source_target_pairs={{0,96},{32,0},{64,32},{96,64},{1,97},{33,1},{65,33},{97,65},{2,98}... | collective-permute-start | bytes 294920 | tf_op jit(solution)/shard_map/ppermute | solution.py:383
  86.1 6.4 %collective-permute-start.14 = (bf16[256,192]{1,0:T(8,128)(2,1)}, bf16[256,192]{1,0:T(8,128)(2,1)S(1)}, u32[]{:S(2)}, u32[]{:S(2)}) collective-permute-start(bf16[256,192]{1,0:T(8,128)(2,1)} %get-tuple-element.69), channel_id=1, source_target_pairs={{0,64},{32,96},{64,0},{96,32},{1,65},{33,97},{65,1},{97,33},{2,66}... | collective-permute-start | bytes 294920 | tf_op jit(solution)/shard_map/ppermute | solution.py:383
  86.9 9.1 %collective-permute-start.15 = (bf16[256,192]{1,0:T(8,128)(2,1)}, bf16[256,192]{1,0:T(8,128)(2,1)S(1)}, u32[]{:S(2)}, u32[]{:S(2)}) collective-permute-start(bf16[256,192]{1,0:T(8,128)(2,1)} %get-tuple-element.70), channel_id=1, source_target_pairs={{0,32},{32,64},{64,96},{96,0},{1,33},{33,65},{65,97},{97,1},{2,34}... | collective-permute-start | bytes 294920 | tf_op jit(solution)/shard_map/ppermute | solution.py:383
  91.9 4.1 %copy-start.30 = (bf16[256,192]{1,0:T(8,128)(2,1)}, bf16[256,192]{1,0:T(8,128)(2,1)S(1)}, u32[]{:S(2)}) copy-start(bf16[256,192]{1,0:T(8,128)(2,1)S(1)} %collective-permute-done.13.a1) | copy-start | bytes 294916
  100.2 2.1 collective-permute-start.17
  116.5 1.9 collective-permute-start.20
  125.9 9.0 %collective-permute-start.21 = (bf16[256,192]{1,0:T(8,128)(2,1)S(1)}, bf16[256,192]{1,0:T(8,128)(2,1)S(1)}, u32[]{:S(2)}, u32[]{:S(2)}) collective-permute-start(bf16[256,192]{1,0:T(8,128)(2,1)S(1)} %copy-done.35), channel_id=1, source_target_pairs={{0,32},{32,64},{64,96},{96,0},{1,33},{33,65},{65,97},{97,1},{2,34}... | collective-permute-start | bytes 294920 | tf_op jit(solution)/shard_map/ppermute | solution.py:383
  126.1 8.8 %collective-permute-start.22 = (bf16[256,192]{1,0:T(8,128)(2,1)S(1)}, bf16[256,192]{1,0:T(8,128)(2,1)S(1)}, u32[]{:S(2)}, u32[]{:S(2)}) collective-permute-start(bf16[256,192]{1,0:T(8,128)(2,1)S(1)} %copy-done.34), channel_id=1, source_target_pairs={{0,64},{32,96},{64,0},{96,32},{1,65},{33,97},{65,1},{97,33},{2,66}... | collective-permute-start | bytes 294920 | tf_op jit(solution)/shard_map/ppermute | solution.py:383
  127.6 7.6 %collective-permute-start.23 = (bf16[256,192]{1,0:T(8,128)(2,1)S(1)}, bf16[256,192]{1,0:T(8,128)(2,1)S(1)}, u32[]{:S(2)}, u32[]{:S(2)}) collective-permute-start(bf16[256,192]{1,0:T(8,128)(2,1)S(1)} %copy-done.33), channel_id=1, source_target_pairs={{0,96},{32,0},{64,32},{96,64},{1,97},{33,1},{65,33},{97,65},{2,98}... | collective-permute-start | bytes 294920 | tf_op jit(solution)/shard_map/ppermute | solution.py:383
  162.5 2.5 collective-permute-start.24
  170.8 8.9 %copy-start.26 = (bf16[256,768]{1,0:T(8,128)(2,1)S(1)}, bf16[256,768]{1,0:T(8,128)(2,1)}, u32[]{:S(2)}) copy-start(bf16[256,768]{1,0:T(8,128)(2,1)} %get-tuple-element.98.n1) | copy-start | bytes 1179652
  170.8 12.1 %copy-start.25 = (bf16[256,768]{1,0:T(8,128)(2,1)S(1)}, bf16[256,768]{1,0:T(8,128)(2,1)}, u32[]{:S(2)}) copy-start(bf16[256,768]{1,0:T(8,128)(2,1)} %get-tuple-element.99.n2) | copy-start | bytes 1179652
  170.8 12.1 %copy-start.24 = (bf16[256,768]{1,0:T(8,128)(2,1)S(1)}, bf16[256,768]{1,0:T(8,128)(2,1)}, u32[]{:S(2)}) copy-start(bf16[256,768]{1,0:T(8,128)(2,1)} %get-tuple-element.100.n3) | copy-start | bytes 1179652
  179.7 4.9 %collective-permute-start.25 = (bf16[4,4,48,576]{3,2,1,0:T(8,128)(2,1)}, bf16[4,4,48,576]{3,2,1,0:T(8,128)(2,1)S(1)}, u32[]{:S(2)}, u32[]{:S(2)}) collective-permute-start(bf16[4,4,48,576]{3,2,1,0:T(8,128)(2,1)} %get-tuple-element.104), channel_id=1, source_target_pairs={{0,16},{16,0},{1,17},{17,1},{2,18},{18,2},{3,19},{19,3},{4,20},{20... | collective-permute-start | bytes 2654216 | tf_op jit(solution)/shard_map/ppermute | solution.py:387
  179.7 19.5 %collective-permute-start.29 = (bf16[256,768]{1,0:T(8,128)(2,1)S(1)}, bf16[256,768]{1,0:T(8,128)(2,1)S(1)}, u32[]{:S(2)}, u32[]{:S(2)}) collective-permute-start(bf16[256,768]{1,0:T(8,128)(2,1)S(1)} %copy-done.26), channel_id=1, source_target_pairs={{0,96},{32,0},{64,32},{96,64},{1,97},{33,1},{65,33},{97,65},{2,98}... | collective-permute-start | bytes 1179656 | tf_op jit(solution)/shard_map/ppermute | solution.py:383
  182.9 16.3 %collective-permute-start.30 = (bf16[256,768]{1,0:T(8,128)(2,1)S(1)}, bf16[256,768]{1,0:T(8,128)(2,1)}, u32[]{:S(2)}, u32[]{:S(2)}) collective-permute-start(bf16[256,768]{1,0:T(8,128)(2,1)S(1)} %copy-done.25), channel_id=1, source_target_pairs={{0,64},{32,96},{64,0},{96,32},{1,65},{33,97},{65,1},{97,33},{2,66}... | collective-permute-start | bytes 1179656 | tf_op jit(solution)/shard_map/ppermute | solution.py:383
  182.9 21.2 %collective-permute-start.31 = (bf16[256,768]{1,0:T(8,128)(2,1)S(1)}, bf16[256,768]{1,0:T(8,128)(2,1)}, u32[]{:S(2)}, u32[]{:S(2)}) collective-permute-start(bf16[256,768]{1,0:T(8,128)(2,1)S(1)} %copy-done.24), channel_id=1, source_target_pairs={{0,32},{32,64},{64,96},{96,0},{1,33},{33,65},{65,97},{97,1},{2,34}... | collective-permute-start | bytes 1179656 | tf_op jit(solution)/shard_map/ppermute | solution.py:383
  183.6 44.4 %collective-permute-start.19 = (bf16[256,768]{1,0:T(8,128)(2,1)}, bf16[256,768]{1,0:T(8,128)(2,1)S(1)}, u32[]{:S(2)}, u32[]{:S(2)}) collective-permute-start(bf16[256,768]{1,0:T(8,128)(2,1)} %get-tuple-element.75), channel_id=1, source_target_pairs={{0,16},{16,0},{1,17},{17,1},{2,18},{18,2},{3,19},{19,3},{4,20},{20... | collective-permute-start | bytes 1179656 | tf_op jit(solution)/shard_map/ppermute | solution.py:387
  186.0 21.4 %collective-permute-start.26 = (bf16[4,48,576]{2,1,0:T(8,128)(2,1)S(1)}, bf16[4,48,576]{2,1,0:T(8,128)(2,1)S(1)}, u32[]{:S(2)}, u32[]{:S(2)}) collective-permute-start(bf16[4,48,576]{2,1,0:T(8,128)(2,1)S(1)} %get-tuple-element.119), channel_id=1, source_target_pairs={{0,4},{4,8},{8,12},{12,0},{1,5},{5,9},{9,13},{13,1},{2,6},{6,10},{... | collective-permute-start | bytes 663560 | tf_op jit(solution)/shard_map/ppermute | solution.py:383
  199.3 4.8 %copy-start.27 = (bf16[256,768]{1,0:T(8,128)(2,1)}, bf16[256,768]{1,0:T(8,128)(2,1)S(1)}, u32[]{:S(2)}) copy-start(bf16[256,768]{1,0:T(8,128)(2,1)S(1)} %collective-permute-done.29.n1) | copy-start | bytes 1179652
  199.3 9.4 %collective-permute-start.28 = (bf16[4,48,576]{2,1,0:T(8,128)(2,1)S(1)}, bf16[4,48,576]{2,1,0:T(8,128)(2,1)S(1)}, u32[]{:S(2)}, u32[]{:S(2)}) collective-permute-start(bf16[4,48,576]{2,1,0:T(8,128)(2,1)S(1)} %get-tuple-element.120), channel_id=1, source_target_pairs={{0,12},{4,0},{8,4},{12,8},{1,13},{5,1},{9,5},{13,9},{2,14},{6,2},{... | collective-permute-start | bytes 663560 | tf_op jit(solution)/shard_map/ppermute | solution.py:383
  199.3 9.4 %collective-permute-start.27 = (bf16[4,48,576]{2,1,0:T(8,128)(2,1)S(1)}, bf16[4,48,576]{2,1,0:T(8,128)(2,1)S(1)}, u32[]{:S(2)}, u32[]{:S(2)}) collective-permute-start(bf16[4,48,576]{2,1,0:T(8,128)(2,1)S(1)} %get-tuple-element.121), channel_id=1, source_target_pairs={{0,8},{4,12},{8,0},{12,4},{1,9},{5,13},{9,1},{13,5},{2,10},{6,14},... | collective-permute-start | bytes 663560 | tf_op jit(solution)/shard_map/ppermute | solution.py:383
  207.4 20.6 %copy-start.1 = (f32[256,768]{1,0:T(8,128)S(1)}, f32[256,768]{1,0:T(8,128)}, u32[]{:S(2)}) copy-start(f32[256,768]{1,0:T(8,128)} %get-tuple-element.72) | copy-start | bytes 2359300
  207.4 20.6 %copy-start.2 = (f32[256,768]{1,0:T(8,128)S(1)}, f32[256,768]{1,0:T(8,128)}, u32[]{:S(2)}) copy-start(f32[256,768]{1,0:T(8,128)} %get-tuple-element.74) | copy-start | bytes 2359300
  209.8 12.2 %collective-permute-start.32 = (bf16[48,576]{1,0:T(8,128)(2,1)S(1)}, bf16[48,576]{1,0:T(8,128)(2,1)S(1)}, u32[]{:S(2)}, u32[]{:S(2)}) collective-permute-start(bf16[48,576]{1,0:T(8,128)(2,1)S(1)} %get-tuple-element.128), channel_id=1, source_target_pairs={{0,1},{1,2},{2,3},{3,0},{4,5},{5,6},{6,7},{7,4},{8,9},{9,10},{10,1... | collective-permute-start | bytes 165896 | tf_op jit(solution)/shard_map/ppermute | solution.py:383
  211.4 10.6 %collective-permute-start.34 = (bf16[48,576]{1,0:T(8,128)(2,1)S(1)}, bf16[48,576]{1,0:T(8,128)(2,1)S(1)}, u32[]{:S(2)}, u32[]{:S(2)}) collective-permute-start(bf16[48,576]{1,0:T(8,128)(2,1)S(1)} %get-tuple-element.129), channel_id=1, source_target_pairs={{0,3},{1,0},{2,1},{3,2},{4,7},{5,4},{6,5},{7,6},{8,11},{9,8},{10,9... | collective-permute-start | bytes 165896 | tf_op jit(solution)/shard_map/ppermute | solution.py:383
  219.9 4.8 %collective-permute-start.33 = (bf16[48,576]{1,0:T(8,128)(2,1)S(1)}, bf16[48,576]{1,0:T(8,128)(2,1)S(1)}, u32[]{:S(2)}, u32[]{:S(2)}) collective-permute-start(bf16[48,576]{1,0:T(8,128)(2,1)S(1)} %get-tuple-element.130), channel_id=1, source_target_pairs={{0,2},{1,3},{2,0},{3,1},{4,6},{5,7},{6,4},{7,5},{8,10},{9,11},{10,... | collective-permute-start | bytes 165896 | tf_op jit(solution)/shard_map/ppermute | solution.py:383
  224.7 5.4 %collective-permute-start.35 = (bf16[48,576]{1,0:T(8,128)(2,1)S(1)}, bf16[48,576]{1,0:T(8,128)(2,1)S(1)}, u32[]{:S(2)}, u32[]{:S(2)}) collective-permute-start(bf16[48,576]{1,0:T(8,128)(2,1)S(1)} %get-tuple-element.116), channel_id=1, source_target_pairs={{0,96},{32,0},{64,32},{96,64},{1,97},{33,1},{65,33},{97,65},{2,98}... | collective-permute-start | bytes 165896 | tf_op jit(solution)/shard_map/ppermute | solution.py:383
  228.9 4.9 %collective-permute-start.37 = (bf16[48,576]{1,0:T(8,128)(2,1)S(1)}, bf16[48,576]{1,0:T(8,128)(2,1)S(1)}, u32[]{:S(2)}, u32[]{:S(2)}) collective-permute-start(bf16[48,576]{1,0:T(8,128)(2,1)S(1)} %get-tuple-element.116), channel_id=1, source_target_pairs={{0,32},{32,64},{64,96},{96,0},{1,33},{33,65},{65,97},{97,1},{2,34}... | collective-permute-start | bytes 165896 | tf_op jit(solution)/shard_map/ppermute | solution.py:383
  228.9 4.7 %collective-permute-start.36 = (bf16[48,576]{1,0:T(8,128)(2,1)S(1)}, bf16[48,576]{1,0:T(8,128)(2,1)S(1)}, u32[]{:S(2)}, u32[]{:S(2)}) collective-permute-start(bf16[48,576]{1,0:T(8,128)(2,1)S(1)} %get-tuple-element.116), channel_id=1, source_target_pairs={{0,64},{32,96},{64,0},{96,32},{1,65},{33,97},{65,1},{97,33},{2,66}... | collective-permute-start | bytes 165896 | tf_op jit(solution)/shard_map/ppermute | solution.py:383
  233.9 10.6 %collective-permute-start.41 = (bf16[240,768]{1,0:T(8,128)(2,1)}, bf16[240,768]{1,0:T(8,128)(2,1)S(1)}, u32[]{:S(2)}, u32[]{:S(2)}) collective-permute-start(bf16[240,768]{1,0:T(8,128)(2,1)} %reduce-scatter.2.cloned.1.call-done), channel_id=1, source_target_pairs={{0,96},{32,0},{64,32},{96,64},{1,97},{33,1},{65,33},{97,65},{2,98}... | collective-permute-start | bytes 1105928 | tf_op jit(solution)/shard_map/ppermute | solution.py:383
  236.3 12.0 %collective-permute-start.40 = (bf16[240,768]{1,0:T(8,128)(2,1)}, bf16[240,768]{1,0:T(8,128)(2,1)S(1)}, u32[]{:S(2)}, u32[]{:S(2)}) collective-permute-start(bf16[240,768]{1,0:T(8,128)(2,1)} %reduce-scatter.2.cloned.1.call-done), channel_id=1, source_target_pairs={{0,32},{32,64},{64,96},{96,0},{1,33},{33,65},{65,97},{97,1},{2,34}... | collective-permute-start | bytes 1105928 | tf_op jit(solution)/shard_map/ppermute | solution.py:383
  236.3 12.7 %collective-permute-start.39 = (bf16[240,768]{1,0:T(8,128)(2,1)}, bf16[240,768]{1,0:T(8,128)(2,1)S(1)}, u32[]{:S(2)}, u32[]{:S(2)}) collective-permute-start(bf16[240,768]{1,0:T(8,128)(2,1)} %reduce-scatter.2.cloned.1.call-done), channel_id=1, source_target_pairs={{0,64},{32,96},{64,0},{96,32},{1,65},{33,97},{65,1},{97,33},{2,66}... | collective-permute-start | bytes 1105928 | tf_op jit(solution)/shard_map/ppermute | solution.py:383
  238.2 19.7 %collective-permute-start.38 = (bf16[4,32,576]{2,1,0:T(8,128)(2,1)S(1)}, bf16[4,32,576]{2,1,0:T(8,128)(2,1)S(1)}, u32[]{:S(2)}, u32[]{:S(2)}) collective-permute-start(bf16[4,32,576]{2,1,0:T(8,128)(2,1)S(1)} %constant_dynamic-slice_fusion.3), channel_id=1, source_target_pairs={{0,16},{16,0},{1,17},{17,1},{2,18},{18,2},{3,19},{19,3},{4,20},{20... | collective-permute-start | bytes 442376 | tf_op jit(solution)/shard_map/ppermute | solution.py:387
  250.3 9.6 %collective-permute-start.42 = (bf16[240,768]{1,0:T(8,128)(2,1)S(1)}, bf16[240,768]{1,0:T(8,128)(2,1)S(1)}, u32[]{:S(2)}, u32[]{:S(2)}) collective-permute-start(bf16[240,768]{1,0:T(8,128)(2,1)S(1)} %get-tuple-element.114), channel_id=1, source_target_pairs={{0,16},{16,0},{1,17},{17,1},{2,18},{18,2},{3,19},{19,3},{4,20},{20... | collective-permute-start | bytes 1105928 | tf_op jit(solution)/shard_map/ppermute | solution.py:387
  (20 other events, 38.1 us)
Sparse Core Ops, SparseCore 0:
  10.9 67.6 all-gather.1
  125.1 82.9 reduce-scatter.1
